TPU v7x, 32 devices: a whole 2x2x4 slice. The times are simulated.
32 devices in a mesh: blk: 2 (over x), table: 16 (over z, y, core).
Axes of the slice: x: 2, y: 2, z: 4, core: 2. Of those that a mesh axis runs over, the one named last changes fastest.
Arguments:
- id_table: bfloat16 [131072, 256], P('table'), may hold values from -6 to 6
- w_first: bfloat16 [256, 4096], replicated, may hold values from -0.375 to 0.375
- w_second: bfloat16 [4096, 256], replicated, may hold values from -0.09375 to 0.09375
- owner_ids: int32 [8192, 8], P(('blk', 'table')), may hold values from 0 to 15, all different within a row; in each aligned block of 256 rows (0 to 255, 256 to 511, ...) at most 192 rows name the same one
- row_ids: int32 [8192, 8], P(('blk', 'table')), may hold values from 0 to 8191
Outputs:
- loss: float32 [8192], P(('blk', 'table'))
- item_grad: float32 [8192, 256], P(('blk', 'table'))
- query_grad: float32 [8192, 256], P(('blk', 'table'))
Inputs may be any that keep to these rules, and one draw needn't show every extreme that they name: `owner_ids`: the 8 ids of one pair name 8 different shards; among the ids of one device's 256 pairs no shard is named more than 192 times, a bound that some block reaches.
All inputs are finite; a program needn't handle non-finite values.
Results may differ from a plain program's by a relative error of at most 0.0056.
Values may be sent and summed in bfloat16 or wider, within the bound.
No kernel may reach another device: no remote copies, remote signals or barrier semaphores. Data moves between devices by JAX's collectives and lax.ppermute only.
A program may use at most 64 MiB of HBM per device.

v0:
```python
import jax
import jax.numpy as jnp
from jax import lax
from jax.sharding import PartitionSpec as P

EPS = 1e-06
INV_TEMP = 20.0


def shifted(shard, axis, by):
    count = lax.axis_size(axis)
    return lax.ppermute(shard, axis, [(i, (i + by) % count) for i in range(count)])


def silu_slope(pre):
    sigma = jax.nn.sigmoid(pre)
    return sigma * (1.0 + pre * (1.0 - sigma))


def unit_rows(vectors):
    scale = lax.rsqrt(jnp.sum(vectors * vectors, axis=-1, keepdims=True) + EPS)
    return (vectors * scale, scale)


def unit_backward(grad, unit, scale):
    return scale * (grad - unit * jnp.sum(unit * grad, axis=-1, keepdims=True))


def row_dot(left, right):
    return lax.dot_general(
        left, right, (((1,), (1,)), ((), ())), preferred_element_type=jnp.float32
    )


def col_dot(left, right):
    return lax.dot_general(
        left, right, (((0,), (0,)), ((), ())), preferred_element_type=jnp.float32
    )


def local(id_table, w_first, w_second, owner_ids, row_ids):
    pair_count, bags = owner_ids.shape
    half = bags // 2
    shards = lax.axis_size("table")
    width = id_table.shape[1]
    capacity = min(pair_count, 3 * pair_count * bags // (2 * shards))
    owners = owner_ids.reshape(-1)
    wanted_rows = row_ids.reshape(-1)
    onehot = (owners[:, None] == jnp.arange(shards, dtype=jnp.int32)[None, :]).astype(jnp.int32)
    earlier = jnp.cumsum(onehot, axis=0) - onehot
    slots = jnp.sum(earlier * onehot, axis=1)
    position = owners * capacity + slots
    requests = jnp.zeros((shards * capacity,), jnp.int32).at[position].set(wanted_rows)
    requests = requests.reshape(shards, capacity)
    found = jnp.take(
        id_table, lax.all_to_all(requests, "table", split_axis=0, concat_axis=0, tiled=True), axis=0
    )
    fetched = lax.all_to_all(found, "table", split_axis=0, concat_axis=0, tiled=True)
    embedded = jnp.take(fetched.reshape(shards * capacity, width), position, axis=0)
    embedded = embedded.reshape(pair_count, bags, width).astype(jnp.float32)
    query_in = jnp.sum(embedded[:, :half], axis=1).astype(jnp.bfloat16)
    item_in = jnp.sum(embedded[:, half:], axis=1)
    hidden_pre = jnp.dot(query_in, w_first, preferred_element_type=jnp.float32)
    hidden = jax.nn.silu(hidden_pre).astype(jnp.bfloat16)
    query_out = jnp.dot(hidden, w_second, preferred_element_type=jnp.float32)
    query_unit, query_scale = unit_rows(query_out)
    item_unit, item_scale = unit_rows(item_in)
    query_bf = query_unit.astype(jnp.bfloat16)
    item_bf = item_unit.astype(jnp.bfloat16)
    blocks = lax.axis_size("blk")

    def score_hop(hop_index, carry):
        visitor, exp_total = carry
        scores = INV_TEMP * row_dot(query_bf, visitor)
        exp_total = exp_total + jnp.sum(jnp.exp(scores), axis=1)
        visitor = shifted(visitor, "blk", 1)
        return (visitor, exp_total)

    returned, exp_total = lax.fori_loop(
        0, blocks, score_hop, (item_bf, jnp.zeros((pair_count,), jnp.float32))
    )
    log_total = jnp.log(exp_total)

    def grad_hop(hop_index, carry):
        visitor, partial_value, query_sum = carry
        scores = INV_TEMP * row_dot(query_bf, visitor)
        probs = jnp.exp(scores - log_total[:, None]).astype(jnp.bfloat16)
        query_sum = query_sum + jnp.dot(probs, visitor, preferred_element_type=jnp.float32)
        partial_value = partial_value + col_dot(probs, query_bf)
        visitor = shifted(visitor, "blk", 1)
        partial_value = shifted(partial_value, "blk", 1)
        return (visitor, partial_value, query_sum)

    empty = jnp.zeros((pair_count, width), jnp.float32)
    returned, item_sum, query_sum = lax.fori_loop(0, blocks, grad_hop, (item_bf, empty, empty))
    own = INV_TEMP * jnp.sum(query_bf.astype(jnp.float32) * item_bf.astype(jnp.float32), axis=1)
    loss = log_total - own
    query_unit_grad = INV_TEMP * (query_sum - item_bf.astype(jnp.float32))
    item_unit_grad = INV_TEMP * (item_sum - query_bf.astype(jnp.float32))
    item_grad = unit_backward(item_unit_grad, item_unit, item_scale)
    out_grad = unit_backward(query_unit_grad, query_unit, query_scale).astype(jnp.bfloat16)
    hidden_grad = (row_dot(out_grad, w_second) * silu_slope(hidden_pre)).astype(jnp.bfloat16)
    query_grad = row_dot(hidden_grad, w_first)
    return (loss, item_grad, query_grad)


def solution(mesh):
    placed = (P("table", None), P(), P(), P(("blk", "table"), None), P(("blk", "table"), None))
    return jax.shard_map(
        local,
        mesh=mesh,
        in_specs=placed,
        out_specs=(P(("blk", "table")), P(("blk", "table"), None), P(("blk", "table"), None)),
        check_vma=False,
    )
```

profile of v0, /device:TPU:0, one launch (start us, length us, event | category | flops | bytes accessed | tf_op | source)
XLA Modules:
  0.0 140.9 jit_solution(11213004109478428393)
XLA Ops:
  0.6 0.8 broadcast_multiply_fusion
  1.5 0.8 copy.39
  2.8 4.5 %reduce-window.6 = s32[16,16,128]{2,1,0:T(8,128)S(1)} reduce-window(s32[16,16,128]{2,1,0:T(8,128)S(1)} %fusion.23, s32[]{:T(128)} %constant.30.clone.1), window={size=1x1x128 pad=0_0x0_0x127_0}, to_apply=%region_0.0 | reduce-window | flops 4161536 | bytes 262148 | tf_op jit(solution)/shard_map/reduce-window
  8.1 0.8 copy.44
  9.1 8.1 %scatter_custom_fusion = s32[3072]{0:T(1024)S(1)} fusion(s32[2048]{0:T(1024)S(1)} %bitcast.65, s32[2048]{0:T(1024)S(1)} %reshape.151, s32[]{:T(128)} %constant.30.clone.1), kind=kCustom, calls=%fused_computation.60 | custom fusion | bytes 12292 | tf_op jit(solution)/shard_map/scatter | solution.py:53
  17.3 13.7 %all_to_all.20 = s32[16,1,192]{2,1,0:T(1,128)S(1)} all-to-all(s32[16,1,192]{2,1,0:T(1,128)S(1)} %all_to_all.13), channel_id=1, replica_groups=mesh['blk'=2,'table'=16] {'table'}, dimensions={0} | all-to-all | bytes 24576 | tf_op jit(solution)/shard_map/all_to_all | solution.py:56
  31.1 14.8 %gather_fusion = bf16[3072,256]{1,0:T(8,128)(2,1)} fusion(bf16[8192,256]{1,0:T(8,128)(2,1)} %param.9, s32[3072]{0:T(1024)S(1)} %broadcast_clamp_fusion), kind=kCustom, calls=%fused_computation | custom fusion | bytes 3158016 | tf_op jit(solution)/shard_map/jit(_take)/gather | solution.py:55
  45.9 2.6 %broadcast_select_fusion = bf16[16,192,256]{2,1,0:T(8,128)(2,1)} fusion(bf16[16,192,256]{2,1,0:T(8,128)(2,1)} %bitcast.62, pred[16,192]{1,0:T(8,128)(4,1)S(1)} %compare_and_fusion), kind=kLoop, calls=%fused_computation.18 | loop fusion | flops 786432 | bytes 3148800 | tf_op jit(solution)/shard_map/jit(_take)/select_n | solution.py:55
  48.6 4.5 %all-to-all-start.1 = ((bf16[16,192,256]{2,1,0:T(8,128)(2,1)}), bf16[16,192,256]{2,1,0:T(8,128)(2,1)}, u32[]{:S(2)}, u32[]{:S(2)}) async-start(bf16[16,192,256]{2,1,0:T(8,128)(2,1)} %broadcast_select_fusion), calls=%async_computation.1 | async-start | bytes 3145728 | tf_op jit(solution)/shard_map/all_to_all | solution.py:58
  53.5 31.6 %all-to-all-done.1 = bf16[16,192,256]{2,1,0:T(8,128)(2,1)} async-done(((bf16[16,192,256]{2,1,0:T(8,128)(2,1)}), bf16[16,192,256]{2,1,0:T(8,128)(2,1)}, u32[]{:S(2)}, u32[]{:S(2)}) %all-to-all-start.1) | async-done | bytes 1572896 | tf_op jit(solution)/shard_map/all_to_all | solution.py:58
  85.0 8.2 %gather_fusion.1 = bf16[2048,256]{1,0:T(8,128)(2,1)S(1)} fusion(bf16[3072,256]{1,0:T(8,128)(2,1)} %bitcast.5, s32[2048]{0:T(1024)S(1)} %broadcast_clamp_fusion.1), kind=kCustom, calls=%fused_computation.1 | custom fusion | bytes 2105344 | tf_op jit(solution)/shard_map/jit(_take)/gather | solution.py:59
  93.6 1.3 slice_reduce_fusion
  95.2 0.7 fusion.31
  95.9 0.9 copy-done.9
  96.9 1.4 %multiply_reduce_fusion.2 = (f32[256]{0:T(256)S(1)}, f32[256,256]{0,1:T(8,128)S(1)}) fusion(bf16[4096,256]{1,0:T(8,128)(2,1)S(1)} %copy-done.9, f32[256,4096]{1,0:T(8,128)S(1)} %fusion.31), kind=kOutput, calls=%fused_computation.34 | convolution fusion | flops 542244608 | bytes 6554624 | tf_op jit(solution)/shard_map/dot_general | solution.py:65
  99.0 0.6 copy-done.4
  99.7 11.7 %while.28 = (s32[]{:T(128)}, bf16[256,256]{1,0:T(8,128)(2,1)S(1)}, f32[256]{0:T(256)S(1)}, bf16[256,256]{1,0:T(8,128)(2,1)S(1)}, s32[]{:T(128)}, /*index=5*/s32[]{:T(128)}) while((s32[]{:T(128)}, bf16[256,256]{1,0:T(8,128)(2,1)S(1)}, f32[256]{0:T(256)S(1)}, bf16[256,256]{1,0:T(8,128)(2,1)S(1)}, s32[]{:T(128)}, ...), condition=%wide.region_10.11_spmd.clone, body=%wide.region_8.10_spmd.clone.sunk | while | flops 33685760 | bytes 1052791 | solution.py:79
  99.7 1.6 %collective-permute-start = (bf16[256,256]{1,0:T(8,128)(2,1)S(1)}, bf16[256,256]{1,0:T(8,128)(2,1)S(1)}, u32[]{:S(2)}, u32[]{:S(2)}) collective-permute-start(bf16[256,256]{1,0:T(8,128)(2,1)S(1)} %copy.63), channel_id=1, source_target_pairs={{0,16},{16,0},{1,17},{17,1},{2,18},{18,2},{3,19},{19,3},{4,20},{20... | collective-permute-start | bytes 393224 | tf_op jit(solution)/shard_map/while/body/eval_jaxpr/ppermute | solution.py:12
  101.5 4.4 %collective-permute-done = bf16[256,256]{1,0:T(8,128)(2,1)S(1)} collective-permute-done((bf16[256,256]{1,0:T(8,128)(2,1)S(1)}, bf16[256,256]{1,0:T(8,128)(2,1)S(1)}, u32[]{:S(2)}, u32[]{:S(2)}) %collective-permute-start) | collective-permute-done | bytes 131104 | tf_op jit(solution)/shard_map/while/body/eval_jaxpr/ppermute | solution.py:12
  106.0 1.6 %collective-permute-start = (bf16[256,256]{1,0:T(8,128)(2,1)S(1)}, bf16[256,256]{1,0:T(8,128)(2,1)S(1)}, u32[]{:S(2)}, u32[]{:S(2)}) collective-permute-start(bf16[256,256]{1,0:T(8,128)(2,1)S(1)} %copy.63), channel_id=1, source_target_pairs={{0,16},{16,0},{1,17},{17,1},{2,18},{18,2},{3,19},{19,3},{4,20},{20... | collective-permute-start | bytes 393224 | tf_op jit(solution)/shard_map/while/body/eval_jaxpr/ppermute | solution.py:12
  107.8 3.5 %collective-permute-done = bf16[256,256]{1,0:T(8,128)(2,1)S(1)} collective-permute-done((bf16[256,256]{1,0:T(8,128)(2,1)S(1)}, bf16[256,256]{1,0:T(8,128)(2,1)S(1)}, u32[]{:S(2)}, u32[]{:S(2)}) %collective-permute-start) | collective-permute-done | bytes 131104 | tf_op jit(solution)/shard_map/while/body/eval_jaxpr/ppermute | solution.py:12
  111.4 20.3 %while.29 = (s32[]{:T(128)}, bf16[256,256]{1,0:T(8,128)(2,1)S(1)}, f32[256,256]{1,0:T(8,128)S(1)}, f32[256,256]{1,0:T(8,128)S(1)}, bf16[256,256]{1,0:T(8,128)(2,...) while((s32[]{:T(128)}, bf16[256,256]{1,0:T(8,128)(2,1)S(1)}, f32[256,256]{1,0:T(8,128)S(1)}, ...), condition=%wide.region_13.14_spmd.clone, body=%wide.region_12.13_spmd.clone.sunk | while | flops 101056512 | bytes 3802287 | solution.py:95
  111.9 1.6 %collective-permute-start.2 = (f32[256,256]{1,0:T(8,128)S(1)}, f32[256,256]{1,0:T(8,128)S(1)}, u32[]{:S(2)}, u32[]{:S(2)}) collective-permute-start(f32[256,256]{1,0:T(8,128)S(1)} %convolution_add_fusion.4), channel_id=1, source_target_pairs={{0,16},{16,0},{1,17},{17,1},{2,18},{18,2},{3,19},{19,3},{4,20},{20... | collective-permute-start | bytes 786440 | tf_op jit(solution)/shard_map/while/body/eval_jaxpr/ppermute | solution.py:12
  114.2 7.8 %collective-permute-done.1 = bf16[256,256]{1,0:T(8,128)(2,1)S(1)} collective-permute-done((bf16[256,256]{1,0:T(8,128)(2,1)S(1)}, bf16[256,256]{1,0:T(8,128)(2,1)S(1)}, u32[]{:S(2)}, u32[]{:S(2)}) %collective-permute-start.1) | collective-permute-done | bytes 131104 | tf_op jit(solution)/shard_map/while/body/eval_jaxpr/ppermute | solution.py:12
  122.5 1.6 %collective-permute-start.2 = (f32[256,256]{1,0:T(8,128)S(1)}, f32[256,256]{1,0:T(8,128)S(1)}, u32[]{:S(2)}, u32[]{:S(2)}) collective-permute-start(f32[256,256]{1,0:T(8,128)S(1)} %convolution_add_fusion.4), channel_id=1, source_target_pairs={{0,16},{16,0},{1,17},{17,1},{2,18},{18,2},{3,19},{19,3},{4,20},{20... | collective-permute-start | bytes 786440 | tf_op jit(solution)/shard_map/while/body/eval_jaxpr/ppermute | solution.py:12
  124.1 0.5 collective-permute-start.1
  124.8 6.9 %collective-permute-done.1 = bf16[256,256]{1,0:T(8,128)(2,1)S(1)} collective-permute-done((bf16[256,256]{1,0:T(8,128)(2,1)S(1)}, bf16[256,256]{1,0:T(8,128)(2,1)S(1)}, u32[]{:S(2)}, u32[]{:S(2)}) %collective-permute-start.1) | collective-permute-done | bytes 131104 | tf_op jit(solution)/shard_map/while/body/eval_jaxpr/ppermute | solution.py:12
  131.9 0.8 copy.51
  132.7 1.3 multiply_reduce_fusion
  134.1 0.8 copy.52
  134.9 5.4 %fusion.7 = f32[256,256]{1,0:T(8,128)} fusion(bf16[256,4096]{1,0:T(8,128)(2,1)S(1)} %copy-done, bf16[4096,256]{1,0:T(8,128)(2,1)} %param.11, f32[256,4096]{1,0:T(8,128)} %copy-done.3, f32[256,256]{0,1:T(8,128)S(1)} %copy-done.7, f32[256,256]{0,1:T(8,128)} %copy.51, bf16[256,256]{0,1:T(8,128)(2,1)S(1)} %copy-done.5, f32[256]{0:T(256)S(1)} %get-tuple-element.151, ...), kind=kOutput, calls=%fused_computation.19 | convolution fusion | flops 1083703296 | bytes 9308160 | tf_op jit(solution)/shard_map/dot_general | solution.py:30
  140.3 0.6 multiply_subtract_fusion
  (71 shorter events, 6.0 us)
Async XLA Ops:
  0.6 94.6 %copy-start = (bf16[256,4096]{1,0:T(8,128)(2,1)S(1)}, bf16[256,4096]{1,0:T(8,128)(2,1)}, u32[]{:S(2)}) copy-start(bf16[256,4096]{1,0:T(8,128)(2,1)} %param.10) | copy-start | bytes 6291460
  48.6 4.7 %copy-start.8 = (s32[256,8]{0,1:T(8,128)S(1)}, s32[256,8]{0,1:T(8,128)}, u32[]{:S(2)}) copy-start(s32[256,8]{0,1:T(8,128)} %param.12) | copy-start | bytes 24580
  48.6 36.5 %all-to-all-start.1 = ((bf16[16,192,256]{2,1,0:T(8,128)(2,1)}), bf16[16,192,256]{2,1,0:T(8,128)(2,1)}, u32[]{:S(2)}, u32[]{:S(2)}) async-start(bf16[16,192,256]{2,1,0:T(8,128)(2,1)} %broadcast_select_fusion), calls=%async_computation.1 | async-start | bytes 3145728 | tf_op jit(solution)/shard_map/all_to_all | solution.py:58
  95.2 3.6 %copy-start.1 = (f32[256,256]{0,1:T(8,128)}, f32[256,256]{0,1:T(8,128)S(1)}, u32[]{:S(2)}) copy-start(f32[256,256]{0,1:T(8,128)S(1)} %copy.45) | copy-start | bytes 786436
  95.2 1.7 %copy-start.9 = (bf16[4096,256]{1,0:T(8,128)(2,1)S(1)}, bf16[4096,256]{1,0:T(8,128)(2,1)}, u32[]{:S(2)}) copy-start(bf16[4096,256]{1,0:T(8,128)(2,1)} %param.11) | copy-start | bytes 6291460
  96.9 1.9 %copy-start.3 = (f32[256,4096]{1,0:T(8,128)}, f32[256,4096]{1,0:T(8,128)S(1)}, u32[]{:S(2)}) copy-start(f32[256,4096]{1,0:T(8,128)S(1)} %fusion.31) | copy-start | bytes 12582916
  98.8 0.9 copy-start.6
  98.9 0.7 copy-start.4
  99.7 6.2 %collective-permute-start = (bf16[256,256]{1,0:T(8,128)(2,1)S(1)}, bf16[256,256]{1,0:T(8,128)(2,1)S(1)}, u32[]{:S(2)}, u32[]{:S(2)}) collective-permute-start(bf16[256,256]{1,0:T(8,128)(2,1)S(1)} %copy.63), channel_id=1, source_target_pairs={{0,16},{16,0},{1,17},{17,1},{2,18},{18,2},{3,19},{19,3},{4,20},{20... | collective-permute-start | bytes 393224 | tf_op jit(solution)/shard_map/while/body/eval_jaxpr/ppermute | solution.py:12
  106.0 5.4 %collective-permute-start = (bf16[256,256]{1,0:T(8,128)(2,1)S(1)}, bf16[256,256]{1,0:T(8,128)(2,1)S(1)}, u32[]{:S(2)}, u32[]{:S(2)}) collective-permute-start(bf16[256,256]{1,0:T(8,128)(2,1)S(1)} %copy.63), channel_id=1, source_target_pairs={{0,16},{16,0},{1,17},{17,1},{2,18},{18,2},{3,19},{19,3},{4,20},{20... | collective-permute-start | bytes 393224 | tf_op jit(solution)/shard_map/while/body/eval_jaxpr/ppermute | solution.py:12
  111.9 10.1 %collective-permute-start.2 = (f32[256,256]{1,0:T(8,128)S(1)}, f32[256,256]{1,0:T(8,128)S(1)}, u32[]{:S(2)}, u32[]{:S(2)}) collective-permute-start(f32[256,256]{1,0:T(8,128)S(1)} %convolution_add_fusion.4), channel_id=1, source_target_pairs={{0,16},{16,0},{1,17},{17,1},{2,18},{18,2},{3,19},{19,3},{4,20},{20... | collective-permute-start | bytes 786440 | tf_op jit(solution)/shard_map/while/body/eval_jaxpr/ppermute | solution.py:12
  113.4 8.6 %collective-permute-start.1 = (bf16[256,256]{1,0:T(8,128)(2,1)S(1)}, bf16[256,256]{1,0:T(8,128)(2,1)S(1)}, u32[]{:S(2)}, u32[]{:S(2)}) collective-permute-start(bf16[256,256]{1,0:T(8,128)(2,1)S(1)} %copy.73), channel_id=1, source_target_pairs={{0,16},{16,0},{1,17},{17,1},{2,18},{18,2},{3,19},{19,3},{4,20},{20... | collective-permute-start | bytes 393224 | tf_op jit(solution)/shard_map/while/body/eval_jaxpr/ppermute | solution.py:12
  122.5 9.2 %collective-permute-start.2 = (f32[256,256]{1,0:T(8,128)S(1)}, f32[256,256]{1,0:T(8,128)S(1)}, u32[]{:S(2)}, u32[]{:S(2)}) collective-permute-start(f32[256,256]{1,0:T(8,128)S(1)} %convolution_add_fusion.4), channel_id=1, source_target_pairs={{0,16},{16,0},{1,17},{17,1},{2,18},{18,2},{3,19},{19,3},{4,20},{20... | collective-permute-start | bytes 786440 | tf_op jit(solution)/shard_map/while/body/eval_jaxpr/ppermute | solution.py:12
  124.1 7.7 %collective-permute-start.1 = (bf16[256,256]{1,0:T(8,128)(2,1)S(1)}, bf16[256,256]{1,0:T(8,128)(2,1)S(1)}, u32[]{:S(2)}, u32[]{:S(2)}) collective-permute-start(bf16[256,256]{1,0:T(8,128)(2,1)S(1)} %copy.73), channel_id=1, source_target_pairs={{0,16},{16,0},{1,17},{17,1},{2,18},{18,2},{3,19},{19,3},{4,20},{20... | collective-permute-start | bytes 393224 | tf_op jit(solution)/shard_map/while/body/eval_jaxpr/ppermute | solution.py:12
  131.7 2.3 %copy-start.2 = (f32[256,256]{0,1:T(8,128)S(1)}, f32[256,256]{0,1:T(8,128)}, u32[]{:S(2)}) copy-start(f32[256,256]{0,1:T(8,128)} %copy-done.1) | copy-start | bytes 786436
  131.7 3.2 %copy-start.5 = (bf16[256,256]{0,1:T(8,128)(2,1)S(1)}, bf16[256,256]{0,1:T(8,128)(2,1)}, u32[]{:S(2)}) copy-start(bf16[256,256]{0,1:T(8,128)(2,1)} %copy-done.4) | copy-start | bytes 393220
  131.9 3.0 %copy-start.7 = (f32[256,256]{0,1:T(8,128)S(1)}, f32[256,256]{0,1:T(8,128)}, u32[]{:S(2)}) copy-start(f32[256,256]{0,1:T(8,128)} %copy-done.6) | copy-start | bytes 786436
where the time goes:
time: 143 us; the launch traced here: 141 us
  waiting for transfers between devices  54.2 us (38%)
  local copies, waits for them, and re-layouts  38.5 us (27%)
  blocking collectives  13.7 us (10%)
  other arithmetic  12.2 us (9%)
  starting transfers between devices  11.8 us (8%)
  matrix products  9.45 us (7%)
    all_to_all x1, waiting for transfers between devices, local(): lax.all_to_all(found, 'table', split_axis=0, concat_axis=0, tiled=True)  31.6 us
    ppermute x6, waiting for transfers between devices, shifted(): lax.ppermute(shard, axis, [(i, (i + by) % count) for i in range(count)])  22.7 us
    gather x1, local copies, waits for them, and re-layouts, local(): jnp.take(id_table, lax.all_to_all(requests, 'table', split_axis=0, concat...  14.8 us
    all_to_all x1, blocking collectives, local(): lax.all_to_all(requests, 'table', split_axis=0, concat_axis=0, tiled=True)  13.7 us
    gather x1, local copies, waits for them, and re-layouts, local(): jnp.take(fetched.reshape(shards * capacity, width), position, axis=0)  8.25 us
    scatter x1, local copies, waits for them, and re-layouts, local(): jnp.zeros((shards * capacity,), jnp.int32).at[position].set(wanted_rows)  8.06 us
    ppermute x6, starting transfers between devices, shifted(): lax.ppermute(shard, axis, [(i, (i + by) % count) for i in range(count)])  7.29 us
    dot_general x5, matrix products, row_dot(): lax.dot_general(left, right, (((1,), (1,)), ((), ())), preferred_element_...  6.42 us
  transfers between devices with their start and end apart: 7, of which 5 were waited for; matrix products, arithmetic and copies ran while one was open for 1% of the time, Pallas kernels for 0%

commit v1 on v0

v1 whole, which is shorter than its diff:
```python
import functools

import jax
import jax.numpy as jnp
from jax import lax
from jax.experimental import pallas as pl
from jax.experimental.pallas import tpu as pltpu
from jax.sharding import PartitionSpec as P

EPS = 1e-06
INV_TEMP = 20.0


def params(mebibytes):
    return pltpu.CompilerParams(vmem_limit_bytes=mebibytes * 1024 * 1024)


def iota(shape, dim):
    return lax.broadcasted_iota(jnp.int32, shape, dim)


def row_dot(left, right):
    return lax.dot_general(
        left, right, (((1,), (1,)), ((), ())), preferred_element_type=jnp.float32
    )


def col_dot(left, right):
    return lax.dot_general(
        left, right, (((0,), (0,)), ((), ())), preferred_element_type=jnp.float32
    )


def dot(left, right):
    return jnp.dot(left, right, preferred_element_type=jnp.float32)


def unit_rows(vectors):
    scale = lax.rsqrt(jnp.sum(vectors * vectors, axis=-1, keepdims=True) + EPS)
    return vectors * scale, scale


def unit_backward(grad, unit, scale):
    return scale * (grad - unit * jnp.sum(unit * grad, axis=-1, keepdims=True))


def route_kernel(relative, rows_dev, *refs):
    codes, near_ref, far_ref, request_refs = refs[:4], refs[4], refs[5], refs[6:]
    chips = len(request_refs)
    bags, pairs = codes[0].shape
    capacity = near_ref.shape[1]
    lists = 6 * chips
    place = lax.axis_index("table")
    half = 2 * chips
    list_of = iota((lists, pairs), 0)
    chip = relative(place % half // 2, list_of % chips)
    asker = list_of // chips
    core = jnp.where(asker < 4, place % 2, 1 - place % 2)
    start = (place // half * half + chip * 2 + core) * rows_dev
    named = jnp.zeros((lists, pairs), jnp.float32)
    rows = jnp.zeros((lists, pairs), jnp.int32)
    kind = jnp.zeros((lists, pairs), jnp.int32)
    for k in range(bags):
        code = codes[0][k : k + 1, :]
        for r, at in ((1, 1), (2, 2), (3, 3), (5, 2)):
            code = jnp.where(asker == r, codes[at][k : k + 1, :], code)
        row = code - start
        hit = (row >= 0) & (row < rows_dev)
        named = jnp.where(hit, 1.0, named)
        rows = jnp.where(hit, row, rows)
        kind = jnp.where(hit, 1 if k < bags // 2 else 2, kind)
    before = jnp.where(iota((pairs, pairs), 0) < iota((pairs, pairs), 1), 1.0, 0.0)
    slot = dot(named.astype(jnp.bfloat16), before.astype(jnp.bfloat16)).astype(jnp.int32)
    slot = jnp.where(named > 0.0, slot, -1)
    digits = [rows // 256, rows % 256, kind, iota((lists, pairs), 1)]
    packed = jnp.concatenate([d.astype(jnp.float32) for d in digits], axis=0).astype(jnp.bfloat16)
    places = iota((capacity, pairs), 0)
    for s in range(lists):
        chosen = jnp.where(slot[s : s + 1, :] == places, 1.0, 0.0).astype(jnp.bfloat16)
        got = row_dot(packed, chosen).astype(jnp.int32)
        high, low, which, pair = [got[i * lists + s : i * lists + s + 1, :] for i in range(4)]
        asked, j = s // chips, s % chips
        if asked < 4:
            request_refs[j][asked : asked + 1, :] = 2 * (high * 256 + low)
        if asked in (0, 2, 4, 5):
            at = j if asked < 4 else chips + j
            bag_ref = near_ref if asked in (0, 4) else far_ref
            bag_ref[at : at + 1, :] = (which - 1) * pairs + pair


def widen_kernel(table_ref, wide_ref):
    width = table_ref.shape[1]
    step = 128

    def widen(i, carry):
        start = pl.multiple_of(i * step, step)
        part = table_ref[pl.ds(start, step), :].astype(jnp.float32)
        wide_ref[pl.ds(2 * start, step, stride=2), :] = part[:, : width // 2]
        wide_ref[pl.ds(2 * start + 1, step, stride=2), :] = part[:, width // 2 :]
        return carry

    lax.fori_loop(0, table_ref.shape[0] // step, widen, 0)


def gather_kernel(chips, asker, *refs):
    wanted, wide_ref, out_ref, stage = refs[:chips], refs[chips], refs[chips + 1], refs[-1]
    _, capacity, width = out_ref.shape
    group = 16
    for j in range(chips):
        index_ref = wanted[chips - 1 - j]
        for base in range(0, capacity, group):
            found = [wide_ref[pl.ds(index_ref[asker, base + i], 2), :] for i in range(group)]
            for i in range(group):
                stage[pl.ds(2 * (base + i), 2), :] = found[i]
        for part in range(2):
            values = stage[pl.ds(part, capacity, stride=2), :]
            out_ref[j, :, part * (width // 2) : (part + 1) * (width // 2)] = values.astype(
                jnp.bfloat16
            )


def pack_kernel(chips, same_ref, swapped_ref, *out_refs):
    for out_ref, j in zip(out_refs, range(chips - 1, 0, -1)):
        out_ref[0] = same_ref[j]
        out_ref[1] = swapped_ref[j]


def bag_sums(bag_ref, rows, bags):
    total = None
    for at, values in enumerate(rows):
        chosen = bag_ref[at : at + 1, :] == iota((bags, bag_ref.shape[1]), 0)
        part = dot(jnp.where(chosen, 1.0, 0.0).astype(jnp.bfloat16), values)
        total = part if total is None else total + part
    return total


def lists_of(order, same_ref, swapped_ref, message_refs):
    chips = len(order) + 1
    return [
        own_ref[0] if j == 0 else message_refs[order.index(j)][f]
        for f, own_ref in enumerate((same_ref, swapped_ref))
        for j in range(chips)
    ]


def far_kernel(order, bag_ref, same_ref, swapped_ref, *refs):
    messages, (query_ref, item_ref) = refs[:-2], refs[-2:]
    pairs = query_ref.shape[0]
    total = bag_sums(bag_ref, lists_of(order, same_ref, swapped_ref, messages), 2 * pairs)
    query_ref[...] = total[:pairs].astype(jnp.bfloat16)
    item_ref[...] = total[pairs:].astype(jnp.bfloat16)


def item_kernel(order, bag_ref, far_ref, same_ref, swapped_ref, *refs):
    messages, (query_ref, unit_ref, scale_ref, bf_ref) = refs[:-4], refs[-4:]
    pairs = query_ref.shape[0]
    total = bag_sums(bag_ref, lists_of(order, same_ref, swapped_ref, messages), 2 * pairs)
    query_ref[...] = total[:pairs]
    unit, scale = unit_rows(total[pairs:] + far_ref[...].astype(jnp.float32))
    unit_ref[...] = unit
    scale_ref[...] = scale
    bf_ref[...] = unit.astype(jnp.bfloat16)


def tower_kernel(
    near_ref, far_ref, first_ref, second_ref, unit_ref, scale_ref, bf_ref, slope_ref
):
    query_in = (near_ref[...] + far_ref[...].astype(jnp.float32)).astype(jnp.bfloat16)
    step = 1024
    total = None
    for at in range(0, first_ref.shape[1], step):
        pre = dot(query_in, first_ref[:, at : at + step])
        sigma = 1.0 / (1.0 + jnp.exp(-pre))
        hidden = pre * sigma
        slope_ref[:, at : at + step] = sigma * (1.0 + pre * (1.0 - sigma))
        part = dot(hidden.astype(jnp.bfloat16), second_ref[at : at + step, :])
        total = part if total is None else total + part
    unit, scale = unit_rows(total)
    unit_ref[...] = unit
    scale_ref[...] = scale
    bf_ref[...] = unit.astype(jnp.bfloat16)


def group_exps(query, item):
    return jnp.exp(INV_TEMP * row_dot(query, item))


def row_sums(values):
    return jnp.sum(values, axis=1, keepdims=True)


def query_grad_kernel(blocks, *refs):
    query_ref, items, refs = refs[0], refs[1 : 1 + blocks], refs[1 + blocks :]
    first_ref, second_ref, slope_ref, unit_ref, scale_ref, loss_ref, grad_ref, item_sum_ref = refs
    query = query_ref[...]
    kept = [group_exps(query, item[...]) for item in items[:2]]
    total = sum(row_sums(exps) for exps in kept)
    for item in items[2:]:
        total = total + row_sums(group_exps(query, item[...]))
    inverse = 1.0 / total
    query_sum = jnp.zeros(query.shape, jnp.float32)
    for j, item in enumerate(items):
        exps = kept[j] if j < 2 else group_exps(query, item[...])
        probs = (exps * inverse).astype(jnp.bfloat16)
        query_sum = query_sum + dot(probs, item[...])
        if j == 0:
            item_sum_ref[...] = col_dot(probs, query)
    wide_item = items[0][...].astype(jnp.float32)
    own = INV_TEMP * row_sums(query.astype(jnp.float32) * wide_item)
    loss_ref[...] = (jnp.log(total) - own).T
    out_grad = unit_backward(
        INV_TEMP * (query_sum - wide_item), unit_ref[...], scale_ref[...]
    ).astype(jnp.bfloat16)
    step = 1024
    total = None
    for at in range(0, first_ref.shape[1], step):
        back = row_dot(out_grad, second_ref[at : at + step, :])
        hidden_grad = (back * slope_ref[:, at : at + step]).astype(jnp.bfloat16)
        part = row_dot(hidden_grad, first_ref[:, at : at + step])
        total = part if total is None else total + part
    grad_ref[...] = total


def item_grad_kernel(blocks, *refs):
    queries, items, refs = refs[:blocks], refs[blocks : 2 * blocks], refs[2 * blocks :]
    item_sum_ref, unit_ref, scale_ref, grad_ref, all_queries, all_items = refs
    for b in range(blocks):
        all_queries[b] = queries[b][...]
        all_items[b] = items[b][...]
    own_item = all_items[0]

    def add(i, total):
        query = all_queries[i]
        own_exps = group_exps(query, own_item)

        def add_total(j, sums):
            return sums + row_sums(group_exps(query, all_items[j]))

        sums = lax.fori_loop(1, blocks, add_total, row_sums(own_exps), unroll=blocks == 2)
        probs = (own_exps * (1.0 / sums)).astype(jnp.bfloat16)
        return total + col_dot(probs, query)

    item_sum = lax.fori_loop(1, blocks, add, item_sum_ref[...], unroll=blocks == 2)
    grad_ref[...] = unit_backward(
        INV_TEMP * (item_sum - all_queries[0].astype(jnp.float32)), unit_ref[...], scale_ref[...]
    )


def rotated(shard, axis, by):
    count = lax.axis_size(axis)
    return lax.ppermute(shard, axis, [(i, (i + by) % count) for i in range(count)])


def struct(shape, dtype):
    return jax.ShapeDtypeStruct(shape, dtype)


def local(id_table, w_first, w_second, owner_ids, row_ids):
    pairs, bags = owner_ids.shape
    shards = lax.axis_size("table")
    blocks = lax.axis_size("blk")
    width = id_table.shape[1]
    hidden_units = w_first.shape[1]
    capacity = min(pairs, 3 * pairs * bags // (2 * shards))
    bf, f32 = jnp.bfloat16, jnp.float32

    half = shards // 2
    chips = half // 2
    power = chips & (chips - 1) == 0

    def relative(chip, j):
        return chip ^ j if power else (chip + j) % chips

    def to_chip(values, j, flip=0):
        if j == 0 and flip == 0:
            return values
        route = [
            (t, t // half * half + relative(t % half // 2, j) * 2 + (t % 2 ^ flip))
            for t in range(shards)
        ]
        return lax.ppermute(values, "table", route)

    def to_mirror(values, flip=0):
        route = [(t, ((t + half) % shards) ^ flip) for t in range(shards)]
        return lax.ppermute(values, "table", route)

    code = owner_ids * id_table.shape[0] + row_ids
    codes = [code, to_chip(code, 0, 1), to_mirror(code), to_mirror(code, 1)]
    wide = pl.pallas_call(
        widen_kernel,
        out_shape=struct((2 * id_table.shape[0], width // 2), f32),
        compiler_params=params(8),
        name="widen",
    )(id_table)
    *codes, wide = lax.optimization_barrier((*codes, wide))
    near_bags, far_bags, *requests = pl.pallas_call(
        functools.partial(route_kernel, relative, id_table.shape[0]),
        out_shape=[struct((half, capacity), jnp.int32)] * 2
        + [struct((4, capacity), jnp.int32)] * chips,
        compiler_params=params(4),
        name="route",
    )(*[c.T for c in codes])
    wanted = [to_chip(requests[j], j) for j in reversed(range(chips))][::-1]

    def gather(asker, wide):
        return pl.pallas_call(
            functools.partial(gather_kernel, chips, asker),
            in_specs=[pl.BlockSpec(memory_space=pltpu.SMEM)] * chips
            + [pl.BlockSpec(memory_space=pltpu.VMEM)],
            out_shape=struct((chips, capacity, width), bf),
            scratch_shapes=[pltpu.VMEM((2 * capacity, width // 2), f32)],
            compiler_params=params(8),
            name="gather",
        )(*wanted[::-1], wide)

    def answered(first, wide, order):
        swapped = to_chip(gather(first + 1, wide), 0, 1)
        same = gather(first, wide)
        messages = pl.pallas_call(
            functools.partial(pack_kernel, chips),
            out_shape=[struct((2, capacity, width), bf)] * (chips - 1),
            compiler_params=params(8),
            name="pack",
        )(same, swapped)
        arrived = []
        for j in order:
            back = j if power else (chips - j) % chips
            arrived.append(to_chip(messages[chips - 1 - back], back))
        return (same, swapped, *arrived), messages

    order = list(range(chips - 1, 0, -1))
    far_rows, far_messages = answered(2, wide, order)
    wide, _ = lax.optimization_barrier((wide, far_messages[-1]))
    near_rows, near_messages = answered(0, wide, order)
    far_bags, _ = lax.optimization_barrier((far_bags, near_messages[-1]))
    far_query, far_item = pl.pallas_call(
        functools.partial(far_kernel, order),
        out_shape=[struct((pairs, width), bf)] * 2,
        compiler_params=params(8),
        name="far_bags",
    )(far_bags, *far_rows)
    far_item = to_mirror(far_item)
    far_query = to_mirror(far_query)
    near_query, item_unit, item_scale, item_bf = pl.pallas_call(
        functools.partial(item_kernel, order),
        out_shape=[
            struct((pairs, width), f32),
            struct((pairs, width), f32),
            struct((pairs, 1), f32),
            struct((pairs, width), bf),
        ],
        compiler_params=params(8),
        name="items",
    )(near_bags, far_item, *near_rows)
    items = [item_bf] + [rotated(item_bf, "blk", by) for by in range(1, blocks)]
    query_unit, query_scale, query_bf, slope = pl.pallas_call(
        tower_kernel,
        out_shape=[
            struct((pairs, width), f32),
            struct((pairs, 1), f32),
            struct((pairs, width), bf),
            struct((pairs, hidden_units), f32),
        ],
        compiler_params=params(12),
        name="tower",
    )(near_query, far_query, w_first, w_second)
    queries = [query_bf] + [rotated(query_bf, "blk", by) for by in range(1, blocks)]
    loss, query_grad, own_sum = pl.pallas_call(
        functools.partial(query_grad_kernel, blocks),
        out_shape=[
            struct((1, pairs), f32),
            struct((pairs, width), f32),
            struct((pairs, width), f32),
        ],
        compiler_params=params(12),
        name="query_grads",
    )(query_bf, *items, w_first, w_second, slope, query_unit, query_scale)
    item_grad = pl.pallas_call(
        functools.partial(item_grad_kernel, blocks),
        out_shape=struct((pairs, width), f32),
        scratch_shapes=[pltpu.VMEM((blocks, pairs, width), bf)] * 2,
        compiler_params=params(12),
        name="item_grads",
    )(*queries, *items, own_sum, item_unit, item_scale)
    return loss.reshape(pairs), item_grad, query_grad


def solution(mesh):
    placed = (P("table", None), P(), P(), P(("blk", "table"), None), P(("blk", "table"), None))
    return jax.shard_map(
        local,
        mesh=mesh,
        in_specs=placed,
        out_specs=(P(("blk", "table")), P(("blk", "table"), None), P(("blk", "table"), None)),
        check_vma=False,
    )
```

time: 143 us -> 58.9 us (0.41); the launches traced: 141 us -> 58.7 us
  local copies, waits for them, and re-layouts: 38.5 us -> 2.19 us
  waiting for transfers between devices: 54.2 us -> 19.6 us
  Pallas kernels: 0 us -> 15.3 us
  blocking collectives: 13.7 us -> 0 us
  other arithmetic: 12.2 us -> 0.72 us
  matrix products: 9.45 us -> 0 us
  starting transfers between devices: 11.8 us -> 20.1 us
    all_to_all x1 -> x0, waiting for transfers between devices: 31.6 us -> none  [local(): lax.all_to_all(found, 'table', split_axis=0, concat_axis=0, tiled=True)]
    gather x2 -> x0, local copies, waits for them, and re-layouts: 23.1 us -> none  [the longest x1 14.8 us: local(): jnp.take(id_table, lax.all_to_all(requests, 'table', split_axis=0, concat...]
    pallas_call x0 -> x13, Pallas kernels: none -> 15.3 us  [the longest x4 5.44 us: gather(): pl.pallas_call(functools.partial(gather_kernel, chips, asker), in_specs=[...]
    all_to_all x1 -> x0, blocking collectives: 13.7 us -> none  [local(): lax.all_to_all(requests, 'table', split_axis=0, concat_axis=0, tiled=True)]
    ppermute x6 -> x18, starting transfers between devices: 7.29 us -> 20.1 us  [the longest x12 9.94 us: to_chip(): return lax.ppermute(values, 'table', route)]
    dot_general x11 -> x0, matrix products: 9.45 us -> none  [the longest x5 6.42 us: row_dot(): lax.dot_general(left, right, (((1,), (1,)), ((), ())), preferred_element_...]
    scatter x1 -> x0, local copies, waits for them, and re-layouts: 8.06 us -> none  [local(): jnp.zeros((shards * capacity,), jnp.int32).at[position].set(wanted_rows)]
    another operation x3 -> x0, other arithmetic: 4.82 us -> none
  transfers between devices with their start and end apart: 7 -> 18, of which waited for: 5 -> 12; matrix products, arithmetic and copies ran while one was open for 1% -> 0% of each run, Pallas kernels for 0% -> 17%
where the time goes in v1:
time: 58.9 us; the launch traced here: 58.7 us
  starting transfers between devices  20.1 us (34%)
  waiting for transfers between devices  19.6 us (33%)
  Pallas kernels  15.3 us (26%)
  local copies, waits for them, and re-layouts  2.19 us (4%)
  other arithmetic  0.72 us (1%)
  between operations  0.72 us (1%)
    ppermute x12, waiting for transfers between devices, to_chip(): return lax.ppermute(values, 'table', route)  10.5 us
    ppermute x12, starting transfers between devices, to_chip(): return lax.ppermute(values, 'table', route)  9.94 us
    ppermute x4, waiting for transfers between devices, to_mirror(): return lax.ppermute(values, 'table', route)  8.69 us
    ppermute x4, starting transfers between devices, to_mirror(): return lax.ppermute(values, 'table', route)  7.08 us
    pallas_call x4, Pallas kernels, gather(): pl.pallas_call(functools.partial(gather_kernel, chips, asker), in_specs=[...  5.44 us
    ppermute x2, starting transfers between devices, rotated(): lax.ppermute(shard, axis, [(i, (i + by) % count) for i in range(count)])  3.12 us
    pallas_call x1, Pallas kernels, local(): pl.pallas_call(functools.partial(query_grad_kernel, blocks), out_shape=[s...  3.03 us
    unnamed x6, local copies, waits for them, and re-layouts  2.19 us
  transfers between devices with their start and end apart: 18, of which 12 were waited for; matrix products, arithmetic and copies ran while one was open for 0% of the time, Pallas kernels for 17%

profile of v1, /device:TPU:0, one launch (start us, length us, event | category | flops | bytes accessed | tf_op | source)
XLA Modules:
  0.0 58.7 jit_solution(1797997529320442793)
XLA Ops:
  0.6 0.7 %multiply_add_fusion = s32[256,8]{0,1:T(8,128)S(1)} fusion(s32[256,8]{0,1:T(8,128)} %param.9, s32[256,8]{0,1:T(8,128)} %param.8), kind=kLoop, calls=%fused_computation | loop fusion | flops 4096 | bytes 24576 | tf_op jit(solution)/shard_map/add | solution.py:287
  1.3 3.5 %collective-permute-start.2 = (s32[256,8]{0,1:T(8,128)S(1)}, s32[256,8]{0,1:T(8,128)S(1)}, u32[]{:S(2)}, u32[]{:S(2)}) collective-permute-start(s32[256,8]{0,1:T(8,128)S(1)} %multiply_add_fusion), channel_id=1, source_target_pairs={{0,9},{1,8},{2,11},{3,10},{4,13},{5,12},{6,15},{7,14},{8,1},{9,0},... | collective-permute-start | bytes 24584 | tf_op jit(solution)/shard_map/ppermute | solution.py:285
  4.8 0.6 %collective-permute-start.1 = (s32[256,8]{0,1:T(8,128)S(1)}, s32[256,8]{0,1:T(8,128)S(1)}, u32[]{:S(2)}, u32[]{:S(2)}) collective-permute-start(s32[256,8]{0,1:T(8,128)S(1)} %multiply_add_fusion), channel_id=1, source_target_pairs={{0,8},{1,9},{2,10},{3,11},{4,12},{5,13},{6,14},{7,15},{8,0},{9,1},... | collective-permute-start | bytes 24584 | tf_op jit(solution)/shard_map/ppermute | solution.py:285
  5.5 2.2 %copy-done.2 = bf16[8192,256]{1,0:T(8,128)(2,1)S(1)} copy-done((bf16[8192,256]{1,0:T(8,128)(2,1)S(1)}, bf16[8192,256]{1,0:T(8,128)(2,1)}, u32[]{:S(2)}) %copy-start.2) | copy-done | bytes 4194328
  7.7 0.7 %widen.1.refs_4_ = f32[16384,128]{1,0:T(8,128)S(1)} custom-call(bf16[8192,256]{1,0:T(8,128)(2,1)S(1)} %copy-done.2), custom_call_target="tpu_custom_call" | custom-call | tf_op jit(solution)/shard_map/widen/pallas_call | solution.py:289
  8.4 1.0 %collective-permute-done.1 = s32[256,8]{0,1:T(8,128)S(1)} collective-permute-done((s32[256,8]{0,1:T(8,128)S(1)}, s32[256,8]{0,1:T(8,128)S(1)}, u32[]{:S(2)}, u32[]{:S(2)}) %collective-permute-start.1) | collective-permute-done | bytes 8224 | tf_op jit(solution)/shard_map/ppermute | solution.py:285
  9.4 1.1 %route.1 = (s32[8,192]{1,0:T(8,128)S(1)}, s32[8,192]{1,0:T(8,128)S(1)}, s32[4,192]{1,0:T(4,128)S(1)}, s32[4,192]{1,0:T(4,128)S(1)}, s32[4,192]{1,0:T(4,128)S(1)}, /*index=5*/s32[4,192]{1,0:T(4,128)S(1)}) custom-call(s32[8,256]{1,0:T(8,128)S(1)} %bitcast.5, s32[8,256]{1,0:T(8,128)S(1)} %bitcast.8, s32[8,256]{1,0:T(8,128)S(1)} %bitcast.7, s32[8,256]{1,0:T(8,128)S(1)} %bitcast.6), custom_call_target="tpu_custom_call" | custom-call | tf_op jit(solution)/shard_map/route/pallas_call | solution.py:296
  10.5 2.6 %collective-permute-start.3 = (s32[4,192]{1,0:T(4,128)S(1)}, s32[4,192]{1,0:T(4,128)S(1)}, u32[]{:S(2)}, u32[]{:S(2)}) collective-permute-start(s32[4,192]{1,0:T(4,128)S(1)} %get-tuple-element.41), channel_id=1, source_target_pairs={{0,6},{1,7},{2,4},{3,5},{4,2},{5,3},{6,0},{7,1},{8,14},{9,15},{10,... | collective-permute-start | bytes 9224 | tf_op jit(solution)/shard_map/ppermute | solution.py:281
  14.0 1.0 %collective-permute-done.3.refs_0_ = s32[4,192]{1,0:T(4,128)S(1)} collective-permute-done((s32[4,192]{1,0:T(4,128)S(1)}, s32[4,192]{1,0:T(4,128)S(1)}, u32[]{:S(2)}, u32[]{:S(2)}) %collective-permute-start.3) | collective-permute-done | bytes 3104 | tf_op jit(solution)/shard_map/ppermute | solution.py:281
  15.1 1.6 %collective-permute-done.4.refs_1_ = s32[4,192]{1,0:T(4,128)S(1)} collective-permute-done((s32[4,192]{1,0:T(4,128)S(1)}, s32[4,192]{1,0:T(4,128)S(1)}, u32[]{:S(2)}, u32[]{:S(2)}) %collective-permute-start.4) | collective-permute-done | bytes 3104 | tf_op jit(solution)/shard_map/ppermute | solution.py:281
  17.1 1.4 %gather.5 = bf16[4,192,256]{2,1,0:T(8,128)(2,1)S(1)} custom-call(s32[4,192]{1,0:T(4,128)S(1)} %collective-permute-done.3.refs_0_, s32[4,192]{1,0:T(4,128)S(1)} %collective-permute-done.4.refs_1_, s32[4,192]{1,0:T(4,128)S(1)} %collective-permute-done.5.refs_2_, s32[4,192]{1,0:T(4,128)S(1)} %get-tuple-element.44.refs_3_, f32[16384,128]{1,0:T(8,128)S(1)} %widen.1.refs_4_), custom_call_target="tpu_custom_call" | custom-call | tf_op jit(solution)/shard_map/gather/pallas_call | solution.py:306
  18.6 1.4 %gather.4.same_ref = bf16[4,192,256]{2,1,0:T(8,128)(2,1)S(1)} custom-call(s32[4,192]{1,0:T(4,128)S(1)} %collective-permute-done.3.refs_0_, s32[4,192]{1,0:T(4,128)S(1)} %collective-permute-done.4.refs_1_, s32[4,192]{1,0:T(4,128)S(1)} %collective-permute-done.5.refs_2_, s32[4,192]{1,0:T(4,128)S(1)} %get-tuple-element.44.refs_3_, f32[16384,128]{1,0:T(8,128)S(1)} %widen.1.refs_4_), custom_call_target="tpu_custom_call" | custom-call | tf_op jit(solution)/shard_map/gather/pallas_call | solution.py:306
  20.3 1.4 %gather.7 = bf16[4,192,256]{2,1,0:T(8,128)(2,1)S(1)} custom-call(s32[4,192]{1,0:T(4,128)S(1)} %collective-permute-done.3.refs_0_, s32[4,192]{1,0:T(4,128)S(1)} %collective-permute-done.4.refs_1_, s32[4,192]{1,0:T(4,128)S(1)} %collective-permute-done.5.refs_2_, s32[4,192]{1,0:T(4,128)S(1)} %get-tuple-element.44.refs_3_, f32[16384,128]{1,0:T(8,128)S(1)} %widen.1.refs_4_), custom_call_target="tpu_custom_call" | custom-call | tf_op jit(solution)/shard_map/gather/pallas_call | solution.py:306
  21.9 1.5 %collective-permute-start.8 = (bf16[2,192,256]{2,1,0:T(8,128)(2,1)S(1)}, bf16[2,192,256]{2,1,0:T(8,128)(2,1)S(1)}, u32[]{:S(2)}, u32[]{:S(2)}) collective-permute-start(bf16[2,192,256]{2,1,0:T(8,128)(2,1)S(1)} %get-tuple-element.50), channel_id=1, source_target_pairs={{0,6},{1,7},{2,4},{3,5},{4,2},{5,3},{6,0},{7,1},{8,14},{9,15},{10,... | collective-permute-start | bytes 589832 | tf_op jit(solution)/shard_map/ppermute | solution.py:281
  23.9 1.5 %collective-permute-start.10 = (bf16[2,192,256]{2,1,0:T(8,128)(2,1)S(1)}, bf16[2,192,256]{2,1,0:T(8,128)(2,1)S(1)}, u32[]{:S(2)}, u32[]{:S(2)}) collective-permute-start(bf16[2,192,256]{2,1,0:T(8,128)(2,1)S(1)} %get-tuple-element.46), channel_id=1, source_target_pairs={{0,2},{1,3},{2,0},{3,1},{4,6},{5,7},{6,4},{7,5},{8,10},{9,11},{10,... | collective-permute-start | bytes 589832 | tf_op jit(solution)/shard_map/ppermute | solution.py:281
  25.4 1.4 %gather.6.same_ref = bf16[4,192,256]{2,1,0:T(8,128)(2,1)S(1)} custom-call(s32[4,192]{1,0:T(4,128)S(1)} %collective-permute-done.3.refs_0_, s32[4,192]{1,0:T(4,128)S(1)} %collective-permute-done.4.refs_1_, s32[4,192]{1,0:T(4,128)S(1)} %collective-permute-done.5.refs_2_, s32[4,192]{1,0:T(4,128)S(1)} %get-tuple-element.44.refs_3_, f32[16384,128]{1,0:T(8,128)S(1)} %widen.1.refs_4_), custom_call_target="tpu_custom_call" | custom-call | tf_op jit(solution)/shard_map/gather/pallas_call | solution.py:306
  26.8 1.6 %collective-permute-start.12 = (bf16[2,192,256]{2,1,0:T(8,128)(2,1)S(1)}, bf16[2,192,256]{2,1,0:T(8,128)(2,1)S(1)}, u32[]{:S(2)}, u32[]{:S(2)}) collective-permute-start(bf16[2,192,256]{2,1,0:T(8,128)(2,1)S(1)} %get-tuple-element.53), channel_id=1, source_target_pairs={{0,6},{1,7},{2,4},{3,5},{4,2},{5,3},{6,0},{7,1},{8,14},{9,15},{10,... | collective-permute-start | bytes 589832 | tf_op jit(solution)/shard_map/ppermute | solution.py:281
  28.9 1.7 %collective-permute-done.8.refs_0_ = bf16[2,192,256]{2,1,0:T(8,128)(2,1)S(1)} collective-permute-done((bf16[2,192,256]{2,1,0:T(8,128)(2,1)S(1)}, bf16[2,192,256]{2,1,0:T(8,128)(2,1)S(1)}, u32[]{:S(2)}, u32[]{:S(2)}) %collective-permute-start.8) | collective-permute-done | bytes 196640 | tf_op jit(solution)/shard_map/ppermute | solution.py:281
  31.1 2.7 %collective-permute-done.9.refs_1_ = bf16[2,192,256]{2,1,0:T(8,128)(2,1)S(1)} collective-permute-done((bf16[2,192,256]{2,1,0:T(8,128)(2,1)S(1)}, bf16[2,192,256]{2,1,0:T(8,128)(2,1)S(1)}, u32[]{:S(2)}, u32[]{:S(2)}) %collective-permute-start.9) | collective-permute-done | bytes 196640 | tf_op jit(solution)/shard_map/ppermute | solution.py:281
  33.8 1.0 %collective-permute-done.10.refs_2_ = bf16[2,192,256]{2,1,0:T(8,128)(2,1)S(1)} collective-permute-done((bf16[2,192,256]{2,1,0:T(8,128)(2,1)S(1)}, bf16[2,192,256]{2,1,0:T(8,128)(2,1)S(1)}, u32[]{:S(2)}, u32[]{:S(2)}) %collective-permute-start.10) | collective-permute-done | bytes 196640 | tf_op jit(solution)/shard_map/ppermute | solution.py:281
  34.8 0.7 %far_bags.1 = (bf16[256,256]{1,0:T(8,128)(2,1)S(1)}, bf16[256,256]{1,0:T(8,128)(2,1)S(1)}) custom-call(s32[8,192]{1,0:T(8,128)S(1)} %get-tuple-element.49.bag_ref, bf16[4,192,256]{2,1,0:T(8,128)(2,1)S(1)} %gather.4.same_ref, bf16[4,192,256]{2,1,0:T(8,128)(2,1)S(1)} %collective-permute-done.6.swapped_ref, ...), custom_call_target="tpu_custom_call" | custom-call | tf_op jit(solution)/shard_map/far_bags/pallas_call | solution.py:336
  35.6 1.8 %collective-permute-start.11 = (bf16[256,256]{1,0:T(8,128)(2,1)S(1)}, bf16[256,256]{1,0:T(8,128)(2,1)S(1)}, u32[]{:S(2)}, u32[]{:S(2)}) collective-permute-start(bf16[256,256]{1,0:T(8,128)(2,1)S(1)} %get-tuple-element.52), channel_id=1, source_target_pairs={{0,8},{1,9},{2,10},{3,11},{4,12},{5,13},{6,14},{7,15},{8,0},{9,1},... | collective-permute-start | bytes 393224 | tf_op jit(solution)/shard_map/ppermute | solution.py:285
  37.3 1.2 %collective-permute-start.15 = (bf16[256,256]{1,0:T(8,128)(2,1)S(1)}, bf16[256,256]{1,0:T(8,128)(2,1)S(1)}, u32[]{:S(2)}, u32[]{:S(2)}) collective-permute-start(bf16[256,256]{1,0:T(8,128)(2,1)S(1)} %get-tuple-element.56), channel_id=1, source_target_pairs={{0,8},{1,9},{2,10},{3,11},{4,12},{5,13},{6,14},{7,15},{8,0},{9,1},... | collective-permute-start | bytes 393224 | tf_op jit(solution)/shard_map/ppermute | solution.py:285
  38.5 5.7 %collective-permute-done.11.far_ref = bf16[256,256]{1,0:T(8,128)(2,1)S(1)} collective-permute-done((bf16[256,256]{1,0:T(8,128)(2,1)S(1)}, bf16[256,256]{1,0:T(8,128)(2,1)S(1)}, u32[]{:S(2)}, u32[]{:S(2)}) %collective-permute-start.11) | collective-permute-done | bytes 131104 | tf_op jit(solution)/shard_map/ppermute | solution.py:285
  44.3 1.5 %collective-permute-done.13.refs_1_ = bf16[2,192,256]{2,1,0:T(8,128)(2,1)S(1)} collective-permute-done((bf16[2,192,256]{2,1,0:T(8,128)(2,1)S(1)}, bf16[2,192,256]{2,1,0:T(8,128)(2,1)S(1)}, u32[]{:S(2)}, u32[]{:S(2)}) %collective-permute-start.13) | collective-permute-done | bytes 196640 | tf_op jit(solution)/shard_map/ppermute | solution.py:281
  45.8 0.8 %items.1 = (f32[256,256]{1,0:T(8,128)S(1)}, f32[256,256]{1,0:T(8,128)S(1)}, f32[256,1]{1,0:T(8,128)S(1)}, bf16[256,256]{1,0:T(8,128)(2,1)S(1)}) custom-call(s32[8,192]{1,0:T(8,128)S(1)} %get-tuple-element.39.bag_ref, bf16[256,256]{1,0:T(8,128)(2,1)S(1)} %collective-permute-done.11.far_ref, bf16[4,192,256]{2,1,0:T(8,128)(2,1)S(1)} %gather.6.same_ref, ...), custom_call_target="tpu_custom_call" | custom-call | tf_op jit(solution)/shard_map/items/pallas_call | solution.py:344
  46.6 1.6 %collective-permute-start.16 = (bf16[256,256]{1,0:T(8,128)(2,1)S(1)}, bf16[256,256]{1,0:T(8,128)(2,1)S(1)}, u32[]{:S(2)}, u32[]{:S(2)}) collective-permute-start(bf16[256,256]{1,0:T(8,128)(2,1)S(1)} %get-tuple-element.58.refs_1_.refs_2_), channel_id=1, source_target_pairs={{0,16},{16,0},{1,17},{17,1},{2,18},{18,2},{3,19},{19,3},{4,20},{20... | collective-permute-start | bytes 393224 | tf_op jit(solution)/shard_map/ppermute | solution.py:251
  48.2 2.0 %collective-permute-done.15.far_ref = bf16[256,256]{1,0:T(8,128)(2,1)S(1)} collective-permute-done((bf16[256,256]{1,0:T(8,128)(2,1)S(1)}, bf16[256,256]{1,0:T(8,128)(2,1)S(1)}, u32[]{:S(2)}, u32[]{:S(2)}) %collective-permute-start.15) | collective-permute-done | bytes 131104 | tf_op jit(solution)/shard_map/ppermute | solution.py:285
  50.2 2.1 %tower.1 = (f32[256,256]{1,0:T(8,128)S(1)}, f32[256,1]{1,0:T(8,128)S(1)}, bf16[256,256]{1,0:T(8,128)(2,1)S(1)}, f32[256,4096]{1,0:T(8,128)S(1)}) custom-call(f32[256,256]{1,0:T(8,128)S(1)} %get-tuple-element.55.near_ref, bf16[256,256]{1,0:T(8,128)(2,1)S(1)} %collective-permute-done.15.far_ref, bf16[256,4096]{1,0:T(8,128)(2,1)S(1)} %copy-done, ...), custom_call_target="tpu_custom_call" | custom-call | tf_op jit(solution)/shard_map/tower/pallas_call | solution.py:356
  52.2 1.6 %collective-permute-start.17 = (bf16[256,256]{1,0:T(8,128)(2,1)S(1)}, bf16[256,256]{1,0:T(8,128)(2,1)S(1)}, u32[]{:S(2)}, u32[]{:S(2)}) collective-permute-start(bf16[256,256]{1,0:T(8,128)(2,1)S(1)} %get-tuple-element.57.refs_0_), channel_id=1, source_target_pairs={{0,16},{16,0},{1,17},{17,1},{2,18},{18,2},{3,19},{19,3},{4,20},{20... | collective-permute-start | bytes 393224 | tf_op jit(solution)/shard_map/ppermute | solution.py:251
  53.8 3.0 %query_grads.1 = (f32[1,256]{1,0:T(1,128)}, f32[256,256]{1,0:T(8,128)}, f32[256,256]{1,0:T(8,128)S(1)}) custom-call(bf16[256,256]{1,0:T(8,128)(2,1)S(1)} %get-tuple-element.57.refs_0_, bf16[256,256]{1,0:T(8,128)(2,1)S(1)} %get-tuple-element.58.refs_1_.refs_2_, bf16[256,256]{1,0:T(8,128)(2,1)S(1)} %collective-permute-done.16.refs_2_.refs_3_, ...), custom_call_target="tpu_custom_call" | custom-call | tf_op jit(solution)/shard_map/query_grads/pallas_call | solution.py:368
  57.3 1.4 %item_grads.1 = f32[256,256]{1,0:T(8,128)} custom-call(bf16[256,256]{1,0:T(8,128)(2,1)S(1)} %get-tuple-element.57.refs_0_, bf16[256,256]{1,0:T(8,128)(2,1)S(1)} %collective-permute-done.17.refs_1_, bf16[256,256]{1,0:T(8,128)(2,1)S(1)} %get-tuple-element.58.refs_1_.refs_2_, bf16[256,256]{1,0:T(8,128)(2,1)S(1)} %collective-permute-done.16.refs_2_.refs_3_, ...), custom_call_target="tpu_custom_call" | custom-call | tf_op jit(solution)/shard_map/item_grads/pallas_call | solution.py:378
  (24 shorter events, 4.0 us)
Async XLA Ops:
  1.3 7.1 %collective-permute-start.2 = (s32[256,8]{0,1:T(8,128)S(1)}, s32[256,8]{0,1:T(8,128)S(1)}, u32[]{:S(2)}, u32[]{:S(2)}) collective-permute-start(s32[256,8]{0,1:T(8,128)S(1)} %multiply_add_fusion), channel_id=1, source_target_pairs={{0,9},{1,8},{2,11},{3,10},{4,13},{5,12},{6,15},{7,14},{8,1},{9,0},... | collective-permute-start | bytes 24584 | tf_op jit(solution)/shard_map/ppermute | solution.py:285
  4.8 4.5 %collective-permute-start.1 = (s32[256,8]{0,1:T(8,128)S(1)}, s32[256,8]{0,1:T(8,128)S(1)}, u32[]{:S(2)}, u32[]{:S(2)}) collective-permute-start(s32[256,8]{0,1:T(8,128)S(1)} %multiply_add_fusion), channel_id=1, source_target_pairs={{0,8},{1,9},{2,10},{3,11},{4,12},{5,13},{6,14},{7,15},{8,0},{9,1},... | collective-permute-start | bytes 24584 | tf_op jit(solution)/shard_map/ppermute | solution.py:285
  5.4 3.9 %collective-permute-start = (s32[256,8]{0,1:T(8,128)S(1)}, s32[256,8]{0,1:T(8,128)S(1)}, u32[]{:S(2)}, u32[]{:S(2)}) collective-permute-start(s32[256,8]{0,1:T(8,128)S(1)} %multiply_add_fusion), channel_id=1, source_target_pairs={{0,1},{1,0},{2,3},{3,2},{4,5},{5,4},{6,7},{7,6},{8,9},{9,8},{10,11... | collective-permute-start | bytes 24584 | tf_op jit(solution)/shard_map/ppermute | solution.py:281
  5.5 2.2 %copy-start.2 = (bf16[8192,256]{1,0:T(8,128)(2,1)S(1)}, bf16[8192,256]{1,0:T(8,128)(2,1)}, u32[]{:S(2)}) copy-start(bf16[8192,256]{1,0:T(8,128)(2,1)} %table_ref.1) | copy-start | bytes 12582916
  10.5 4.6 %collective-permute-start.3 = (s32[4,192]{1,0:T(4,128)S(1)}, s32[4,192]{1,0:T(4,128)S(1)}, u32[]{:S(2)}, u32[]{:S(2)}) collective-permute-start(s32[4,192]{1,0:T(4,128)S(1)} %get-tuple-element.41), channel_id=1, source_target_pairs={{0,6},{1,7},{2,4},{3,5},{4,2},{5,3},{6,0},{7,1},{8,14},{9,15},{10,... | collective-permute-start | bytes 9224 | tf_op jit(solution)/shard_map/ppermute | solution.py:281
  13.1 3.6 %collective-permute-start.4 = (s32[4,192]{1,0:T(4,128)S(1)}, s32[4,192]{1,0:T(4,128)S(1)}, u32[]{:S(2)}, u32[]{:S(2)}) collective-permute-start(s32[4,192]{1,0:T(4,128)S(1)} %get-tuple-element.42), channel_id=1, source_target_pairs={{0,4},{1,5},{2,6},{3,7},{4,0},{5,1},{6,2},{7,3},{8,12},{9,13},{10,... | collective-permute-start | bytes 9224 | tf_op jit(solution)/shard_map/ppermute | solution.py:281
  13.5 3.6 %collective-permute-start.5 = (s32[4,192]{1,0:T(4,128)S(1)}, s32[4,192]{1,0:T(4,128)S(1)}, u32[]{:S(2)}, u32[]{:S(2)}) collective-permute-start(s32[4,192]{1,0:T(4,128)S(1)} %get-tuple-element.43), channel_id=1, source_target_pairs={{0,2},{1,3},{2,0},{3,1},{4,6},{5,7},{6,4},{7,5},{8,10},{9,11},{10,... | collective-permute-start | bytes 9224 | tf_op jit(solution)/shard_map/ppermute | solution.py:281
  18.5 1.8 %collective-permute-start.6 = (bf16[4,192,256]{2,1,0:T(8,128)(2,1)S(1)}, bf16[4,192,256]{2,1,0:T(8,128)(2,1)S(1)}, u32[]{:S(2)}, u32[]{:S(2)}) collective-permute-start(bf16[4,192,256]{2,1,0:T(8,128)(2,1)S(1)} %gather.5), channel_id=1, source_target_pairs={{0,1},{1,0},{2,3},{3,2},{4,5},{5,4},{6,7},{7,6},{8,9},{9,8},{10,11... | collective-permute-start | bytes 1179656 | tf_op jit(solution)/shard_map/ppermute | solution.py:281
  21.7 5.1 %collective-permute-start.7 = (bf16[4,192,256]{2,1,0:T(8,128)(2,1)S(1)}, bf16[4,192,256]{2,1,0:T(8,128)(2,1)S(1)}, u32[]{:S(2)}, u32[]{:S(2)}) collective-permute-start(bf16[4,192,256]{2,1,0:T(8,128)(2,1)S(1)} %gather.7), channel_id=1, source_target_pairs={{0,1},{1,0},{2,3},{3,2},{4,5},{5,4},{6,7},{7,6},{8,9},{9,8},{10,11... | collective-permute-start | bytes 1179656 | tf_op jit(solution)/shard_map/ppermute | solution.py:281
  21.9 8.7 %collective-permute-start.8 = (bf16[2,192,256]{2,1,0:T(8,128)(2,1)S(1)}, bf16[2,192,256]{2,1,0:T(8,128)(2,1)S(1)}, u32[]{:S(2)}, u32[]{:S(2)}) collective-permute-start(bf16[2,192,256]{2,1,0:T(8,128)(2,1)S(1)} %get-tuple-element.50), channel_id=1, source_target_pairs={{0,6},{1,7},{2,4},{3,5},{4,2},{5,3},{6,0},{7,1},{8,14},{9,15},{10,... | collective-permute-start | bytes 589832 | tf_op jit(solution)/shard_map/ppermute | solution.py:281
  23.4 26.7 %copy-start = (bf16[256,4096]{1,0:T(8,128)(2,1)S(1)}, bf16[256,4096]{1,0:T(8,128)(2,1)}, u32[]{:S(2)}) copy-start(bf16[256,4096]{1,0:T(8,128)(2,1)} %refs_3_.1) | copy-start | bytes 6291460
  23.4 26.7 %copy-start.1 = (bf16[4096,256]{1,0:T(8,128)(2,1)S(1)}, bf16[4096,256]{1,0:T(8,128)(2,1)}, u32[]{:S(2)}) copy-start(bf16[4096,256]{1,0:T(8,128)(2,1)} %refs_4_.1) | copy-start | bytes 6291460
  23.5 10.4 %collective-permute-start.9 = (bf16[2,192,256]{2,1,0:T(8,128)(2,1)S(1)}, bf16[2,192,256]{2,1,0:T(8,128)(2,1)S(1)}, u32[]{:S(2)}, u32[]{:S(2)}) collective-permute-start(bf16[2,192,256]{2,1,0:T(8,128)(2,1)S(1)} %get-tuple-element.51), channel_id=1, source_target_pairs={{0,4},{1,5},{2,6},{3,7},{4,0},{5,1},{6,2},{7,3},{8,12},{9,13},{10,... | collective-permute-start | bytes 589832 | tf_op jit(solution)/shard_map/ppermute | solution.py:281
  23.9 11.0 %collective-permute-start.10 = (bf16[2,192,256]{2,1,0:T(8,128)(2,1)S(1)}, bf16[2,192,256]{2,1,0:T(8,128)(2,1)S(1)}, u32[]{:S(2)}, u32[]{:S(2)}) collective-permute-start(bf16[2,192,256]{2,1,0:T(8,128)(2,1)S(1)} %get-tuple-element.46), channel_id=1, source_target_pairs={{0,2},{1,3},{2,0},{3,1},{4,6},{5,7},{6,4},{7,5},{8,10},{9,11},{10,... | collective-permute-start | bytes 589832 | tf_op jit(solution)/shard_map/ppermute | solution.py:281
  26.8 17.4 %collective-permute-start.12 = (bf16[2,192,256]{2,1,0:T(8,128)(2,1)S(1)}, bf16[2,192,256]{2,1,0:T(8,128)(2,1)S(1)}, u32[]{:S(2)}, u32[]{:S(2)}) collective-permute-start(bf16[2,192,256]{2,1,0:T(8,128)(2,1)S(1)} %get-tuple-element.53), channel_id=1, source_target_pairs={{0,6},{1,7},{2,4},{3,5},{4,2},{5,3},{6,0},{7,1},{8,14},{9,15},{10,... | collective-permute-start | bytes 589832 | tf_op jit(solution)/shard_map/ppermute | solution.py:281
  28.4 17.4 %collective-permute-start.13 = (bf16[2,192,256]{2,1,0:T(8,128)(2,1)S(1)}, bf16[2,192,256]{2,1,0:T(8,128)(2,1)S(1)}, u32[]{:S(2)}, u32[]{:S(2)}) collective-permute-start(bf16[2,192,256]{2,1,0:T(8,128)(2,1)S(1)} %get-tuple-element.54), channel_id=1, source_target_pairs={{0,4},{1,5},{2,6},{3,7},{4,0},{5,1},{6,2},{7,3},{8,12},{9,13},{10,... | collective-permute-start | bytes 589832 | tf_op jit(solution)/shard_map/ppermute | solution.py:281
  30.6 15.2 %collective-permute-start.14 = (bf16[2,192,256]{2,1,0:T(8,128)(2,1)S(1)}, bf16[2,192,256]{2,1,0:T(8,128)(2,1)S(1)}, u32[]{:S(2)}, u32[]{:S(2)}) collective-permute-start(bf16[2,192,256]{2,1,0:T(8,128)(2,1)S(1)} %get-tuple-element.48), channel_id=1, source_target_pairs={{0,2},{1,3},{2,0},{3,1},{4,6},{5,7},{6,4},{7,5},{8,10},{9,11},{10,... | collective-permute-start | bytes 589832 | tf_op jit(solution)/shard_map/ppermute | solution.py:281
  35.6 8.7 %collective-permute-start.11 = (bf16[256,256]{1,0:T(8,128)(2,1)S(1)}, bf16[256,256]{1,0:T(8,128)(2,1)S(1)}, u32[]{:S(2)}, u32[]{:S(2)}) collective-permute-start(bf16[256,256]{1,0:T(8,128)(2,1)S(1)} %get-tuple-element.52), channel_id=1, source_target_pairs={{0,8},{1,9},{2,10},{3,11},{4,12},{5,13},{6,14},{7,15},{8,0},{9,1},... | collective-permute-start | bytes 393224 | tf_op jit(solution)/shard_map/ppermute | solution.py:285
  37.3 12.8 %collective-permute-start.15 = (bf16[256,256]{1,0:T(8,128)(2,1)S(1)}, bf16[256,256]{1,0:T(8,128)(2,1)S(1)}, u32[]{:S(2)}, u32[]{:S(2)}) collective-permute-start(bf16[256,256]{1,0:T(8,128)(2,1)S(1)} %get-tuple-element.56), channel_id=1, source_target_pairs={{0,8},{1,9},{2,10},{3,11},{4,12},{5,13},{6,14},{7,15},{8,0},{9,1},... | collective-permute-start | bytes 393224 | tf_op jit(solution)/shard_map/ppermute | solution.py:285
  46.6 7.2 %collective-permute-start.16 = (bf16[256,256]{1,0:T(8,128)(2,1)S(1)}, bf16[256,256]{1,0:T(8,128)(2,1)S(1)}, u32[]{:S(2)}, u32[]{:S(2)}) collective-permute-start(bf16[256,256]{1,0:T(8,128)(2,1)S(1)} %get-tuple-element.58.refs_1_.refs_2_), channel_id=1, source_target_pairs={{0,16},{16,0},{1,17},{17,1},{2,18},{18,2},{3,19},{19,3},{4,20},{20... | collective-permute-start | bytes 393224 | tf_op jit(solution)/shard_map/ppermute | solution.py:251
  52.2 5.0 %collective-permute-start.17 = (bf16[256,256]{1,0:T(8,128)(2,1)S(1)}, bf16[256,256]{1,0:T(8,128)(2,1)S(1)}, u32[]{:S(2)}, u32[]{:S(2)}) collective-permute-start(bf16[256,256]{1,0:T(8,128)(2,1)S(1)} %get-tuple-element.57.refs_0_), channel_id=1, source_target_pairs={{0,16},{16,0},{1,17},{17,1},{2,18},{18,2},{3,19},{19,3},{4,20},{20... | collective-permute-start | bytes 393224 | tf_op jit(solution)/shard_map/ppermute | solution.py:251

commit v2 on v1

--- a/solution.py
+++ b/solution.py
@@ -102,21 +102,32 @@
     lax.fori_loop(0, table_ref.shape[0] // step, widen, 0)
 
 
-def gather_kernel(chips, asker, *refs):
-    wanted, wide_ref, out_ref, stage = refs[:chips], refs[chips], refs[chips + 1], refs[-1]
-    _, capacity, width = out_ref.shape
+def gather_kernel(chips, askers, *refs):
+    wanted, wide_ref, refs = refs[:chips], refs[chips], refs[chips + 1 :]
+    outs, (index_ref, stage, sems) = refs[: len(askers)], refs[len(askers) :]
+    _, capacity, width = outs[0].shape
     group = 16
-    for j in range(chips):
-        index_ref = wanted[chips - 1 - j]
-        for base in range(0, capacity, group):
-            found = [wide_ref[pl.ds(index_ref[asker, base + i], 2), :] for i in range(group)]
-            for i in range(group):
-                stage[pl.ds(2 * (base + i), 2), :] = found[i]
-        for part in range(2):
-            values = stage[pl.ds(part, capacity, stride=2), :]
-            out_ref[j, :, part * (width // 2) : (part + 1) * (width // 2)] = values.astype(
-                jnp.bfloat16
-            )
+    copies = [
+        pltpu.make_async_copy(wanted[chips - 1 - j], index_ref.at[j], sems.at[j])
+        for j in range(chips)
+    ]
+    for copy in copies:
+        copy.start()
+    for copy in copies:
+        copy.wait()
+    for asker, out_ref in zip(askers, outs):
+        for j in range(chips):
+            for base in range(0, capacity, group):
+                found = [
+                    wide_ref[pl.ds(index_ref[j, asker, base + i], 2), :] for i in range(group)
+                ]
+                for i in range(group):
+                    stage[pl.ds(2 * (base + i), 2), :] = found[i]
+            for part in range(2):
+                values = stage[pl.ds(part, capacity, stride=2), :]
+                out_ref[j, :, part * (width // 2) : (part + 1) * (width // 2)] = values.astype(
+                    jnp.bfloat16
+                )
 
 
 def pack_kernel(chips, same_ref, swapped_ref, *out_refs):
@@ -170,7 +181,7 @@
     total = None
     for at in range(0, first_ref.shape[1], step):
         pre = dot(query_in, first_ref[:, at : at + step])
-        sigma = 1.0 / (1.0 + jnp.exp(-pre))
+        sigma = 0.5 + 0.5 * jnp.tanh(0.5 * pre)
         hidden = pre * sigma
         slope_ref[:, at : at + step] = sigma * (1.0 + pre * (1.0 - sigma))
         part = dot(hidden.astype(jnp.bfloat16), second_ref[at : at + step, :])
@@ -223,26 +234,17 @@
 
 def item_grad_kernel(blocks, *refs):
     queries, items, refs = refs[:blocks], refs[blocks : 2 * blocks], refs[2 * blocks :]
-    item_sum_ref, unit_ref, scale_ref, grad_ref, all_queries, all_items = refs
-    for b in range(blocks):
-        all_queries[b] = queries[b][...]
-        all_items[b] = items[b][...]
-    own_item = all_items[0]
-
-    def add(i, total):
-        query = all_queries[i]
-        own_exps = group_exps(query, own_item)
-
-        def add_total(j, sums):
-            return sums + row_sums(group_exps(query, all_items[j]))
-
-        sums = lax.fori_loop(1, blocks, add_total, row_sums(own_exps), unroll=blocks == 2)
-        probs = (own_exps * (1.0 / sums)).astype(jnp.bfloat16)
-        return total + col_dot(probs, query)
-
-    item_sum = lax.fori_loop(1, blocks, add, item_sum_ref[...], unroll=blocks == 2)
+    item_sum_ref, unit_ref, scale_ref, grad_ref = refs
+    item_sum = item_sum_ref[...]
+    for i in range(1, blocks):
+        query = queries[i][...]
+        own_exps = group_exps(query, items[0][...])
+        total = row_sums(own_exps)
+        for j in range(1, blocks):
+            total = total + row_sums(group_exps(query, items[j][...]))
+        item_sum = item_sum + col_dot((own_exps * (1.0 / total)).astype(jnp.bfloat16), query)
     grad_ref[...] = unit_backward(
-        INV_TEMP * (item_sum - all_queries[0].astype(jnp.float32)), unit_ref[...], scale_ref[...]
+        INV_TEMP * (item_sum - queries[0][...].astype(jnp.float32)), unit_ref[...], scale_ref[...]
     )
 
 
@@ -280,19 +282,18 @@
         ]
         return lax.ppermute(values, "table", route)
 
-    def to_mirror(values, flip=0):
-        route = [(t, ((t + half) % shards) ^ flip) for t in range(shards)]
-        return lax.ppermute(values, "table", route)
+    def to_mirror(values):
+        return lax.ppermute(values, "table", [(t, (t + half) % shards) for t in range(shards)])
 
     code = owner_ids * id_table.shape[0] + row_ids
-    codes = [code, to_chip(code, 0, 1), to_mirror(code), to_mirror(code, 1)]
+    mirror_code = to_mirror(code)
+    codes = [code, to_chip(code, 0, 1), mirror_code, to_chip(mirror_code, 0, 1)]
     wide = pl.pallas_call(
         widen_kernel,
         out_shape=struct((2 * id_table.shape[0], width // 2), f32),
         compiler_params=params(8),
         name="widen",
     )(id_table)
-    *codes, wide = lax.optimization_barrier((*codes, wide))
     near_bags, far_bags, *requests = pl.pallas_call(
         functools.partial(route_kernel, relative, id_table.shape[0]),
         out_shape=[struct((half, capacity), jnp.int32)] * 2
@@ -302,20 +303,24 @@
     )(*[c.T for c in codes])
     wanted = [to_chip(requests[j], j) for j in reversed(range(chips))][::-1]
 
-    def gather(asker, wide):
+    def gather(askers):
         return pl.pallas_call(
-            functools.partial(gather_kernel, chips, asker),
-            in_specs=[pl.BlockSpec(memory_space=pltpu.SMEM)] * chips
+            functools.partial(gather_kernel, chips, askers),
+            in_specs=[pl.BlockSpec(memory_space=pl.ANY)] * chips
             + [pl.BlockSpec(memory_space=pltpu.VMEM)],
-            out_shape=struct((chips, capacity, width), bf),
-            scratch_shapes=[pltpu.VMEM((2 * capacity, width // 2), f32)],
+            out_shape=[struct((chips, capacity, width), bf)] * len(askers),
+            scratch_shapes=[
+                pltpu.SMEM((chips, 4, capacity), jnp.int32),
+                pltpu.VMEM((2 * capacity, width // 2), f32),
+                pltpu.SemaphoreType.DMA((chips,)),
+            ],
             compiler_params=params(8),
             name="gather",
         )(*wanted[::-1], wide)
 
-    def answered(first, wide, order):
-        swapped = to_chip(gather(first + 1, wide), 0, 1)
-        same = gather(first, wide)
+    order = list(range(chips - 1, 0, -1))
+
+    def answered(same, swapped):
         messages = pl.pallas_call(
             functools.partial(pack_kernel, chips),
             out_shape=[struct((2, capacity, width), bf)] * (chips - 1),
@@ -328,10 +333,10 @@
             arrived.append(to_chip(messages[chips - 1 - back], back))
         return (same, swapped, *arrived), messages
 
-    order = list(range(chips - 1, 0, -1))
-    far_rows, far_messages = answered(2, wide, order)
-    wide, _ = lax.optimization_barrier((wide, far_messages[-1]))
-    near_rows, near_messages = answered(0, wide, order)
+    far_other, near_other = [to_chip(rows, 0, 1) for rows in gather((3, 1))]
+    far_same, near_same = gather((2, 0))
+    far_rows, _ = answered(far_same, far_other)
+    near_rows, near_messages = answered(near_same, near_other)
     far_bags, _ = lax.optimization_barrier((far_bags, near_messages[-1]))
     far_query, far_item = pl.pallas_call(
         functools.partial(far_kernel, order),
@@ -378,7 +383,6 @@
     item_grad = pl.pallas_call(
         functools.partial(item_grad_kernel, blocks),
         out_shape=struct((pairs, width), f32),
-        scratch_shapes=[pltpu.VMEM((blocks, pairs, width), bf)] * 2,
         compiler_params=params(12),
         name="item_grads",
     )(*queries, *items, own_sum, item_unit, item_scale)

time: 58.9 us -> 57.9 us (0.983)
  starting transfers between devices: 20.1 us -> 22 us
  Pallas kernels: 15.3 us -> 13.6 us
  waiting for transfers between devices: 19.6 us -> 18.2 us
    ppermute x4 -> x3, waiting for transfers between devices: 8.69 us -> 1.67 us  [to_mirror(): lax.ppermute(values, 'table', [(t, (t + half) % shards) for t in range(sh...]
    ppermute x12 -> x13, waiting for transfers between devices: 10.5 us -> 16.1 us  [to_chip(): return lax.ppermute(values, 'table', route)]
    ppermute x12 -> x13, starting transfers between devices: 9.94 us -> 11.9 us  [to_chip(): return lax.ppermute(values, 'table', route)]
    pallas_call x4 -> x2, Pallas kernels: 5.44 us -> 3.9 us  [gather(): pl.pallas_call(functools.partial(gather_kernel, chips, askers), in_specs=...]
    ppermute x4 -> x3, starting transfers between devices: 7.08 us -> 7.03 us  [to_mirror(): lax.ppermute(values, 'table', [(t, (t + half) % shards) for t in range(sh...]
  transfers between devices with their start and end apart: 18 -> 18, of which waited for: 12 -> 10; matrix products, arithmetic and copies ran while one was open for 0% -> 0% of each run, Pallas kernels for 17% -> 16%
where the time goes in v2:
time: 57.9 us; the launch traced here: 57.6 us
  starting transfers between devices  22 us (38%)
  waiting for transfers between devices  18.2 us (31%)
  Pallas kernels  13.6 us (23%)
  local copies, waits for them, and re-layouts  2.2 us (4%)
  between operations  0.75 us (1%)
  other arithmetic  0.72 us (1%)
    ppermute x13, waiting for transfers between devices, to_chip(): return lax.ppermute(values, 'table', route)  16.1 us
    ppermute x13, starting transfers between devices, to_chip(): return lax.ppermute(values, 'table', route)  11.9 us
    ppermute x3, starting transfers between devices, to_mirror(): lax.ppermute(values, 'table', [(t, (t + half) % shards) for t in range(sh...  7.03 us
    pallas_call x2, Pallas kernels, gather(): pl.pallas_call(functools.partial(gather_kernel, chips, askers), in_specs=...  3.9 us
    ppermute x2, starting transfers between devices, rotated(): lax.ppermute(shard, axis, [(i, (i + by) % count) for i in range(count)])  3.12 us
    pallas_call x1, Pallas kernels, local(): pl.pallas_call(functools.partial(query_grad_kernel, blocks), out_shape=[s...  3.03 us
    unnamed x6, local copies, waits for them, and re-layouts  2.2 us
    pallas_call x1, Pallas kernels, local(): pl.pallas_call(tower_kernel, out_shape=[struct((pairs, width), f32), stru...  1.95 us
  transfers between devices with their start and end apart: 18, of which 10 were waited for; matrix products, arithmetic and copies ran while one was open for 0% of the time, Pallas kernels for 16%

profile of v2, /device:TPU:0, one launch (start us, length us, event | category | flops | bytes accessed | tf_op | source)
XLA Modules:
  0.0 57.6 jit_solution(11890177427238906782)
XLA Ops:
  0.6 0.7 %multiply_add_fusion = s32[256,8]{0,1:T(8,128)S(1)} fusion(s32[256,8]{0,1:T(8,128)} %param.9, s32[256,8]{0,1:T(8,128)} %param.8), kind=kLoop, calls=%fused_computation | loop fusion | flops 4096 | bytes 24576 | tf_op jit(solution)/shard_map/add | solution.py:288
  1.3 4.0 %collective-permute-start.1 = (s32[256,8]{0,1:T(8,128)S(1)}, s32[256,8]{0,1:T(8,128)S(1)}, u32[]{:S(2)}, u32[]{:S(2)}) collective-permute-start(s32[256,8]{0,1:T(8,128)S(1)} %multiply_add_fusion), channel_id=1, source_target_pairs={{0,8},{1,9},{2,10},{3,11},{4,12},{5,13},{6,14},{7,15},{8,0},{9,1},... | collective-permute-start | bytes 24584 | tf_op jit(solution)/shard_map/ppermute | solution.py:286
  5.4 1.6 %collective-permute-done.1 = s32[256,8]{0,1:T(8,128)S(1)} collective-permute-done((s32[256,8]{0,1:T(8,128)S(1)}, s32[256,8]{0,1:T(8,128)S(1)}, u32[]{:S(2)}, u32[]{:S(2)}) %collective-permute-start.1) | collective-permute-done | bytes 8224 | tf_op jit(solution)/shard_map/ppermute | solution.py:286
  7.0 1.2 %collective-permute-done.2 = s32[256,8]{0,1:T(8,128)S(1)} collective-permute-done((s32[256,8]{0,1:T(8,128)S(1)}, s32[256,8]{0,1:T(8,128)S(1)}, u32[]{:S(2)}, u32[]{:S(2)}) %collective-permute-start.2) | collective-permute-done | bytes 8224 | tf_op jit(solution)/shard_map/ppermute | solution.py:283
  8.2 1.1 %route.1 = (s32[8,192]{1,0:T(8,128)S(1)}, s32[8,192]{1,0:T(8,128)S(1)}, s32[4,192]{1,0:T(4,128)S(1)}, s32[4,192]{1,0:T(4,128)S(1)}, s32[4,192]{1,0:T(4,128)S(1)}, /*index=5*/s32[4,192]{1,0:T(4,128)S(1)}) custom-call(s32[8,256]{1,0:T(8,128)S(1)} %bitcast.5, s32[8,256]{1,0:T(8,128)S(1)} %bitcast.7, s32[8,256]{1,0:T(8,128)S(1)} %bitcast.6, s32[8,256]{1,0:T(8,128)S(1)} %bitcast.8), custom_call_target="tpu_custom_call" | custom-call | tf_op jit(solution)/shard_map/route/pallas_call | solution.py:297
  9.3 2.9 %collective-permute-start.3 = (s32[4,192]{1,0:T(4,128)S(1)}, s32[4,192]{1,0:T(4,128)S(1)}, u32[]{:S(2)}, u32[]{:S(2)}) collective-permute-start(s32[4,192]{1,0:T(4,128)S(1)} %get-tuple-element.35), channel_id=1, source_target_pairs={{0,6},{1,7},{2,4},{3,5},{4,2},{5,3},{6,0},{7,1},{8,14},{9,15},{10,... | collective-permute-start | bytes 9224 | tf_op jit(solution)/shard_map/ppermute | solution.py:283
  12.2 0.4 collective-permute-start.4
  12.9 2.2 %copy-done.2 = bf16[8192,256]{1,0:T(8,128)(2,1)S(1)} copy-done((bf16[8192,256]{1,0:T(8,128)(2,1)S(1)}, bf16[8192,256]{1,0:T(8,128)(2,1)}, u32[]{:S(2)}) %copy-start.2) | copy-done | bytes 4194328
  15.1 0.7 %widen.1.refs_4_ = f32[16384,128]{1,0:T(8,128)S(1)} custom-call(bf16[8192,256]{1,0:T(8,128)(2,1)S(1)} %copy-done.2), custom_call_target="tpu_custom_call" | custom-call | tf_op jit(solution)/shard_map/widen/pallas_call | solution.py:291
  15.8 0.4 collective-permute-done.5.refs_2_
  16.3 2.0 %gather.3 = (bf16[4,192,256]{2,1,0:T(8,128)(2,1)S(1)}, bf16[4,192,256]{2,1,0:T(8,128)(2,1)S(1)}) custom-call(s32[4,192]{1,0:T(4,128)S(1)} %collective-permute-done.3.refs_0_, s32[4,192]{1,0:T(4,128)S(1)} %collective-permute-done.4.refs_1_, s32[4,192]{1,0:T(4,128)S(1)} %collective-permute-done.5.refs_2_, s32[4,192]{1,0:T(4,128)S(1)} %get-tuple-element.38.refs_3_, ...), custom_call_target="tpu_custom_call" | custom-call | tf_op jit(solution)/shard_map/gather/pallas_call | solution.py:307
  18.3 0.5 collective-permute-start.6
  18.8 1.9 %gather.2 = (bf16[4,192,256]{2,1,0:T(8,128)(2,1)S(1)}, bf16[4,192,256]{2,1,0:T(8,128)(2,1)S(1)}) custom-call(s32[4,192]{1,0:T(4,128)S(1)} %collective-permute-done.3.refs_0_, s32[4,192]{1,0:T(4,128)S(1)} %collective-permute-done.4.refs_1_, s32[4,192]{1,0:T(4,128)S(1)} %collective-permute-done.5.refs_2_, s32[4,192]{1,0:T(4,128)S(1)} %get-tuple-element.38.refs_3_, ...), custom_call_target="tpu_custom_call" | custom-call | tf_op jit(solution)/shard_map/gather/pallas_call | solution.py:307
  20.9 2.4 %collective-permute-start.8 = (bf16[2,192,256]{2,1,0:T(8,128)(2,1)S(1)}, bf16[2,192,256]{2,1,0:T(8,128)(2,1)S(1)}, u32[]{:S(2)}, u32[]{:S(2)}) collective-permute-start(bf16[2,192,256]{2,1,0:T(8,128)(2,1)S(1)} %get-tuple-element.45), channel_id=1, source_target_pairs={{0,6},{1,7},{2,4},{3,5},{4,2},{5,3},{6,0},{7,1},{8,14},{9,15},{10,... | collective-permute-start | bytes 589832 | tf_op jit(solution)/shard_map/ppermute | solution.py:283
  23.3 0.4 collective-permute-start.9
  23.7 0.7 %collective-permute-start.10 = (bf16[2,192,256]{2,1,0:T(8,128)(2,1)S(1)}, bf16[2,192,256]{2,1,0:T(8,128)(2,1)S(1)}, u32[]{:S(2)}, u32[]{:S(2)}) collective-permute-start(bf16[2,192,256]{2,1,0:T(8,128)(2,1)S(1)} %get-tuple-element.47), channel_id=1, source_target_pairs={{0,2},{1,3},{2,0},{3,1},{4,6},{5,7},{6,4},{7,5},{8,10},{9,11},{10,... | collective-permute-start | bytes 589832 | tf_op jit(solution)/shard_map/ppermute | solution.py:283
  24.5 2.4 %collective-permute-start.12 = (bf16[2,192,256]{2,1,0:T(8,128)(2,1)S(1)}, bf16[2,192,256]{2,1,0:T(8,128)(2,1)S(1)}, u32[]{:S(2)}, u32[]{:S(2)}) collective-permute-start(bf16[2,192,256]{2,1,0:T(8,128)(2,1)S(1)} %get-tuple-element.49), channel_id=1, source_target_pairs={{0,6},{1,7},{2,4},{3,5},{4,2},{5,3},{6,0},{7,1},{8,14},{9,15},{10,... | collective-permute-start | bytes 589832 | tf_op jit(solution)/shard_map/ppermute | solution.py:283
  26.9 0.4 collective-permute-start.13
  27.3 2.3 %collective-permute-done.8.refs_0_ = bf16[2,192,256]{2,1,0:T(8,128)(2,1)S(1)} collective-permute-done((bf16[2,192,256]{2,1,0:T(8,128)(2,1)S(1)}, bf16[2,192,256]{2,1,0:T(8,128)(2,1)S(1)}, u32[]{:S(2)}, u32[]{:S(2)}) %collective-permute-start.8) | collective-permute-done | bytes 196640 | tf_op jit(solution)/shard_map/ppermute | solution.py:283
  29.6 1.3 %collective-permute-start.14 = (bf16[2,192,256]{2,1,0:T(8,128)(2,1)S(1)}, bf16[2,192,256]{2,1,0:T(8,128)(2,1)S(1)}, u32[]{:S(2)}, u32[]{:S(2)}) collective-permute-start(bf16[2,192,256]{2,1,0:T(8,128)(2,1)S(1)} %get-tuple-element.41), channel_id=1, source_target_pairs={{0,2},{1,3},{2,0},{3,1},{4,6},{5,7},{6,4},{7,5},{8,10},{9,11},{10,... | collective-permute-start | bytes 589832 | tf_op jit(solution)/shard_map/ppermute | solution.py:283
  31.0 2.7 %collective-permute-done.9.refs_1_ = bf16[2,192,256]{2,1,0:T(8,128)(2,1)S(1)} collective-permute-done((bf16[2,192,256]{2,1,0:T(8,128)(2,1)S(1)}, bf16[2,192,256]{2,1,0:T(8,128)(2,1)S(1)}, u32[]{:S(2)}, u32[]{:S(2)}) %collective-permute-start.9) | collective-permute-done | bytes 196640 | tf_op jit(solution)/shard_map/ppermute | solution.py:283
  33.9 0.7 %far_bags.1 = (bf16[256,256]{1,0:T(8,128)(2,1)S(1)}, bf16[256,256]{1,0:T(8,128)(2,1)S(1)}) custom-call(s32[8,192]{1,0:T(8,128)S(1)} %get-tuple-element.42.bag_ref, bf16[4,192,256]{2,1,0:T(8,128)(2,1)S(1)} %get-tuple-element.43.same_ref, bf16[4,192,256]{2,1,0:T(8,128)(2,1)S(1)} %collective-permute-done.7.swapped_ref, ...), custom_call_target="tpu_custom_call" | custom-call | tf_op jit(solution)/shard_map/far_bags/pallas_call | solution.py:341
  34.6 2.7 %collective-permute-start.11 = (bf16[256,256]{1,0:T(8,128)(2,1)S(1)}, bf16[256,256]{1,0:T(8,128)(2,1)S(1)}, u32[]{:S(2)}, u32[]{:S(2)}) collective-permute-start(bf16[256,256]{1,0:T(8,128)(2,1)S(1)} %get-tuple-element.48), channel_id=1, source_target_pairs={{0,8},{1,9},{2,10},{3,11},{4,12},{5,13},{6,14},{7,15},{8,0},{9,1},... | collective-permute-start | bytes 393224 | tf_op jit(solution)/shard_map/ppermute | solution.py:286
  37.6 0.5 collective-permute-done.12.refs_0_
  38.1 8.7 %collective-permute-done.13.refs_1_ = bf16[2,192,256]{2,1,0:T(8,128)(2,1)S(1)} collective-permute-done((bf16[2,192,256]{2,1,0:T(8,128)(2,1)S(1)}, bf16[2,192,256]{2,1,0:T(8,128)(2,1)S(1)}, u32[]{:S(2)}, u32[]{:S(2)}) %collective-permute-start.13) | collective-permute-done | bytes 196640 | tf_op jit(solution)/shard_map/ppermute | solution.py:283
  46.8 0.8 %items.1 = (f32[256,256]{1,0:T(8,128)S(1)}, f32[256,256]{1,0:T(8,128)S(1)}, f32[256,1]{1,0:T(8,128)S(1)}, bf16[256,256]{1,0:T(8,128)(2,1)S(1)}) custom-call(s32[8,192]{1,0:T(8,128)S(1)} %get-tuple-element.33.bag_ref, bf16[256,256]{1,0:T(8,128)(2,1)S(1)} %collective-permute-done.11.far_ref, bf16[4,192,256]{2,1,0:T(8,128)(2,1)S(1)} %get-tuple-element.39.same_ref, ...), custom_call_target="tpu_custom_call" | custom-call | tf_op jit(solution)/shard_map/items/pallas_call | solution.py:349
  47.6 1.6 %collective-permute-start.16 = (bf16[256,256]{1,0:T(8,128)(2,1)S(1)}, bf16[256,256]{1,0:T(8,128)(2,1)S(1)}, u32[]{:S(2)}, u32[]{:S(2)}) collective-permute-start(bf16[256,256]{1,0:T(8,128)(2,1)S(1)} %get-tuple-element.54.refs_1_.refs_2_), channel_id=1, source_target_pairs={{0,16},{16,0},{1,17},{17,1},{2,18},{18,2},{3,19},{19,3},{4,20},{20... | collective-permute-start | bytes 393224 | tf_op jit(solution)/shard_map/ppermute | solution.py:253
  49.2 2.0 %tower.1 = (f32[256,256]{1,0:T(8,128)S(1)}, f32[256,1]{1,0:T(8,128)S(1)}, bf16[256,256]{1,0:T(8,128)(2,1)S(1)}, f32[256,4096]{1,0:T(8,128)S(1)}) custom-call(f32[256,256]{1,0:T(8,128)S(1)} %get-tuple-element.51.near_ref, bf16[256,256]{1,0:T(8,128)(2,1)S(1)} %collective-permute-done.15.far_ref, bf16[256,4096]{1,0:T(8,128)(2,1)S(1)} %copy-done, ...), custom_call_target="tpu_custom_call" | custom-call | tf_op jit(solution)/shard_map/tower/pallas_call | solution.py:361
  51.2 1.6 %collective-permute-start.17 = (bf16[256,256]{1,0:T(8,128)(2,1)S(1)}, bf16[256,256]{1,0:T(8,128)(2,1)S(1)}, u32[]{:S(2)}, u32[]{:S(2)}) collective-permute-start(bf16[256,256]{1,0:T(8,128)(2,1)S(1)} %get-tuple-element.53.refs_0_), channel_id=1, source_target_pairs={{0,16},{16,0},{1,17},{17,1},{2,18},{18,2},{3,19},{19,3},{4,20},{20... | collective-permute-start | bytes 393224 | tf_op jit(solution)/shard_map/ppermute | solution.py:253
  52.7 3.0 %query_grads.1 = (f32[1,256]{1,0:T(1,128)}, f32[256,256]{1,0:T(8,128)}, f32[256,256]{1,0:T(8,128)S(1)}) custom-call(bf16[256,256]{1,0:T(8,128)(2,1)S(1)} %get-tuple-element.53.refs_0_, bf16[256,256]{1,0:T(8,128)(2,1)S(1)} %get-tuple-element.54.refs_1_.refs_2_, bf16[256,256]{1,0:T(8,128)(2,1)S(1)} %collective-permute-done.16.refs_2_.refs_3_, ...), custom_call_target="tpu_custom_call" | custom-call | tf_op jit(solution)/shard_map/query_grads/pallas_call | solution.py:373
  55.8 0.4 collective-permute-done.17.refs_1_
  56.2 1.4 %item_grads.1 = f32[256,256]{1,0:T(8,128)} custom-call(bf16[256,256]{1,0:T(8,128)(2,1)S(1)} %get-tuple-element.53.refs_0_, bf16[256,256]{1,0:T(8,128)(2,1)S(1)} %collective-permute-done.17.refs_1_, bf16[256,256]{1,0:T(8,128)(2,1)S(1)} %get-tuple-element.54.refs_1_.refs_2_, bf16[256,256]{1,0:T(8,128)(2,1)S(1)} %collective-permute-done.16.refs_2_.refs_3_, ...), custom_call_target="tpu_custom_call" | custom-call | tf_op jit(solution)/shard_map/item_grads/pallas_call | solution.py:383
  (22 shorter events, 1.0 us)
Async XLA Ops:
  1.3 5.7 %collective-permute-start.1 = (s32[256,8]{0,1:T(8,128)S(1)}, s32[256,8]{0,1:T(8,128)S(1)}, u32[]{:S(2)}, u32[]{:S(2)}) collective-permute-start(s32[256,8]{0,1:T(8,128)S(1)} %multiply_add_fusion), channel_id=1, source_target_pairs={{0,8},{1,9},{2,10},{3,11},{4,12},{5,13},{6,14},{7,15},{8,0},{9,1},... | collective-permute-start | bytes 24584 | tf_op jit(solution)/shard_map/ppermute | solution.py:286
  5.4 1.6 %collective-permute-start = (s32[256,8]{0,1:T(8,128)S(1)}, s32[256,8]{0,1:T(8,128)S(1)}, u32[]{:S(2)}, u32[]{:S(2)}) collective-permute-start(s32[256,8]{0,1:T(8,128)S(1)} %multiply_add_fusion), channel_id=1, source_target_pairs={{0,1},{1,0},{2,3},{3,2},{4,5},{5,4},{6,7},{7,6},{8,9},{9,8},{10,11... | collective-permute-start | bytes 24584 | tf_op jit(solution)/shard_map/ppermute | solution.py:283
  7.0 1.2 %collective-permute-start.2 = (s32[256,8]{0,1:T(8,128)S(1)}, s32[256,8]{0,1:T(8,128)S(1)}, u32[]{:S(2)}, u32[]{:S(2)}) collective-permute-start(s32[256,8]{0,1:T(8,128)S(1)} %collective-permute-done.1), channel_id=1, source_target_pairs={{0,1},{1,0},{2,3},{3,2},{4,5},{5,4},{6,7},{7,6},{8,9},{9,8},{10,11... | collective-permute-start | bytes 24584 | tf_op jit(solution)/shard_map/ppermute | solution.py:283
  9.3 6.5 %collective-permute-start.3 = (s32[4,192]{1,0:T(4,128)S(1)}, s32[4,192]{1,0:T(4,128)S(1)}, u32[]{:S(2)}, u32[]{:S(2)}) collective-permute-start(s32[4,192]{1,0:T(4,128)S(1)} %get-tuple-element.35), channel_id=1, source_target_pairs={{0,6},{1,7},{2,4},{3,5},{4,2},{5,3},{6,0},{7,1},{8,14},{9,15},{10,... | collective-permute-start | bytes 9224 | tf_op jit(solution)/shard_map/ppermute | solution.py:283
  12.2 3.6 %collective-permute-start.4 = (s32[4,192]{1,0:T(4,128)S(1)}, s32[4,192]{1,0:T(4,128)S(1)}, u32[]{:S(2)}, u32[]{:S(2)}) collective-permute-start(s32[4,192]{1,0:T(4,128)S(1)} %get-tuple-element.36), channel_id=1, source_target_pairs={{0,4},{1,5},{2,6},{3,7},{4,0},{5,1},{6,2},{7,3},{8,12},{9,13},{10,... | collective-permute-start | bytes 9224 | tf_op jit(solution)/shard_map/ppermute | solution.py:283
  12.7 3.6 %collective-permute-start.5 = (s32[4,192]{1,0:T(4,128)S(1)}, s32[4,192]{1,0:T(4,128)S(1)}, u32[]{:S(2)}, u32[]{:S(2)}) collective-permute-start(s32[4,192]{1,0:T(4,128)S(1)} %get-tuple-element.37), channel_id=1, source_target_pairs={{0,2},{1,3},{2,0},{3,1},{4,6},{5,7},{6,4},{7,5},{8,10},{9,11},{10,... | collective-permute-start | bytes 9224 | tf_op jit(solution)/shard_map/ppermute | solution.py:283
  12.9 2.2 %copy-start.2 = (bf16[8192,256]{1,0:T(8,128)(2,1)S(1)}, bf16[8192,256]{1,0:T(8,128)(2,1)}, u32[]{:S(2)}) copy-start(bf16[8192,256]{1,0:T(8,128)(2,1)} %table_ref.1) | copy-start | bytes 12582916
  18.2 2.6 %collective-permute-start.7 = (bf16[4,192,256]{2,1,0:T(8,128)(2,1)S(1)}, bf16[4,192,256]{2,1,0:T(8,128)(2,1)S(1)}, u32[]{:S(2)}, u32[]{:S(2)}) collective-permute-start(bf16[4,192,256]{2,1,0:T(8,128)(2,1)S(1)} %get-tuple-element.44), channel_id=1, source_target_pairs={{0,1},{1,0},{2,3},{3,2},{4,5},{5,4},{6,7},{7,6},{8,9},{9,8},{10,11... | collective-permute-start | bytes 1179656 | tf_op jit(solution)/shard_map/ppermute | solution.py:283
  18.3 6.1 %collective-permute-start.6 = (bf16[4,192,256]{2,1,0:T(8,128)(2,1)S(1)}, bf16[4,192,256]{2,1,0:T(8,128)(2,1)S(1)}, u32[]{:S(2)}, u32[]{:S(2)}) collective-permute-start(bf16[4,192,256]{2,1,0:T(8,128)(2,1)S(1)} %get-tuple-element.40), channel_id=1, source_target_pairs={{0,1},{1,0},{2,3},{3,2},{4,5},{5,4},{6,7},{7,6},{8,9},{9,8},{10,11... | collective-permute-start | bytes 1179656 | tf_op jit(solution)/shard_map/ppermute | solution.py:283
  20.8 28.4 %copy-start = (bf16[256,4096]{1,0:T(8,128)(2,1)S(1)}, bf16[256,4096]{1,0:T(8,128)(2,1)}, u32[]{:S(2)}) copy-start(bf16[256,4096]{1,0:T(8,128)(2,1)} %refs_3_.1) | copy-start | bytes 6291460
  20.8 28.4 %copy-start.1 = (bf16[4096,256]{1,0:T(8,128)(2,1)S(1)}, bf16[4096,256]{1,0:T(8,128)(2,1)}, u32[]{:S(2)}) copy-start(bf16[4096,256]{1,0:T(8,128)(2,1)} %refs_4_.1) | copy-start | bytes 6291460
  20.9 8.8 %collective-permute-start.8 = (bf16[2,192,256]{2,1,0:T(8,128)(2,1)S(1)}, bf16[2,192,256]{2,1,0:T(8,128)(2,1)S(1)}, u32[]{:S(2)}, u32[]{:S(2)}) collective-permute-start(bf16[2,192,256]{2,1,0:T(8,128)(2,1)S(1)} %get-tuple-element.45), channel_id=1, source_target_pairs={{0,6},{1,7},{2,4},{3,5},{4,2},{5,3},{6,0},{7,1},{8,14},{9,15},{10,... | collective-permute-start | bytes 589832 | tf_op jit(solution)/shard_map/ppermute | solution.py:283
  23.3 10.4 %collective-permute-start.9 = (bf16[2,192,256]{2,1,0:T(8,128)(2,1)S(1)}, bf16[2,192,256]{2,1,0:T(8,128)(2,1)S(1)}, u32[]{:S(2)}, u32[]{:S(2)}) collective-permute-start(bf16[2,192,256]{2,1,0:T(8,128)(2,1)S(1)} %get-tuple-element.46), channel_id=1, source_target_pairs={{0,4},{1,5},{2,6},{3,7},{4,0},{5,1},{6,2},{7,3},{8,12},{9,13},{10,... | collective-permute-start | bytes 589832 | tf_op jit(solution)/shard_map/ppermute | solution.py:283
  23.7 10.2 %collective-permute-start.10 = (bf16[2,192,256]{2,1,0:T(8,128)(2,1)S(1)}, bf16[2,192,256]{2,1,0:T(8,128)(2,1)S(1)}, u32[]{:S(2)}, u32[]{:S(2)}) collective-permute-start(bf16[2,192,256]{2,1,0:T(8,128)(2,1)S(1)} %get-tuple-element.47), channel_id=1, source_target_pairs={{0,2},{1,3},{2,0},{3,1},{4,6},{5,7},{6,4},{7,5},{8,10},{9,11},{10,... | collective-permute-start | bytes 589832 | tf_op jit(solution)/shard_map/ppermute | solution.py:283
  24.5 13.6 %collective-permute-start.12 = (bf16[2,192,256]{2,1,0:T(8,128)(2,1)S(1)}, bf16[2,192,256]{2,1,0:T(8,128)(2,1)S(1)}, u32[]{:S(2)}, u32[]{:S(2)}) collective-permute-start(bf16[2,192,256]{2,1,0:T(8,128)(2,1)S(1)} %get-tuple-element.49), channel_id=1, source_target_pairs={{0,6},{1,7},{2,4},{3,5},{4,2},{5,3},{6,0},{7,1},{8,14},{9,15},{10,... | collective-permute-start | bytes 589832 | tf_op jit(solution)/shard_map/ppermute | solution.py:283
  26.9 19.9 %collective-permute-start.13 = (bf16[2,192,256]{2,1,0:T(8,128)(2,1)S(1)}, bf16[2,192,256]{2,1,0:T(8,128)(2,1)S(1)}, u32[]{:S(2)}, u32[]{:S(2)}) collective-permute-start(bf16[2,192,256]{2,1,0:T(8,128)(2,1)S(1)} %get-tuple-element.50), channel_id=1, source_target_pairs={{0,4},{1,5},{2,6},{3,7},{4,0},{5,1},{6,2},{7,3},{8,12},{9,13},{10,... | collective-permute-start | bytes 589832 | tf_op jit(solution)/shard_map/ppermute | solution.py:283
  29.6 17.2 %collective-permute-start.14 = (bf16[2,192,256]{2,1,0:T(8,128)(2,1)S(1)}, bf16[2,192,256]{2,1,0:T(8,128)(2,1)S(1)}, u32[]{:S(2)}, u32[]{:S(2)}) collective-permute-start(bf16[2,192,256]{2,1,0:T(8,128)(2,1)S(1)} %get-tuple-element.41), channel_id=1, source_target_pairs={{0,2},{1,3},{2,0},{3,1},{4,6},{5,7},{6,4},{7,5},{8,10},{9,11},{10,... | collective-permute-start | bytes 589832 | tf_op jit(solution)/shard_map/ppermute | solution.py:283
  34.6 12.2 %collective-permute-start.11 = (bf16[256,256]{1,0:T(8,128)(2,1)S(1)}, bf16[256,256]{1,0:T(8,128)(2,1)S(1)}, u32[]{:S(2)}, u32[]{:S(2)}) collective-permute-start(bf16[256,256]{1,0:T(8,128)(2,1)S(1)} %get-tuple-element.48), channel_id=1, source_target_pairs={{0,8},{1,9},{2,10},{3,11},{4,12},{5,13},{6,14},{7,15},{8,0},{9,1},... | collective-permute-start | bytes 393224 | tf_op jit(solution)/shard_map/ppermute | solution.py:286
  37.3 11.9 %collective-permute-start.15 = (bf16[256,256]{1,0:T(8,128)(2,1)S(1)}, bf16[256,256]{1,0:T(8,128)(2,1)S(1)}, u32[]{:S(2)}, u32[]{:S(2)}) collective-permute-start(bf16[256,256]{1,0:T(8,128)(2,1)S(1)} %get-tuple-element.52), channel_id=1, source_target_pairs={{0,8},{1,9},{2,10},{3,11},{4,12},{5,13},{6,14},{7,15},{8,0},{9,1},... | collective-permute-start | bytes 393224 | tf_op jit(solution)/shard_map/ppermute | solution.py:286
  47.6 5.1 %collective-permute-start.16 = (bf16[256,256]{1,0:T(8,128)(2,1)S(1)}, bf16[256,256]{1,0:T(8,128)(2,1)S(1)}, u32[]{:S(2)}, u32[]{:S(2)}) collective-permute-start(bf16[256,256]{1,0:T(8,128)(2,1)S(1)} %get-tuple-element.54.refs_1_.refs_2_), channel_id=1, source_target_pairs={{0,16},{16,0},{1,17},{17,1},{2,18},{18,2},{3,19},{19,3},{4,20},{20... | collective-permute-start | bytes 393224 | tf_op jit(solution)/shard_map/ppermute | solution.py:253
  51.2 5.0 %collective-permute-start.17 = (bf16[256,256]{1,0:T(8,128)(2,1)S(1)}, bf16[256,256]{1,0:T(8,128)(2,1)S(1)}, u32[]{:S(2)}, u32[]{:S(2)}) collective-permute-start(bf16[256,256]{1,0:T(8,128)(2,1)S(1)} %get-tuple-element.53.refs_0_), channel_id=1, source_target_pairs={{0,16},{16,0},{1,17},{17,1},{2,18},{18,2},{3,19},{19,3},{4,20},{20... | collective-permute-start | bytes 393224 | tf_op jit(solution)/shard_map/ppermute | solution.py:253

commit v3 on v2

--- a/solution.py
+++ b/solution.py
@@ -136,10 +136,10 @@
         out_ref[1] = swapped_ref[j]
 
 
-def bag_sums(bag_ref, rows, bags):
+def bag_sums(bag_ref, rows, bags, first):
     total = None
     for at, values in enumerate(rows):
-        chosen = bag_ref[at : at + 1, :] == iota((bags, bag_ref.shape[1]), 0)
+        chosen = bag_ref[at : at + 1, :] == first + iota((bags, bag_ref.shape[1]), 0)
         part = dot(jnp.where(chosen, 1.0, 0.0).astype(jnp.bfloat16), values)
         total = part if total is None else total + part
     return total
@@ -154,20 +154,19 @@
     ]
 
 
-def far_kernel(order, bag_ref, same_ref, swapped_ref, *refs):
-    messages, (query_ref, item_ref) = refs[:-2], refs[-2:]
-    pairs = query_ref.shape[0]
-    total = bag_sums(bag_ref, lists_of(order, same_ref, swapped_ref, messages), 2 * pairs)
-    query_ref[...] = total[:pairs].astype(jnp.bfloat16)
-    item_ref[...] = total[pairs:].astype(jnp.bfloat16)
+def sum_kernel(order, kind, bag_ref, same_ref, swapped_ref, *refs):
+    out_ref = refs[-1]
+    pairs = out_ref.shape[0]
+    rows = lists_of(order, same_ref, swapped_ref, refs[:-1])
+    out_ref[...] = bag_sums(bag_ref, rows, pairs, kind * pairs).astype(out_ref.dtype)
 
 
 def item_kernel(order, bag_ref, far_ref, same_ref, swapped_ref, *refs):
-    messages, (query_ref, unit_ref, scale_ref, bf_ref) = refs[:-4], refs[-4:]
-    pairs = query_ref.shape[0]
-    total = bag_sums(bag_ref, lists_of(order, same_ref, swapped_ref, messages), 2 * pairs)
-    query_ref[...] = total[:pairs]
-    unit, scale = unit_rows(total[pairs:] + far_ref[...].astype(jnp.float32))
+    messages, (unit_ref, scale_ref, bf_ref) = refs[:-3], refs[-3:]
+    pairs = bf_ref.shape[0]
+    rows = lists_of(order, same_ref, swapped_ref, messages)
+    total = bag_sums(bag_ref, rows, pairs, pairs) + far_ref[...].astype(jnp.float32)
+    unit, scale = unit_rows(total)
     unit_ref[...] = unit
     scale_ref[...] = scale
     bf_ref[...] = unit.astype(jnp.bfloat16)
@@ -177,13 +176,15 @@
     near_ref, far_ref, first_ref, second_ref, unit_ref, scale_ref, bf_ref, slope_ref
 ):
     query_in = (near_ref[...] + far_ref[...].astype(jnp.float32)).astype(jnp.bfloat16)
+    query_in = (0.5 * query_in.astype(jnp.float32)).astype(jnp.bfloat16)
     step = 1024
     total = None
     for at in range(0, first_ref.shape[1], step):
         pre = dot(query_in, first_ref[:, at : at + step])
-        sigma = 0.5 + 0.5 * jnp.tanh(0.5 * pre)
-        hidden = pre * sigma
-        slope_ref[:, at : at + step] = sigma * (1.0 + pre * (1.0 - sigma))
+        turn = jnp.tanh(pre)
+        hidden = pre + pre * turn
+        turn = 0.5 * turn
+        slope_ref[:, at : at + step] = (0.5 + turn) + hidden * (0.5 - turn)
         part = dot(hidden.astype(jnp.bfloat16), second_ref[at : at + step, :])
         total = part if total is None else total + part
     unit, scale = unit_rows(total)
@@ -338,18 +339,22 @@
     far_rows, _ = answered(far_same, far_other)
     near_rows, near_messages = answered(near_same, near_other)
     far_bags, _ = lax.optimization_barrier((far_bags, near_messages[-1]))
-    far_query, far_item = pl.pallas_call(
-        functools.partial(far_kernel, order),
-        out_shape=[struct((pairs, width), bf)] * 2,
-        compiler_params=params(8),
-        name="far_bags",
-    )(far_bags, *far_rows)
+
+    def sums(kind, bags, rows, dtype):
+        return pl.pallas_call(
+            functools.partial(sum_kernel, order, kind),
+            out_shape=struct((pairs, width), dtype),
+            compiler_params=params(8),
+            name="item_sums" if kind else "query_sums",
+        )(bags, *rows)
+
+    far_item = sums(1, far_bags, far_rows, bf)
+    far_bags, _ = lax.optimization_barrier((far_bags, far_item))
+    far_query = to_mirror(sums(0, far_bags, far_rows, bf))
     far_item = to_mirror(far_item)
-    far_query = to_mirror(far_query)
-    near_query, item_unit, item_scale, item_bf = pl.pallas_call(
+    item_unit, item_scale, item_bf = pl.pallas_call(
         functools.partial(item_kernel, order),
         out_shape=[
-            struct((pairs, width), f32),
             struct((pairs, width), f32),
             struct((pairs, 1), f32),
             struct((pairs, width), bf),
@@ -357,6 +362,8 @@
         compiler_params=params(8),
         name="items",
     )(near_bags, far_item, *near_rows)
+    near_bags, _ = lax.optimization_barrier((near_bags, item_bf))
+    near_query = sums(0, near_bags, near_rows, f32)
     items = [item_bf] + [rotated(item_bf, "blk", by) for by in range(1, blocks)]
     query_unit, query_scale, query_bf, slope = pl.pallas_call(
         tower_kernel,

time: 57.9 us -> 58 us (level)
  starting transfers between devices: 22 us -> 21.2 us
  waiting for transfers between devices: 18.2 us -> 19 us
    ppermute x2, starting transfers between devices: 3.12 us -> 2.16 us  [rotated(): lax.ppermute(shard, axis, [(i, (i + by) % count) for i in range(count)])]
    ppermute x2, waiting for transfers between devices: 0.44 us -> 1.4 us  [rotated(): lax.ppermute(shard, axis, [(i, (i + by) % count) for i in range(count)])]
    pallas_call x1 -> x3, Pallas kernels: 0.7 us -> 1.28 us  [sums(): pl.pallas_call(functools.partial(sum_kernel, order, kind), out_shape=stru...]
  transfers between devices with their start and end apart: 18 -> 18, of which waited for: 10 -> 11; matrix products, arithmetic and copies ran while one was open for 0% -> 0% of each run, Pallas kernels for 16% -> 16%
where the time goes in v3:
time: 58 us; the launch traced here: 57.7 us
  starting transfers between devices  21.2 us (37%)
  waiting for transfers between devices  19 us (33%)
  Pallas kernels  13.8 us (24%)
  local copies, waits for them, and re-layouts  2.2 us (4%)
  between operations  0.79 us (1%)
  other arithmetic  0.72 us (1%)
    ppermute x13, waiting for transfers between devices, to_chip(): return lax.ppermute(values, 'table', route)  16 us
    ppermute x13, starting transfers between devices, to_chip(): return lax.ppermute(values, 'table', route)  11.9 us
    ppermute x3, starting transfers between devices, to_mirror(): lax.ppermute(values, 'table', [(t, (t + half) % shards) for t in range(sh...  7.09 us
    pallas_call x2, Pallas kernels, gather(): pl.pallas_call(functools.partial(gather_kernel, chips, askers), in_specs=...  3.91 us
    pallas_call x1, Pallas kernels, local(): pl.pallas_call(functools.partial(query_grad_kernel, blocks), out_shape=[s...  3.03 us
    unnamed x6, local copies, waits for them, and re-layouts  2.2 us
    ppermute x2, starting transfers between devices, rotated(): lax.ppermute(shard, axis, [(i, (i + by) % count) for i in range(count)])  2.16 us
    pallas_call x1, Pallas kernels, local(): pl.pallas_call(tower_kernel, out_shape=[struct((pairs, width), f32), stru...  1.79 us
  transfers between devices with their start and end apart: 18, of which 11 were waited for; matrix products, arithmetic and copies ran while one was open for 0% of the time, Pallas kernels for 16%

profile of v3, /device:TPU:0, one launch (start us, length us, event | category | flops | bytes accessed | tf_op | source)
XLA Modules:
  0.0 57.7 jit_solution(17138676864171554799)
XLA Ops:
  0.6 0.7 %multiply_add_fusion = s32[256,8]{0,1:T(8,128)S(1)} fusion(s32[256,8]{0,1:T(8,128)} %param.9, s32[256,8]{0,1:T(8,128)} %param.8), kind=kLoop, calls=%fused_computation | loop fusion | flops 4096 | bytes 24576 | tf_op jit(solution)/shard_map/add | solution.py:289
  1.3 4.0 %collective-permute-start.1 = (s32[256,8]{0,1:T(8,128)S(1)}, s32[256,8]{0,1:T(8,128)S(1)}, u32[]{:S(2)}, u32[]{:S(2)}) collective-permute-start(s32[256,8]{0,1:T(8,128)S(1)} %multiply_add_fusion), channel_id=1, source_target_pairs={{0,8},{1,9},{2,10},{3,11},{4,12},{5,13},{6,14},{7,15},{8,0},{9,1},... | collective-permute-start | bytes 24584 | tf_op jit(solution)/shard_map/ppermute | solution.py:287
  5.4 1.6 %collective-permute-done.1 = s32[256,8]{0,1:T(8,128)S(1)} collective-permute-done((s32[256,8]{0,1:T(8,128)S(1)}, s32[256,8]{0,1:T(8,128)S(1)}, u32[]{:S(2)}, u32[]{:S(2)}) %collective-permute-start.1) | collective-permute-done | bytes 8224 | tf_op jit(solution)/shard_map/ppermute | solution.py:287
  7.0 1.2 %collective-permute-done.2 = s32[256,8]{0,1:T(8,128)S(1)} collective-permute-done((s32[256,8]{0,1:T(8,128)S(1)}, s32[256,8]{0,1:T(8,128)S(1)}, u32[]{:S(2)}, u32[]{:S(2)}) %collective-permute-start.2) | collective-permute-done | bytes 8224 | tf_op jit(solution)/shard_map/ppermute | solution.py:284
  8.2 1.1 %route.1 = (s32[8,192]{1,0:T(8,128)S(1)}, s32[8,192]{1,0:T(8,128)S(1)}, s32[4,192]{1,0:T(4,128)S(1)}, s32[4,192]{1,0:T(4,128)S(1)}, s32[4,192]{1,0:T(4,128)S(1)}, /*index=5*/s32[4,192]{1,0:T(4,128)S(1)}) custom-call(s32[8,256]{1,0:T(8,128)S(1)} %bitcast.5, s32[8,256]{1,0:T(8,128)S(1)} %bitcast.7, s32[8,256]{1,0:T(8,128)S(1)} %bitcast.6, s32[8,256]{1,0:T(8,128)S(1)} %bitcast.8), custom_call_target="tpu_custom_call" | custom-call | tf_op jit(solution)/shard_map/route/pallas_call | solution.py:298
  9.3 2.9 %collective-permute-start.3 = (s32[4,192]{1,0:T(4,128)S(1)}, s32[4,192]{1,0:T(4,128)S(1)}, u32[]{:S(2)}, u32[]{:S(2)}) collective-permute-start(s32[4,192]{1,0:T(4,128)S(1)} %get-tuple-element.34), channel_id=1, source_target_pairs={{0,6},{1,7},{2,4},{3,5},{4,2},{5,3},{6,0},{7,1},{8,14},{9,15},{10,... | collective-permute-start | bytes 9224 | tf_op jit(solution)/shard_map/ppermute | solution.py:284
  12.2 0.4 collective-permute-start.4
  12.9 2.2 %copy-done.2 = bf16[8192,256]{1,0:T(8,128)(2,1)S(1)} copy-done((bf16[8192,256]{1,0:T(8,128)(2,1)S(1)}, bf16[8192,256]{1,0:T(8,128)(2,1)}, u32[]{:S(2)}) %copy-start.2) | copy-done | bytes 4194328
  15.1 0.7 %widen.1.refs_4_ = f32[16384,128]{1,0:T(8,128)S(1)} custom-call(bf16[8192,256]{1,0:T(8,128)(2,1)S(1)} %copy-done.2), custom_call_target="tpu_custom_call" | custom-call | tf_op jit(solution)/shard_map/widen/pallas_call | solution.py:292
  15.8 0.4 collective-permute-done.5.refs_2_
  16.3 2.0 %gather.3 = (bf16[4,192,256]{2,1,0:T(8,128)(2,1)S(1)}, bf16[4,192,256]{2,1,0:T(8,128)(2,1)S(1)}) custom-call(s32[4,192]{1,0:T(4,128)S(1)} %collective-permute-done.3.refs_0_, s32[4,192]{1,0:T(4,128)S(1)} %collective-permute-done.4.refs_1_, s32[4,192]{1,0:T(4,128)S(1)} %collective-permute-done.5.refs_2_, s32[4,192]{1,0:T(4,128)S(1)} %get-tuple-element.37.refs_3_, ...), custom_call_target="tpu_custom_call" | custom-call | tf_op jit(solution)/shard_map/gather/pallas_call | solution.py:308
  18.3 0.5 collective-permute-start.6
  18.8 2.0 %gather.2 = (bf16[4,192,256]{2,1,0:T(8,128)(2,1)S(1)}, bf16[4,192,256]{2,1,0:T(8,128)(2,1)S(1)}) custom-call(s32[4,192]{1,0:T(4,128)S(1)} %collective-permute-done.3.refs_0_, s32[4,192]{1,0:T(4,128)S(1)} %collective-permute-done.4.refs_1_, s32[4,192]{1,0:T(4,128)S(1)} %collective-permute-done.5.refs_2_, s32[4,192]{1,0:T(4,128)S(1)} %get-tuple-element.37.refs_3_, ...), custom_call_target="tpu_custom_call" | custom-call | tf_op jit(solution)/shard_map/gather/pallas_call | solution.py:308
  20.9 2.4 %collective-permute-start.8 = (bf16[2,192,256]{2,1,0:T(8,128)(2,1)S(1)}, bf16[2,192,256]{2,1,0:T(8,128)(2,1)S(1)}, u32[]{:S(2)}, u32[]{:S(2)}) collective-permute-start(bf16[2,192,256]{2,1,0:T(8,128)(2,1)S(1)} %get-tuple-element.44), channel_id=1, source_target_pairs={{0,6},{1,7},{2,4},{3,5},{4,2},{5,3},{6,0},{7,1},{8,14},{9,15},{10,... | collective-permute-start | bytes 589832 | tf_op jit(solution)/shard_map/ppermute | solution.py:284
  23.3 0.5 collective-permute-start.9
  23.7 0.7 %collective-permute-start.10 = (bf16[2,192,256]{2,1,0:T(8,128)(2,1)S(1)}, bf16[2,192,256]{2,1,0:T(8,128)(2,1)S(1)}, u32[]{:S(2)}, u32[]{:S(2)}) collective-permute-start(bf16[2,192,256]{2,1,0:T(8,128)(2,1)S(1)} %get-tuple-element.46), channel_id=1, source_target_pairs={{0,2},{1,3},{2,0},{3,1},{4,6},{5,7},{6,4},{7,5},{8,10},{9,11},{10,... | collective-permute-start | bytes 589832 | tf_op jit(solution)/shard_map/ppermute | solution.py:284
  24.5 2.4 %collective-permute-start.12 = (bf16[2,192,256]{2,1,0:T(8,128)(2,1)S(1)}, bf16[2,192,256]{2,1,0:T(8,128)(2,1)S(1)}, u32[]{:S(2)}, u32[]{:S(2)}) collective-permute-start(bf16[2,192,256]{2,1,0:T(8,128)(2,1)S(1)} %get-tuple-element.47), channel_id=1, source_target_pairs={{0,6},{1,7},{2,4},{3,5},{4,2},{5,3},{6,0},{7,1},{8,14},{9,15},{10,... | collective-permute-start | bytes 589832 | tf_op jit(solution)/shard_map/ppermute | solution.py:284
  26.9 0.5 collective-permute-start.13
  27.3 2.3 %collective-permute-done.8.refs_0_ = bf16[2,192,256]{2,1,0:T(8,128)(2,1)S(1)} collective-permute-done((bf16[2,192,256]{2,1,0:T(8,128)(2,1)S(1)}, bf16[2,192,256]{2,1,0:T(8,128)(2,1)S(1)}, u32[]{:S(2)}, u32[]{:S(2)}) %collective-permute-start.8) | collective-permute-done | bytes 196640 | tf_op jit(solution)/shard_map/ppermute | solution.py:284
  29.6 1.3 %collective-permute-start.14 = (bf16[2,192,256]{2,1,0:T(8,128)(2,1)S(1)}, bf16[2,192,256]{2,1,0:T(8,128)(2,1)S(1)}, u32[]{:S(2)}, u32[]{:S(2)}) collective-permute-start(bf16[2,192,256]{2,1,0:T(8,128)(2,1)S(1)} %get-tuple-element.40), channel_id=1, source_target_pairs={{0,2},{1,3},{2,0},{3,1},{4,6},{5,7},{6,4},{7,5},{8,10},{9,11},{10,... | collective-permute-start | bytes 589832 | tf_op jit(solution)/shard_map/ppermute | solution.py:284
  31.0 2.7 %collective-permute-done.9.refs_1_ = bf16[2,192,256]{2,1,0:T(8,128)(2,1)S(1)} collective-permute-done((bf16[2,192,256]{2,1,0:T(8,128)(2,1)S(1)}, bf16[2,192,256]{2,1,0:T(8,128)(2,1)S(1)}, u32[]{:S(2)}, u32[]{:S(2)}) %collective-permute-start.9) | collective-permute-done | bytes 196640 | tf_op jit(solution)/shard_map/ppermute | solution.py:284
  34.3 2.6 %collective-permute-start.11 = (bf16[256,256]{1,0:T(8,128)(2,1)S(1)}, bf16[256,256]{1,0:T(8,128)(2,1)S(1)}, u32[]{:S(2)}, u32[]{:S(2)}) collective-permute-start(bf16[256,256]{1,0:T(8,128)(2,1)S(1)} %item_sums.1), channel_id=1, source_target_pairs={{0,8},{1,9},{2,10},{3,11},{4,12},{5,13},{6,14},{7,15},{8,0},{9,1},... | collective-permute-start | bytes 393224 | tf_op jit(solution)/shard_map/ppermute | solution.py:287
  37.0 0.4 query_sums.3
  38.1 8.8 %collective-permute-done.13.refs_1_ = bf16[2,192,256]{2,1,0:T(8,128)(2,1)S(1)} collective-permute-done((bf16[2,192,256]{2,1,0:T(8,128)(2,1)S(1)}, bf16[2,192,256]{2,1,0:T(8,128)(2,1)S(1)}, u32[]{:S(2)}, u32[]{:S(2)}) %collective-permute-start.13) | collective-permute-done | bytes 196640 | tf_op jit(solution)/shard_map/ppermute | solution.py:284
  46.9 0.5 items.1
  47.5 1.6 %collective-permute-start.16 = (bf16[256,256]{1,0:T(8,128)(2,1)S(1)}, bf16[256,256]{1,0:T(8,128)(2,1)S(1)}, u32[]{:S(2)}, u32[]{:S(2)}) collective-permute-start(bf16[256,256]{1,0:T(8,128)(2,1)S(1)} %get-tuple-element.49.refs_1_.refs_2_), channel_id=1, source_target_pairs={{0,16},{16,0},{1,17},{17,1},{2,18},{18,2},{3,19},{19,3},{4,20},{20... | collective-permute-start | bytes 393224 | tf_op jit(solution)/shard_map/ppermute | solution.py:254
  49.5 1.8 %tower.1 = (f32[256,256]{1,0:T(8,128)S(1)}, f32[256,1]{1,0:T(8,128)S(1)}, bf16[256,256]{1,0:T(8,128)(2,1)S(1)}, f32[256,4096]{1,0:T(8,128)S(1)}) custom-call(f32[256,256]{1,0:T(8,128)S(1)} %query_sums.2.near_ref, bf16[256,256]{1,0:T(8,128)(2,1)S(1)} %collective-permute-done.15.far_ref, bf16[256,4096]{1,0:T(8,128)(2,1)S(1)} %copy-done, ...), custom_call_target="tpu_custom_call" | custom-call | tf_op jit(solution)/shard_map/tower/pallas_call | solution.py:368
  51.3 0.6 %collective-permute-start.17 = (bf16[256,256]{1,0:T(8,128)(2,1)S(1)}, bf16[256,256]{1,0:T(8,128)(2,1)S(1)}, u32[]{:S(2)}, u32[]{:S(2)}) collective-permute-start(bf16[256,256]{1,0:T(8,128)(2,1)S(1)} %get-tuple-element.52.refs_0_), channel_id=1, source_target_pairs={{0,16},{16,0},{1,17},{17,1},{2,18},{18,2},{3,19},{19,3},{4,20},{20... | collective-permute-start | bytes 393224 | tf_op jit(solution)/shard_map/ppermute | solution.py:254
  51.9 0.6 %collective-permute-done.16.refs_2_.refs_3_ = bf16[256,256]{1,0:T(8,128)(2,1)S(1)} collective-permute-done((bf16[256,256]{1,0:T(8,128)(2,1)S(1)}, bf16[256,256]{1,0:T(8,128)(2,1)S(1)}, u32[]{:S(2)}, u32[]{:S(2)}) %collective-permute-start.16) | collective-permute-done | bytes 131104 | tf_op jit(solution)/shard_map/ppermute | solution.py:254
  52.5 3.0 %query_grads.1 = (f32[1,256]{1,0:T(1,128)}, f32[256,256]{1,0:T(8,128)}, f32[256,256]{1,0:T(8,128)S(1)}) custom-call(bf16[256,256]{1,0:T(8,128)(2,1)S(1)} %get-tuple-element.52.refs_0_, bf16[256,256]{1,0:T(8,128)(2,1)S(1)} %get-tuple-element.49.refs_1_.refs_2_, bf16[256,256]{1,0:T(8,128)(2,1)S(1)} %collective-permute-done.16.refs_2_.refs_3_, ...), custom_call_target="tpu_custom_call" | custom-call | tf_op jit(solution)/shard_map/query_grads/pallas_call | solution.py:380
  55.5 0.8 %collective-permute-done.17.refs_1_ = bf16[256,256]{1,0:T(8,128)(2,1)S(1)} collective-permute-done((bf16[256,256]{1,0:T(8,128)(2,1)S(1)}, bf16[256,256]{1,0:T(8,128)(2,1)S(1)}, u32[]{:S(2)}, u32[]{:S(2)}) %collective-permute-start.17) | collective-permute-done | bytes 131104 | tf_op jit(solution)/shard_map/ppermute | solution.py:254
  56.3 1.4 %item_grads.1 = f32[256,256]{1,0:T(8,128)} custom-call(bf16[256,256]{1,0:T(8,128)(2,1)S(1)} %get-tuple-element.52.refs_0_, bf16[256,256]{1,0:T(8,128)(2,1)S(1)} %collective-permute-done.17.refs_1_, bf16[256,256]{1,0:T(8,128)(2,1)S(1)} %get-tuple-element.49.refs_1_.refs_2_, bf16[256,256]{1,0:T(8,128)(2,1)S(1)} %collective-permute-done.16.refs_2_.refs_3_, ...), custom_call_target="tpu_custom_call" | custom-call | tf_op jit(solution)/shard_map/item_grads/pallas_call | solution.py:390
  (24 shorter events, 2.1 us)
Async XLA Ops:
  1.3 5.7 %collective-permute-start.1 = (s32[256,8]{0,1:T(8,128)S(1)}, s32[256,8]{0,1:T(8,128)S(1)}, u32[]{:S(2)}, u32[]{:S(2)}) collective-permute-start(s32[256,8]{0,1:T(8,128)S(1)} %multiply_add_fusion), channel_id=1, source_target_pairs={{0,8},{1,9},{2,10},{3,11},{4,12},{5,13},{6,14},{7,15},{8,0},{9,1},... | collective-permute-start | bytes 24584 | tf_op jit(solution)/shard_map/ppermute | solution.py:287
  5.4 1.6 %collective-permute-start = (s32[256,8]{0,1:T(8,128)S(1)}, s32[256,8]{0,1:T(8,128)S(1)}, u32[]{:S(2)}, u32[]{:S(2)}) collective-permute-start(s32[256,8]{0,1:T(8,128)S(1)} %multiply_add_fusion), channel_id=1, source_target_pairs={{0,1},{1,0},{2,3},{3,2},{4,5},{5,4},{6,7},{7,6},{8,9},{9,8},{10,11... | collective-permute-start | bytes 24584 | tf_op jit(solution)/shard_map/ppermute | solution.py:284
  7.0 1.2 %collective-permute-start.2 = (s32[256,8]{0,1:T(8,128)S(1)}, s32[256,8]{0,1:T(8,128)S(1)}, u32[]{:S(2)}, u32[]{:S(2)}) collective-permute-start(s32[256,8]{0,1:T(8,128)S(1)} %collective-permute-done.1), channel_id=1, source_target_pairs={{0,1},{1,0},{2,3},{3,2},{4,5},{5,4},{6,7},{7,6},{8,9},{9,8},{10,11... | collective-permute-start | bytes 24584 | tf_op jit(solution)/shard_map/ppermute | solution.py:284
  9.3 6.5 %collective-permute-start.3 = (s32[4,192]{1,0:T(4,128)S(1)}, s32[4,192]{1,0:T(4,128)S(1)}, u32[]{:S(2)}, u32[]{:S(2)}) collective-permute-start(s32[4,192]{1,0:T(4,128)S(1)} %get-tuple-element.34), channel_id=1, source_target_pairs={{0,6},{1,7},{2,4},{3,5},{4,2},{5,3},{6,0},{7,1},{8,14},{9,15},{10,... | collective-permute-start | bytes 9224 | tf_op jit(solution)/shard_map/ppermute | solution.py:284
  12.2 3.6 %collective-permute-start.4 = (s32[4,192]{1,0:T(4,128)S(1)}, s32[4,192]{1,0:T(4,128)S(1)}, u32[]{:S(2)}, u32[]{:S(2)}) collective-permute-start(s32[4,192]{1,0:T(4,128)S(1)} %get-tuple-element.35), channel_id=1, source_target_pairs={{0,4},{1,5},{2,6},{3,7},{4,0},{5,1},{6,2},{7,3},{8,12},{9,13},{10,... | collective-permute-start | bytes 9224 | tf_op jit(solution)/shard_map/ppermute | solution.py:284
  12.7 3.6 %collective-permute-start.5 = (s32[4,192]{1,0:T(4,128)S(1)}, s32[4,192]{1,0:T(4,128)S(1)}, u32[]{:S(2)}, u32[]{:S(2)}) collective-permute-start(s32[4,192]{1,0:T(4,128)S(1)} %get-tuple-element.36), channel_id=1, source_target_pairs={{0,2},{1,3},{2,0},{3,1},{4,6},{5,7},{6,4},{7,5},{8,10},{9,11},{10,... | collective-permute-start | bytes 9224 | tf_op jit(solution)/shard_map/ppermute | solution.py:284
  12.9 2.2 %copy-start.2 = (bf16[8192,256]{1,0:T(8,128)(2,1)S(1)}, bf16[8192,256]{1,0:T(8,128)(2,1)}, u32[]{:S(2)}) copy-start(bf16[8192,256]{1,0:T(8,128)(2,1)} %table_ref.1) | copy-start | bytes 12582916
  18.2 2.6 %collective-permute-start.7 = (bf16[4,192,256]{2,1,0:T(8,128)(2,1)S(1)}, bf16[4,192,256]{2,1,0:T(8,128)(2,1)S(1)}, u32[]{:S(2)}, u32[]{:S(2)}) collective-permute-start(bf16[4,192,256]{2,1,0:T(8,128)(2,1)S(1)} %get-tuple-element.43), channel_id=1, source_target_pairs={{0,1},{1,0},{2,3},{3,2},{4,5},{5,4},{6,7},{7,6},{8,9},{9,8},{10,11... | collective-permute-start | bytes 1179656 | tf_op jit(solution)/shard_map/ppermute | solution.py:284
  18.3 6.1 %collective-permute-start.6 = (bf16[4,192,256]{2,1,0:T(8,128)(2,1)S(1)}, bf16[4,192,256]{2,1,0:T(8,128)(2,1)S(1)}, u32[]{:S(2)}, u32[]{:S(2)}) collective-permute-start(bf16[4,192,256]{2,1,0:T(8,128)(2,1)S(1)} %get-tuple-element.39), channel_id=1, source_target_pairs={{0,1},{1,0},{2,3},{3,2},{4,5},{5,4},{6,7},{7,6},{8,9},{9,8},{10,11... | collective-permute-start | bytes 1179656 | tf_op jit(solution)/shard_map/ppermute | solution.py:284
  20.8 28.7 %copy-start = (bf16[256,4096]{1,0:T(8,128)(2,1)S(1)}, bf16[256,4096]{1,0:T(8,128)(2,1)}, u32[]{:S(2)}) copy-start(bf16[256,4096]{1,0:T(8,128)(2,1)} %refs_3_.1) | copy-start | bytes 6291460
  20.8 28.7 %copy-start.1 = (bf16[4096,256]{1,0:T(8,128)(2,1)S(1)}, bf16[4096,256]{1,0:T(8,128)(2,1)}, u32[]{:S(2)}) copy-start(bf16[4096,256]{1,0:T(8,128)(2,1)} %refs_4_.1) | copy-start | bytes 6291460
  20.9 8.8 %collective-permute-start.8 = (bf16[2,192,256]{2,1,0:T(8,128)(2,1)S(1)}, bf16[2,192,256]{2,1,0:T(8,128)(2,1)S(1)}, u32[]{:S(2)}, u32[]{:S(2)}) collective-permute-start(bf16[2,192,256]{2,1,0:T(8,128)(2,1)S(1)} %get-tuple-element.44), channel_id=1, source_target_pairs={{0,6},{1,7},{2,4},{3,5},{4,2},{5,3},{6,0},{7,1},{8,14},{9,15},{10,... | collective-permute-start | bytes 589832 | tf_op jit(solution)/shard_map/ppermute | solution.py:284
  23.3 10.5 %collective-permute-start.9 = (bf16[2,192,256]{2,1,0:T(8,128)(2,1)S(1)}, bf16[2,192,256]{2,1,0:T(8,128)(2,1)S(1)}, u32[]{:S(2)}, u32[]{:S(2)}) collective-permute-start(bf16[2,192,256]{2,1,0:T(8,128)(2,1)S(1)} %get-tuple-element.45), channel_id=1, source_target_pairs={{0,4},{1,5},{2,6},{3,7},{4,0},{5,1},{6,2},{7,3},{8,12},{9,13},{10,... | collective-permute-start | bytes 589832 | tf_op jit(solution)/shard_map/ppermute | solution.py:284
  23.7 10.2 %collective-permute-start.10 = (bf16[2,192,256]{2,1,0:T(8,128)(2,1)S(1)}, bf16[2,192,256]{2,1,0:T(8,128)(2,1)S(1)}, u32[]{:S(2)}, u32[]{:S(2)}) collective-permute-start(bf16[2,192,256]{2,1,0:T(8,128)(2,1)S(1)} %get-tuple-element.46), channel_id=1, source_target_pairs={{0,2},{1,3},{2,0},{3,1},{4,6},{5,7},{6,4},{7,5},{8,10},{9,11},{10,... | collective-permute-start | bytes 589832 | tf_op jit(solution)/shard_map/ppermute | solution.py:284
  24.5 13.6 %collective-permute-start.12 = (bf16[2,192,256]{2,1,0:T(8,128)(2,1)S(1)}, bf16[2,192,256]{2,1,0:T(8,128)(2,1)S(1)}, u32[]{:S(2)}, u32[]{:S(2)}) collective-permute-start(bf16[2,192,256]{2,1,0:T(8,128)(2,1)S(1)} %get-tuple-element.47), channel_id=1, source_target_pairs={{0,6},{1,7},{2,4},{3,5},{4,2},{5,3},{6,0},{7,1},{8,14},{9,15},{10,... | collective-permute-start | bytes 589832 | tf_op jit(solution)/shard_map/ppermute | solution.py:284
  26.9 20.1 %collective-permute-start.13 = (bf16[2,192,256]{2,1,0:T(8,128)(2,1)S(1)}, bf16[2,192,256]{2,1,0:T(8,128)(2,1)S(1)}, u32[]{:S(2)}, u32[]{:S(2)}) collective-permute-start(bf16[2,192,256]{2,1,0:T(8,128)(2,1)S(1)} %get-tuple-element.48), channel_id=1, source_target_pairs={{0,4},{1,5},{2,6},{3,7},{4,0},{5,1},{6,2},{7,3},{8,12},{9,13},{10,... | collective-permute-start | bytes 589832 | tf_op jit(solution)/shard_map/ppermute | solution.py:284
  29.6 17.3 %collective-permute-start.14 = (bf16[2,192,256]{2,1,0:T(8,128)(2,1)S(1)}, bf16[2,192,256]{2,1,0:T(8,128)(2,1)S(1)}, u32[]{:S(2)}, u32[]{:S(2)}) collective-permute-start(bf16[2,192,256]{2,1,0:T(8,128)(2,1)S(1)} %get-tuple-element.40), channel_id=1, source_target_pairs={{0,2},{1,3},{2,0},{3,1},{4,6},{5,7},{6,4},{7,5},{8,10},{9,11},{10,... | collective-permute-start | bytes 589832 | tf_op jit(solution)/shard_map/ppermute | solution.py:284
  34.3 12.6 %collective-permute-start.11 = (bf16[256,256]{1,0:T(8,128)(2,1)S(1)}, bf16[256,256]{1,0:T(8,128)(2,1)S(1)}, u32[]{:S(2)}, u32[]{:S(2)}) collective-permute-start(bf16[256,256]{1,0:T(8,128)(2,1)S(1)} %item_sums.1), channel_id=1, source_target_pairs={{0,8},{1,9},{2,10},{3,11},{4,12},{5,13},{6,14},{7,15},{8,0},{9,1},... | collective-permute-start | bytes 393224 | tf_op jit(solution)/shard_map/ppermute | solution.py:287
  37.4 12.0 %collective-permute-start.15 = (bf16[256,256]{1,0:T(8,128)(2,1)S(1)}, bf16[256,256]{1,0:T(8,128)(2,1)S(1)}, u32[]{:S(2)}, u32[]{:S(2)}) collective-permute-start(bf16[256,256]{1,0:T(8,128)(2,1)S(1)} %query_sums.3), channel_id=1, source_target_pairs={{0,8},{1,9},{2,10},{3,11},{4,12},{5,13},{6,14},{7,15},{8,0},{9,1},... | collective-permute-start | bytes 393224 | tf_op jit(solution)/shard_map/ppermute | solution.py:287
  47.5 5.0 %collective-permute-start.16 = (bf16[256,256]{1,0:T(8,128)(2,1)S(1)}, bf16[256,256]{1,0:T(8,128)(2,1)S(1)}, u32[]{:S(2)}, u32[]{:S(2)}) collective-permute-start(bf16[256,256]{1,0:T(8,128)(2,1)S(1)} %get-tuple-element.49.refs_1_.refs_2_), channel_id=1, source_target_pairs={{0,16},{16,0},{1,17},{17,1},{2,18},{18,2},{3,19},{19,3},{4,20},{20... | collective-permute-start | bytes 393224 | tf_op jit(solution)/shard_map/ppermute | solution.py:254
  51.3 5.0 %collective-permute-start.17 = (bf16[256,256]{1,0:T(8,128)(2,1)S(1)}, bf16[256,256]{1,0:T(8,128)(2,1)S(1)}, u32[]{:S(2)}, u32[]{:S(2)}) collective-permute-start(bf16[256,256]{1,0:T(8,128)(2,1)S(1)} %get-tuple-element.52.refs_0_), channel_id=1, source_target_pairs={{0,16},{16,0},{1,17},{17,1},{2,18},{18,2},{3,19},{19,3},{4,20},{20... | collective-permute-start | bytes 393224 | tf_op jit(solution)/shard_map/ppermute | solution.py:254

commit v4 on v3

--- a/solution.py
+++ b/solution.py
@@ -45,7 +45,7 @@
 
 
 def route_kernel(relative, rows_dev, *refs):
-    codes, near_ref, far_ref, request_refs = refs[:4], refs[4], refs[5], refs[6:]
+    codes, near_ref, far_ref, request_refs = refs[:4], refs[5], refs[6], refs[7:]
     chips = len(request_refs)
     bags, pairs = codes[0].shape
     capacity = near_ref.shape[1]
@@ -88,6 +88,13 @@
             bag_ref[at : at + 1, :] = (which - 1) * pairs + pair
 
 
+def touch_kernel(table_hbm, out_ref, rows_ref, sem):
+    copy = pltpu.make_async_copy(table_hbm.at[pl.ds(0, rows_ref.shape[0]), :], rows_ref, sem)
+    copy.start()
+    copy.wait()
+    out_ref[...] = rows_ref[...].astype(jnp.float32)
+
+
 def widen_kernel(table_ref, wide_ref):
     width = table_ref.shape[1]
     step = 128
@@ -235,7 +242,13 @@
 
 def item_grad_kernel(blocks, *refs):
     queries, items, refs = refs[:blocks], refs[blocks : 2 * blocks], refs[2 * blocks :]
-    item_sum_ref, unit_ref, scale_ref, grad_ref = refs
+    item_sum_ref, unit_ref, scale_ref, loss_ref, query_grad_ref, grad_ref, *outs, sems = refs
+    copies = [
+        pltpu.make_async_copy(given, out, sems.at[i])
+        for i, (given, out) in enumerate(zip((loss_ref, query_grad_ref), outs))
+    ]
+    for copy in copies:
+        copy.start()
     item_sum = item_sum_ref[...]
     for i in range(1, blocks):
         query = queries[i][...]
@@ -247,6 +260,8 @@
     grad_ref[...] = unit_backward(
         INV_TEMP * (item_sum - queries[0][...].astype(jnp.float32)), unit_ref[...], scale_ref[...]
     )
+    for copy in copies:
+        copy.wait()
 
 
 def rotated(shard, axis, by):
@@ -289,6 +304,14 @@
     code = owner_ids * id_table.shape[0] + row_ids
     mirror_code = to_mirror(code)
     codes = [code, to_chip(code, 0, 1), mirror_code, to_chip(mirror_code, 0, 1)]
+    touched = pl.pallas_call(
+        touch_kernel,
+        in_specs=[pl.BlockSpec(memory_space=pl.ANY)],
+        out_shape=struct((16, width), f32),
+        scratch_shapes=[pltpu.VMEM((16, width), bf), pltpu.SemaphoreType.DMA(())],
+        compiler_params=params(52),
+        name="touch",
+    )(id_table)
     wide = pl.pallas_call(
         widen_kernel,
         out_shape=struct((2 * id_table.shape[0], width // 2), f32),
@@ -301,7 +324,7 @@
         + [struct((4, capacity), jnp.int32)] * chips,
         compiler_params=params(4),
         name="route",
-    )(*[c.T for c in codes])
+    )(*[c.T for c in codes], touched)
     wanted = [to_chip(requests[j], j) for j in reversed(range(chips))][::-1]
 
     def gather(askers):
@@ -387,12 +410,21 @@
         compiler_params=params(12),
         name="query_grads",
     )(query_bf, *items, w_first, w_second, slope, query_unit, query_scale)
-    item_grad = pl.pallas_call(
+    queries, loss = lax.optimization_barrier((queries, loss))
+    in_vmem, anywhere = pl.BlockSpec(memory_space=pltpu.VMEM), pl.BlockSpec(memory_space=pl.ANY)
+    item_grad, loss, query_grad = pl.pallas_call(
         functools.partial(item_grad_kernel, blocks),
-        out_shape=struct((pairs, width), f32),
+        in_specs=[in_vmem] * (2 * blocks + 3) + [anywhere] * 2,
+        out_specs=[in_vmem, anywhere, anywhere],
+        out_shape=[
+            struct((pairs, width), f32),
+            struct((1, pairs), f32),
+            struct((pairs, width), f32),
+        ],
+        scratch_shapes=[pltpu.SemaphoreType.DMA((2,))],
         compiler_params=params(12),
         name="item_grads",
-    )(*queries, *items, own_sum, item_unit, item_scale)
+    )(*queries, *items, own_sum, item_unit, item_scale, loss, query_grad)
     return loss.reshape(pairs), item_grad, query_grad
 
 

time: 58 us -> 57.7 us (level)
  waiting for transfers between devices: 19 us -> 21.9 us
  local copies, waits for them, and re-layouts: 2.2 us -> 0.02 us
  starting transfers between devices: 21.2 us -> 19.9 us
    ppermute x13, starting transfers between devices: 11.9 us -> 9.54 us  [to_chip(): return lax.ppermute(values, 'table', route)]
    unnamed x6, local copies, waits for them, and re-layouts: 2.2 us -> 0.02 us
    ppermute x13, waiting for transfers between devices: 16 us -> 18.1 us  [to_chip(): return lax.ppermute(values, 'table', route)]
    ppermute x3, waiting for transfers between devices: 1.63 us -> 2.72 us  [to_mirror(): lax.ppermute(values, 'table', [(t, (t + half) % shards) for t in range(sh...]
    ppermute x2, starting transfers between devices: 2.16 us -> 3.23 us  [rotated(): lax.ppermute(shard, axis, [(i, (i + by) % count) for i in range(count)])]
    pallas_call x1 -> x2, Pallas kernels: 1.38 us -> 2.18 us  [the longest x1 1.47 us: local(): pl.pallas_call(functools.partial(item_grad_kernel, blocks), in_specs=[in_...]
    pallas_call x1, Pallas kernels: 3.03 us -> 2.39 us  [local(): pl.pallas_call(functools.partial(query_grad_kernel, blocks), out_shape=[s...]
  transfers between devices with their start and end apart: 18 -> 18, of which waited for: 11 -> 12; matrix products, arithmetic and copies ran while one was open for 0% -> 0% of each run, Pallas kernels for 16% -> 16%
where the time goes in v4:
time: 57.7 us; the launch traced here: 57.5 us
  waiting for transfers between devices  21.9 us (38%)
  starting transfers between devices  19.9 us (34%)
  Pallas kernels  14 us (24%)
  other arithmetic  0.87 us (2%)
  between operations  0.78 us (1%)
    ppermute x13, waiting for transfers between devices, to_chip(): return lax.ppermute(values, 'table', route)  18.1 us
    ppermute x13, starting transfers between devices, to_chip(): return lax.ppermute(values, 'table', route)  9.54 us
    ppermute x3, starting transfers between devices, to_mirror(): lax.ppermute(values, 'table', [(t, (t + half) % shards) for t in range(sh...  7.1 us
    pallas_call x2, Pallas kernels, gather(): pl.pallas_call(functools.partial(gather_kernel, chips, askers), in_specs=...  3.91 us
    ppermute x2, starting transfers between devices, rotated(): lax.ppermute(shard, axis, [(i, (i + by) % count) for i in range(count)])  3.23 us
    ppermute x3, waiting for transfers between devices, to_mirror(): lax.ppermute(values, 'table', [(t, (t + half) % shards) for t in range(sh...  2.72 us
    pallas_call x1, Pallas kernels, local(): pl.pallas_call(functools.partial(query_grad_kernel, blocks), out_shape=[s...  2.39 us
    pallas_call x1, Pallas kernels, local(): pl.pallas_call(tower_kernel, out_shape=[struct((pairs, width), f32), stru...  1.84 us
  transfers between devices with their start and end apart: 18, of which 12 were waited for; matrix products, arithmetic and copies ran while one was open for 0% of the time, Pallas kernels for 16%

profile of v4, /device:TPU:0, one launch (start us, length us, event | category | flops | bytes accessed | tf_op | source)
XLA Modules:
  0.0 57.5 jit_solution(7482788557872715110)
XLA Ops:
  0.6 0.9 %multiply_add_fusion = s32[256,8]{0,1:T(8,128)S(1)} fusion(s32[256,8]{0,1:T(8,128)} %param.9, s32[256,8]{0,1:T(8,128)} %param.8), kind=kLoop, calls=%fused_computation | loop fusion | flops 4096 | bytes 24576 | tf_op jit(solution)/shard_map/add | solution.py:304
  1.5 4.0 %collective-permute-start.1 = (s32[256,8]{0,1:T(8,128)S(1)}, s32[256,8]{0,1:T(8,128)S(1)}, u32[]{:S(2)}, u32[]{:S(2)}) collective-permute-start(s32[256,8]{0,1:T(8,128)S(1)} %multiply_add_fusion), channel_id=1, source_target_pairs={{0,8},{1,9},{2,10},{3,11},{4,12},{5,13},{6,14},{7,15},{8,0},{9,1},... | collective-permute-start | bytes 24584 | tf_op jit(solution)/shard_map/ppermute | solution.py:302
  5.6 1.6 %collective-permute-done.1 = s32[256,8]{0,1:T(8,128)S(1)} collective-permute-done((s32[256,8]{0,1:T(8,128)S(1)}, s32[256,8]{0,1:T(8,128)S(1)}, u32[]{:S(2)}, u32[]{:S(2)}) %collective-permute-start.1) | collective-permute-done | bytes 8224 | tf_op jit(solution)/shard_map/ppermute | solution.py:302
  7.2 0.7 %touch.1.refs_4_ = f32[16,256]{1,0:T(8,128)S(1)} custom-call(bf16[8192,256]{1,0:T(8,128)(2,1)} %table_ref.1), custom_call_target="tpu_custom_call" | custom-call | tf_op jit(solution)/shard_map/touch/pallas_call | solution.py:307
  7.9 0.4 collective-permute-done.2
  8.3 1.1 %route.1 = (s32[8,192]{1,0:T(8,128)S(1)}, s32[8,192]{1,0:T(8,128)S(1)}, s32[4,192]{1,0:T(4,128)S(1)}, s32[4,192]{1,0:T(4,128)S(1)}, s32[4,192]{1,0:T(4,128)S(1)}, /*index=5*/s32[4,192]{1,0:T(4,128)S(1)}) custom-call(s32[8,256]{1,0:T(8,128)S(1)} %bitcast.5, s32[8,256]{1,0:T(8,128)S(1)} %bitcast.7, s32[8,256]{1,0:T(8,128)S(1)} %bitcast.6, ...), custom_call_target="tpu_custom_call" | custom-call | tf_op jit(solution)/shard_map/route/pallas_call | solution.py:321
  9.5 2.9 %collective-permute-start.3 = (s32[4,192]{1,0:T(4,128)S(1)}, s32[4,192]{1,0:T(4,128)S(1)}, u32[]{:S(2)}, u32[]{:S(2)}) collective-permute-start(s32[4,192]{1,0:T(4,128)S(1)} %get-tuple-element.40), channel_id=1, source_target_pairs={{0,6},{1,7},{2,4},{3,5},{4,2},{5,3},{6,0},{7,1},{8,14},{9,15},{10,... | collective-permute-start | bytes 9224 | tf_op jit(solution)/shard_map/ppermute | solution.py:299
  12.4 0.4 collective-permute-start.4
  13.0 0.7 %widen.1.refs_4_ = f32[16384,128]{1,0:T(8,128)S(1)} custom-call(bf16[8192,256]{1,0:T(8,128)(2,1)S(1)} %copy-done), custom_call_target="tpu_custom_call" | custom-call | tf_op jit(solution)/shard_map/widen/pallas_call | solution.py:315
  14.0 2.0 %collective-permute-done.4.refs_1_ = s32[4,192]{1,0:T(4,128)S(1)} collective-permute-done((s32[4,192]{1,0:T(4,128)S(1)}, s32[4,192]{1,0:T(4,128)S(1)}, u32[]{:S(2)}, u32[]{:S(2)}) %collective-permute-start.4) | collective-permute-done | bytes 3104 | tf_op jit(solution)/shard_map/ppermute | solution.py:299
  16.0 0.4 collective-permute-done.5.refs_2_
  16.4 2.0 %gather.3 = (bf16[4,192,256]{2,1,0:T(8,128)(2,1)S(1)}, bf16[4,192,256]{2,1,0:T(8,128)(2,1)S(1)}) custom-call(s32[4,192]{1,0:T(4,128)S(1)} %collective-permute-done.3.refs_0_, s32[4,192]{1,0:T(4,128)S(1)} %collective-permute-done.4.refs_1_, s32[4,192]{1,0:T(4,128)S(1)} %collective-permute-done.5.refs_2_, s32[4,192]{1,0:T(4,128)S(1)} %get-tuple-element.43.refs_3_, ...), custom_call_target="tpu_custom_call" | custom-call | tf_op jit(solution)/shard_map/gather/pallas_call | solution.py:331
  18.5 0.5 collective-permute-start.6
  19.0 2.0 %gather.2 = (bf16[4,192,256]{2,1,0:T(8,128)(2,1)S(1)}, bf16[4,192,256]{2,1,0:T(8,128)(2,1)S(1)}) custom-call(s32[4,192]{1,0:T(4,128)S(1)} %collective-permute-done.3.refs_0_, s32[4,192]{1,0:T(4,128)S(1)} %collective-permute-done.4.refs_1_, s32[4,192]{1,0:T(4,128)S(1)} %collective-permute-done.5.refs_2_, s32[4,192]{1,0:T(4,128)S(1)} %get-tuple-element.43.refs_3_, ...), custom_call_target="tpu_custom_call" | custom-call | tf_op jit(solution)/shard_map/gather/pallas_call | solution.py:331
  21.0 1.6 %collective-permute-start.8 = (bf16[2,192,256]{2,1,0:T(8,128)(2,1)S(1)}, bf16[2,192,256]{2,1,0:T(8,128)(2,1)S(1)}, u32[]{:S(2)}, u32[]{:S(2)}) collective-permute-start(bf16[2,192,256]{2,1,0:T(8,128)(2,1)S(1)} %get-tuple-element.50), channel_id=1, source_target_pairs={{0,6},{1,7},{2,4},{3,5},{4,2},{5,3},{6,0},{7,1},{8,14},{9,15},{10,... | collective-permute-start | bytes 589832 | tf_op jit(solution)/shard_map/ppermute | solution.py:299
  22.7 1.9 %collective-permute-start.10 = (bf16[2,192,256]{2,1,0:T(8,128)(2,1)S(1)}, bf16[2,192,256]{2,1,0:T(8,128)(2,1)S(1)}, u32[]{:S(2)}, u32[]{:S(2)}) collective-permute-start(bf16[2,192,256]{2,1,0:T(8,128)(2,1)S(1)} %get-tuple-element.52), channel_id=1, source_target_pairs={{0,2},{1,3},{2,0},{3,1},{4,6},{5,7},{6,4},{7,5},{8,10},{9,11},{10,... | collective-permute-start | bytes 589832 | tf_op jit(solution)/shard_map/ppermute | solution.py:299
  24.6 1.6 %collective-permute-start.12 = (bf16[2,192,256]{2,1,0:T(8,128)(2,1)S(1)}, bf16[2,192,256]{2,1,0:T(8,128)(2,1)S(1)}, u32[]{:S(2)}, u32[]{:S(2)}) collective-permute-start(bf16[2,192,256]{2,1,0:T(8,128)(2,1)S(1)} %get-tuple-element.53), channel_id=1, source_target_pairs={{0,6},{1,7},{2,4},{3,5},{4,2},{5,3},{6,0},{7,1},{8,14},{9,15},{10,... | collective-permute-start | bytes 589832 | tf_op jit(solution)/shard_map/ppermute | solution.py:299
  26.3 3.5 %collective-permute-done.8.refs_0_ = bf16[2,192,256]{2,1,0:T(8,128)(2,1)S(1)} collective-permute-done((bf16[2,192,256]{2,1,0:T(8,128)(2,1)S(1)}, bf16[2,192,256]{2,1,0:T(8,128)(2,1)S(1)}, u32[]{:S(2)}, u32[]{:S(2)}) %collective-permute-start.8) | collective-permute-done | bytes 196640 | tf_op jit(solution)/shard_map/ppermute | solution.py:299
  29.9 2.7 %collective-permute-done.9.refs_1_ = bf16[2,192,256]{2,1,0:T(8,128)(2,1)S(1)} collective-permute-done((bf16[2,192,256]{2,1,0:T(8,128)(2,1)S(1)}, bf16[2,192,256]{2,1,0:T(8,128)(2,1)S(1)}, u32[]{:S(2)}, u32[]{:S(2)}) %collective-permute-start.9) | collective-permute-done | bytes 196640 | tf_op jit(solution)/shard_map/ppermute | solution.py:299
  32.7 1.4 %collective-permute-done.10.refs_2_ = bf16[2,192,256]{2,1,0:T(8,128)(2,1)S(1)} collective-permute-done((bf16[2,192,256]{2,1,0:T(8,128)(2,1)S(1)}, bf16[2,192,256]{2,1,0:T(8,128)(2,1)S(1)}, u32[]{:S(2)}, u32[]{:S(2)}) %collective-permute-start.10) | collective-permute-done | bytes 196640 | tf_op jit(solution)/shard_map/ppermute | solution.py:299
  34.1 0.4 item_sums.1
  34.5 2.6 %collective-permute-start.11 = (bf16[256,256]{1,0:T(8,128)(2,1)S(1)}, bf16[256,256]{1,0:T(8,128)(2,1)S(1)}, u32[]{:S(2)}, u32[]{:S(2)}) collective-permute-start(bf16[256,256]{1,0:T(8,128)(2,1)S(1)} %item_sums.1), channel_id=1, source_target_pairs={{0,8},{1,9},{2,10},{3,11},{4,12},{5,13},{6,14},{7,15},{8,0},{9,1},... | collective-permute-start | bytes 393224 | tf_op jit(solution)/shard_map/ppermute | solution.py:302
  38.0 5.6 %collective-permute-done.12.refs_0_ = bf16[2,192,256]{2,1,0:T(8,128)(2,1)S(1)} collective-permute-done((bf16[2,192,256]{2,1,0:T(8,128)(2,1)S(1)}, bf16[2,192,256]{2,1,0:T(8,128)(2,1)S(1)}, u32[]{:S(2)}, u32[]{:S(2)}) %collective-permute-start.12) | collective-permute-done | bytes 196640 | tf_op jit(solution)/shard_map/ppermute | solution.py:299
  43.6 1.8 %collective-permute-done.13.refs_1_ = bf16[2,192,256]{2,1,0:T(8,128)(2,1)S(1)} collective-permute-done((bf16[2,192,256]{2,1,0:T(8,128)(2,1)S(1)}, bf16[2,192,256]{2,1,0:T(8,128)(2,1)S(1)}, u32[]{:S(2)}, u32[]{:S(2)}) %collective-permute-start.13) | collective-permute-done | bytes 196640 | tf_op jit(solution)/shard_map/ppermute | solution.py:299
  45.4 0.5 items.1
  45.9 1.7 %collective-permute-start.17 = (bf16[256,256]{1,0:T(8,128)(2,1)S(1)}, bf16[256,256]{1,0:T(8,128)(2,1)S(1)}, u32[]{:S(2)}, u32[]{:S(2)}) collective-permute-start(bf16[256,256]{1,0:T(8,128)(2,1)S(1)} %get-tuple-element.55.refs_1_.refs_2_), channel_id=1, source_target_pairs={{0,16},{16,0},{1,17},{17,1},{2,18},{18,2},{3,19},{19,3},{4,20},{20... | collective-permute-start | bytes 393224 | tf_op jit(solution)/shard_map/ppermute | solution.py:269
  48.0 1.1 %collective-permute-done.15.far_ref = bf16[256,256]{1,0:T(8,128)(2,1)S(1)} collective-permute-done((bf16[256,256]{1,0:T(8,128)(2,1)S(1)}, bf16[256,256]{1,0:T(8,128)(2,1)S(1)}, u32[]{:S(2)}, u32[]{:S(2)}) %collective-permute-start.15) | collective-permute-done | bytes 131104 | tf_op jit(solution)/shard_map/ppermute | solution.py:302
  49.1 1.8 %tower.1 = (f32[256,256]{1,0:T(8,128)S(1)}, f32[256,1]{1,0:T(8,128)S(1)}, bf16[256,256]{1,0:T(8,128)(2,1)S(1)}, f32[256,4096]{1,0:T(8,128)S(1)}) custom-call(f32[256,256]{1,0:T(8,128)S(1)} %query_sums.2.near_ref, bf16[256,256]{1,0:T(8,128)(2,1)S(1)} %collective-permute-done.15.far_ref, bf16[256,4096]{1,0:T(8,128)(2,1)S(1)} %copy-done.1, ...), custom_call_target="tpu_custom_call" | custom-call | tf_op jit(solution)/shard_map/tower/pallas_call | solution.py:391
  51.0 1.6 %collective-permute-start.16 = (bf16[256,256]{1,0:T(8,128)(2,1)S(1)}, bf16[256,256]{1,0:T(8,128)(2,1)S(1)}, u32[]{:S(2)}, u32[]{:S(2)}) collective-permute-start(bf16[256,256]{1,0:T(8,128)(2,1)S(1)} %get-tuple-element.63.refs_0_), channel_id=1, source_target_pairs={{0,16},{16,0},{1,17},{17,1},{2,18},{18,2},{3,19},{19,3},{4,20},{20... | collective-permute-start | bytes 393224 | tf_op jit(solution)/shard_map/ppermute | solution.py:269
  52.5 2.4 %query_grads.1 = (f32[1,256]{1,0:T(1,128)S(1)}, f32[256,256]{1,0:T(8,128)S(1)}, f32[256,256]{1,0:T(8,128)S(1)}) custom-call(bf16[256,256]{1,0:T(8,128)(2,1)S(1)} %get-tuple-element.63.refs_0_, bf16[256,256]{1,0:T(8,128)(2,1)S(1)} %get-tuple-element.55.refs_1_.refs_2_, bf16[256,256]{1,0:T(8,128)(2,1)S(1)} %collective-permute-done.17.refs_2_.refs_3_, ...), custom_call_target="tpu_custom_call" | custom-call | tf_op jit(solution)/shard_map/query_grads/pallas_call | solution.py:403
  54.9 1.1 %collective-permute-done.16.refs_1_ = bf16[256,256]{1,0:T(8,128)(2,1)S(1)} collective-permute-done((bf16[256,256]{1,0:T(8,128)(2,1)S(1)}, bf16[256,256]{1,0:T(8,128)(2,1)S(1)}, u32[]{:S(2)}, u32[]{:S(2)}) %collective-permute-start.16) | collective-permute-done | bytes 131104 | tf_op jit(solution)/shard_map/ppermute | solution.py:269
  56.0 1.5 %item_grads.1 = (f32[256,256]{1,0:T(8,128)}, f32[1,256]{1,0:T(1,128)}, f32[256,256]{1,0:T(8,128)}) custom-call(bf16[256,256]{1,0:T(8,128)(2,1)S(1)} %get-tuple-element.63.refs_0_, bf16[256,256]{1,0:T(8,128)(2,1)S(1)} %collective-permute-done.16.refs_1_, bf16[256,256]{1,0:T(8,128)(2,1)S(1)} %get-tuple-element.55.refs_1_.refs_2_, ...), custom_call_target="tpu_custom_call" | custom-call | tf_op jit(solution)/shard_map/item_grads/pallas_call | solution.py:415
  (25 shorter events, 2.3 us)
Async XLA Ops:
  0.6 12.4 %copy-start = (bf16[8192,256]{1,0:T(8,128)(2,1)S(1)}, bf16[8192,256]{1,0:T(8,128)(2,1)}, u32[]{:S(2)}) copy-start(bf16[8192,256]{1,0:T(8,128)(2,1)} %table_ref.1) | copy-start | bytes 12582916
  1.5 5.7 %collective-permute-start.1 = (s32[256,8]{0,1:T(8,128)S(1)}, s32[256,8]{0,1:T(8,128)S(1)}, u32[]{:S(2)}, u32[]{:S(2)}) collective-permute-start(s32[256,8]{0,1:T(8,128)S(1)} %multiply_add_fusion), channel_id=1, source_target_pairs={{0,8},{1,9},{2,10},{3,11},{4,12},{5,13},{6,14},{7,15},{8,0},{9,1},... | collective-permute-start | bytes 24584 | tf_op jit(solution)/shard_map/ppermute | solution.py:302
  5.5 2.3 %collective-permute-start = (s32[256,8]{0,1:T(8,128)S(1)}, s32[256,8]{0,1:T(8,128)S(1)}, u32[]{:S(2)}, u32[]{:S(2)}) collective-permute-start(s32[256,8]{0,1:T(8,128)S(1)} %multiply_add_fusion), channel_id=1, source_target_pairs={{0,1},{1,0},{2,3},{3,2},{4,5},{5,4},{6,7},{7,6},{8,9},{9,8},{10,11... | collective-permute-start | bytes 24584 | tf_op jit(solution)/shard_map/ppermute | solution.py:299
  7.2 1.2 %collective-permute-start.2 = (s32[256,8]{0,1:T(8,128)S(1)}, s32[256,8]{0,1:T(8,128)S(1)}, u32[]{:S(2)}, u32[]{:S(2)}) collective-permute-start(s32[256,8]{0,1:T(8,128)S(1)} %collective-permute-done.1), channel_id=1, source_target_pairs={{0,1},{1,0},{2,3},{3,2},{4,5},{5,4},{6,7},{7,6},{8,9},{9,8},{10,11... | collective-permute-start | bytes 24584 | tf_op jit(solution)/shard_map/ppermute | solution.py:299
  9.5 4.6 %collective-permute-start.3 = (s32[4,192]{1,0:T(4,128)S(1)}, s32[4,192]{1,0:T(4,128)S(1)}, u32[]{:S(2)}, u32[]{:S(2)}) collective-permute-start(s32[4,192]{1,0:T(4,128)S(1)} %get-tuple-element.40), channel_id=1, source_target_pairs={{0,6},{1,7},{2,4},{3,5},{4,2},{5,3},{6,0},{7,1},{8,14},{9,15},{10,... | collective-permute-start | bytes 9224 | tf_op jit(solution)/shard_map/ppermute | solution.py:299
  12.4 3.6 %collective-permute-start.4 = (s32[4,192]{1,0:T(4,128)S(1)}, s32[4,192]{1,0:T(4,128)S(1)}, u32[]{:S(2)}, u32[]{:S(2)}) collective-permute-start(s32[4,192]{1,0:T(4,128)S(1)} %get-tuple-element.41), channel_id=1, source_target_pairs={{0,4},{1,5},{2,6},{3,7},{4,0},{5,1},{6,2},{7,3},{8,12},{9,13},{10,... | collective-permute-start | bytes 9224 | tf_op jit(solution)/shard_map/ppermute | solution.py:299
  12.8 3.6 %collective-permute-start.5 = (s32[4,192]{1,0:T(4,128)S(1)}, s32[4,192]{1,0:T(4,128)S(1)}, u32[]{:S(2)}, u32[]{:S(2)}) collective-permute-start(s32[4,192]{1,0:T(4,128)S(1)} %get-tuple-element.42), channel_id=1, source_target_pairs={{0,2},{1,3},{2,0},{3,1},{4,6},{5,7},{6,4},{7,5},{8,10},{9,11},{10,... | collective-permute-start | bytes 9224 | tf_op jit(solution)/shard_map/ppermute | solution.py:299
  18.4 2.6 %collective-permute-start.7 = (bf16[4,192,256]{2,1,0:T(8,128)(2,1)S(1)}, bf16[4,192,256]{2,1,0:T(8,128)(2,1)S(1)}, u32[]{:S(2)}, u32[]{:S(2)}) collective-permute-start(bf16[4,192,256]{2,1,0:T(8,128)(2,1)S(1)} %get-tuple-element.49), channel_id=1, source_target_pairs={{0,1},{1,0},{2,3},{3,2},{4,5},{5,4},{6,7},{7,6},{8,9},{9,8},{10,11... | collective-permute-start | bytes 1179656 | tf_op jit(solution)/shard_map/ppermute | solution.py:299
  18.5 6.1 %collective-permute-start.6 = (bf16[4,192,256]{2,1,0:T(8,128)(2,1)S(1)}, bf16[4,192,256]{2,1,0:T(8,128)(2,1)S(1)}, u32[]{:S(2)}, u32[]{:S(2)}) collective-permute-start(bf16[4,192,256]{2,1,0:T(8,128)(2,1)S(1)} %get-tuple-element.45), channel_id=1, source_target_pairs={{0,1},{1,0},{2,3},{3,2},{4,5},{5,4},{6,7},{7,6},{8,9},{9,8},{10,11... | collective-permute-start | bytes 1179656 | tf_op jit(solution)/shard_map/ppermute | solution.py:299
  20.9 28.2 %copy-start.1 = (bf16[256,4096]{1,0:T(8,128)(2,1)S(1)}, bf16[256,4096]{1,0:T(8,128)(2,1)}, u32[]{:S(2)}) copy-start(bf16[256,4096]{1,0:T(8,128)(2,1)} %refs_3_.1) | copy-start | bytes 6291460
  21.0 28.2 %copy-start.2 = (bf16[4096,256]{1,0:T(8,128)(2,1)S(1)}, bf16[4096,256]{1,0:T(8,128)(2,1)}, u32[]{:S(2)}) copy-start(bf16[4096,256]{1,0:T(8,128)(2,1)} %refs_4_.1) | copy-start | bytes 6291460
  21.0 8.8 %collective-permute-start.8 = (bf16[2,192,256]{2,1,0:T(8,128)(2,1)S(1)}, bf16[2,192,256]{2,1,0:T(8,128)(2,1)S(1)}, u32[]{:S(2)}, u32[]{:S(2)}) collective-permute-start(bf16[2,192,256]{2,1,0:T(8,128)(2,1)S(1)} %get-tuple-element.50), channel_id=1, source_target_pairs={{0,6},{1,7},{2,4},{3,5},{4,2},{5,3},{6,0},{7,1},{8,14},{9,15},{10,... | collective-permute-start | bytes 589832 | tf_op jit(solution)/shard_map/ppermute | solution.py:299
  22.6 10.1 %collective-permute-start.9 = (bf16[2,192,256]{2,1,0:T(8,128)(2,1)S(1)}, bf16[2,192,256]{2,1,0:T(8,128)(2,1)S(1)}, u32[]{:S(2)}, u32[]{:S(2)}) collective-permute-start(bf16[2,192,256]{2,1,0:T(8,128)(2,1)S(1)} %get-tuple-element.51), channel_id=1, source_target_pairs={{0,4},{1,5},{2,6},{3,7},{4,0},{5,1},{6,2},{7,3},{8,12},{9,13},{10,... | collective-permute-start | bytes 589832 | tf_op jit(solution)/shard_map/ppermute | solution.py:299
  22.7 11.3 %collective-permute-start.10 = (bf16[2,192,256]{2,1,0:T(8,128)(2,1)S(1)}, bf16[2,192,256]{2,1,0:T(8,128)(2,1)S(1)}, u32[]{:S(2)}, u32[]{:S(2)}) collective-permute-start(bf16[2,192,256]{2,1,0:T(8,128)(2,1)S(1)} %get-tuple-element.52), channel_id=1, source_target_pairs={{0,2},{1,3},{2,0},{3,1},{4,6},{5,7},{6,4},{7,5},{8,10},{9,11},{10,... | collective-permute-start | bytes 589832 | tf_op jit(solution)/shard_map/ppermute | solution.py:299
  24.6 19.0 %collective-permute-start.12 = (bf16[2,192,256]{2,1,0:T(8,128)(2,1)S(1)}, bf16[2,192,256]{2,1,0:T(8,128)(2,1)S(1)}, u32[]{:S(2)}, u32[]{:S(2)}) collective-permute-start(bf16[2,192,256]{2,1,0:T(8,128)(2,1)S(1)} %get-tuple-element.53), channel_id=1, source_target_pairs={{0,6},{1,7},{2,4},{3,5},{4,2},{5,3},{6,0},{7,1},{8,14},{9,15},{10,... | collective-permute-start | bytes 589832 | tf_op jit(solution)/shard_map/ppermute | solution.py:299
  26.2 19.2 %collective-permute-start.13 = (bf16[2,192,256]{2,1,0:T(8,128)(2,1)S(1)}, bf16[2,192,256]{2,1,0:T(8,128)(2,1)S(1)}, u32[]{:S(2)}, u32[]{:S(2)}) collective-permute-start(bf16[2,192,256]{2,1,0:T(8,128)(2,1)S(1)} %get-tuple-element.54), channel_id=1, source_target_pairs={{0,4},{1,5},{2,6},{3,7},{4,0},{5,1},{6,2},{7,3},{8,12},{9,13},{10,... | collective-permute-start | bytes 589832 | tf_op jit(solution)/shard_map/ppermute | solution.py:299
  29.8 15.6 %collective-permute-start.14 = (bf16[2,192,256]{2,1,0:T(8,128)(2,1)S(1)}, bf16[2,192,256]{2,1,0:T(8,128)(2,1)S(1)}, u32[]{:S(2)}, u32[]{:S(2)}) collective-permute-start(bf16[2,192,256]{2,1,0:T(8,128)(2,1)S(1)} %get-tuple-element.46), channel_id=1, source_target_pairs={{0,2},{1,3},{2,0},{3,1},{4,6},{5,7},{6,4},{7,5},{8,10},{9,11},{10,... | collective-permute-start | bytes 589832 | tf_op jit(solution)/shard_map/ppermute | solution.py:299
  34.5 10.9 %collective-permute-start.11 = (bf16[256,256]{1,0:T(8,128)(2,1)S(1)}, bf16[256,256]{1,0:T(8,128)(2,1)S(1)}, u32[]{:S(2)}, u32[]{:S(2)}) collective-permute-start(bf16[256,256]{1,0:T(8,128)(2,1)S(1)} %item_sums.1), channel_id=1, source_target_pairs={{0,8},{1,9},{2,10},{3,11},{4,12},{5,13},{6,14},{7,15},{8,0},{9,1},... | collective-permute-start | bytes 393224 | tf_op jit(solution)/shard_map/ppermute | solution.py:302
  37.6 11.5 %collective-permute-start.15 = (bf16[256,256]{1,0:T(8,128)(2,1)S(1)}, bf16[256,256]{1,0:T(8,128)(2,1)S(1)}, u32[]{:S(2)}, u32[]{:S(2)}) collective-permute-start(bf16[256,256]{1,0:T(8,128)(2,1)S(1)} %query_sums.3), channel_id=1, source_target_pairs={{0,8},{1,9},{2,10},{3,11},{4,12},{5,13},{6,14},{7,15},{8,0},{9,1},... | collective-permute-start | bytes 393224 | tf_op jit(solution)/shard_map/ppermute | solution.py:302
  45.9 6.6 %collective-permute-start.17 = (bf16[256,256]{1,0:T(8,128)(2,1)S(1)}, bf16[256,256]{1,0:T(8,128)(2,1)S(1)}, u32[]{:S(2)}, u32[]{:S(2)}) collective-permute-start(bf16[256,256]{1,0:T(8,128)(2,1)S(1)} %get-tuple-element.55.refs_1_.refs_2_), channel_id=1, source_target_pairs={{0,16},{16,0},{1,17},{17,1},{2,18},{18,2},{3,19},{19,3},{4,20},{20... | collective-permute-start | bytes 393224 | tf_op jit(solution)/shard_map/ppermute | solution.py:269
  51.0 5.0 %collective-permute-start.16 = (bf16[256,256]{1,0:T(8,128)(2,1)S(1)}, bf16[256,256]{1,0:T(8,128)(2,1)S(1)}, u32[]{:S(2)}, u32[]{:S(2)}) collective-permute-start(bf16[256,256]{1,0:T(8,128)(2,1)S(1)} %get-tuple-element.63.refs_0_), channel_id=1, source_target_pairs={{0,16},{16,0},{1,17},{17,1},{2,18},{18,2},{3,19},{19,3},{4,20},{20... | collective-permute-start | bytes 393224 | tf_op jit(solution)/shard_map/ppermute | solution.py:269

commit v5 on v4

--- a/solution.py
+++ b/solution.py
@@ -44,26 +44,26 @@
     return scale * (grad - unit * jnp.sum(unit * grad, axis=-1, keepdims=True))
 
 
-def route_kernel(relative, rows_dev, *refs):
-    codes, near_ref, far_ref, request_refs = refs[:4], refs[5], refs[6], refs[7:]
-    chips = len(request_refs)
+def packed_lists(relative, rows_dev, askers, codes, chips, capacity):
     bags, pairs = codes[0].shape
-    capacity = near_ref.shape[1]
-    lists = 6 * chips
+    lists = len(askers) * chips
     place = lax.axis_index("table")
     half = 2 * chips
     list_of = iota((lists, pairs), 0)
     chip = relative(place % half // 2, list_of % chips)
     asker = list_of // chips
-    core = jnp.where(asker < 4, place % 2, 1 - place % 2)
+    core = place % 2
+    for at, name in enumerate(askers):
+        if name >= 4:
+            core = jnp.where(asker == at, 1 - place % 2, core)
     start = (place // half * half + chip * 2 + core) * rows_dev
     named = jnp.zeros((lists, pairs), jnp.float32)
     rows = jnp.zeros((lists, pairs), jnp.int32)
     kind = jnp.zeros((lists, pairs), jnp.int32)
     for k in range(bags):
-        code = codes[0][k : k + 1, :]
-        for r, at in ((1, 1), (2, 2), (3, 3), (5, 2)):
-            code = jnp.where(asker == r, codes[at][k : k + 1, :], code)
+        code = codes[(0, 1, 2, 3, 0, 2)[askers[0]]][k : k + 1, :]
+        for at, name in enumerate(askers[1:], 1):
+            code = jnp.where(asker == at, codes[(0, 1, 2, 3, 0, 2)[name]][k : k + 1, :], code)
         row = code - start
         hit = (row >= 0) & (row < rows_dev)
         named = jnp.where(hit, 1.0, named)
@@ -79,13 +79,26 @@
         chosen = jnp.where(slot[s : s + 1, :] == places, 1.0, 0.0).astype(jnp.bfloat16)
         got = row_dot(packed, chosen).astype(jnp.int32)
         high, low, which, pair = [got[i * lists + s : i * lists + s + 1, :] for i in range(4)]
-        asked, j = s // chips, s % chips
-        if asked < 4:
-            request_refs[j][asked : asked + 1, :] = 2 * (high * 256 + low)
-        if asked in (0, 2, 4, 5):
-            at = j if asked < 4 else chips + j
-            bag_ref = near_ref if asked in (0, 4) else far_ref
-            bag_ref[at : at + 1, :] = (which - 1) * pairs + pair
+        yield s // chips, s % chips, high * 256 + low, which, pair
+
+
+def route_kernel(relative, rows_dev, *refs):
+    codes, requests = refs[:4], refs[5:]
+    capacity = requests[0].shape[1]
+    lists = packed_lists(relative, rows_dev, (0, 1, 2, 3), codes, len(requests), capacity)
+    for at, j, row, _, _ in lists:
+        requests[j][at : at + 1, :] = 2 * row
+
+
+def bag_kernel(relative, rows_dev, *refs):
+    codes, outs = refs[:4], refs[4:]
+    half, capacity = outs[0].shape
+    pairs = codes[0].shape[1]
+    chips = half // 2
+    lists = packed_lists(relative, rows_dev, (0, 4, 2, 5), codes, chips, capacity)
+    for at, j, _, which, pair in lists:
+        place = at % 2 * chips + j
+        outs[at // 2][place : place + 1, :] = (which - 1) * pairs + pair
 
 
 def touch_kernel(table_hbm, out_ref, rows_ref, sem):
@@ -318,14 +331,23 @@
         compiler_params=params(8),
         name="widen",
     )(id_table)
-    near_bags, far_bags, *requests = pl.pallas_call(
+    codes = [c.T for c in codes]
+    requests = pl.pallas_call(
         functools.partial(route_kernel, relative, id_table.shape[0]),
-        out_shape=[struct((half, capacity), jnp.int32)] * 2
-        + [struct((4, capacity), jnp.int32)] * chips,
+        out_shape=[struct((4, capacity), jnp.int32)] * chips,
         compiler_params=params(4),
         name="route",
-    )(*[c.T for c in codes], touched)
+    )(*codes, touched)
+    *codes, _ = lax.optimization_barrier((*codes, requests[0]))
+    near_bags, far_bags = pl.pallas_call(
+        functools.partial(bag_kernel, relative, id_table.shape[0]),
+        out_shape=[struct((half, capacity), jnp.int32)] * 2,
+        compiler_params=params(4),
+        name="bag_lists",
+    )(*codes)
     wanted = [to_chip(requests[j], j) for j in reversed(range(chips))][::-1]
+
+    wide, near_bags, far_bags = lax.optimization_barrier((wide, near_bags, far_bags))
 
     def gather(askers):
         return pl.pallas_call(
@@ -358,7 +380,7 @@
         return (same, swapped, *arrived), messages
 
     far_other, near_other = [to_chip(rows, 0, 1) for rows in gather((3, 1))]
-    far_same, near_same = gather((2, 0))
+    (far_same,), (near_same,) = gather((2,)), gather((0,))
     far_rows, _ = answered(far_same, far_other)
     near_rows, near_messages = answered(near_same, near_other)
     far_bags, _ = lax.optimization_barrier((far_bags, near_messages[-1]))

time: 57.7 us -> 56.8 us (0.984)
  waiting for transfers between devices: 21.9 us -> 19.7 us
  Pallas kernels: 14 us -> 15.4 us
    ppermute x13, waiting for transfers between devices: 18.1 us -> 15.9 us  [to_chip(): return lax.ppermute(values, 'table', route)]
    pallas_call x2 -> x3, Pallas kernels: 3.91 us -> 4.76 us  [gather(): pl.pallas_call(functools.partial(gather_kernel, chips, askers), in_specs=...]
    pallas_call x0 -> x1, Pallas kernels: none -> 0.81 us  [local(): pl.pallas_call(functools.partial(bag_kernel, relative, id_table.shape[0])...]
  transfers between devices with their start and end apart: 18 -> 18, of which waited for: 12 -> 11; matrix products, arithmetic and copies ran while one was open for 0% -> 0% of each run, Pallas kernels for 16% -> 20%
where the time goes in v5:
time: 56.8 us; the launch traced here: 56.6 us
  starting transfers between devices  19.9 us (35%)
  waiting for transfers between devices  19.7 us (35%)
  Pallas kernels  15.4 us (27%)
  other arithmetic  0.87 us (2%)
  between operations  0.81 us (1%)
    ppermute x13, waiting for transfers between devices, to_chip(): return lax.ppermute(values, 'table', route)  15.9 us
    ppermute x13, starting transfers between devices, to_chip(): return lax.ppermute(values, 'table', route)  9.56 us
    ppermute x3, starting transfers between devices, to_mirror(): lax.ppermute(values, 'table', [(t, (t + half) % shards) for t in range(sh...  7.09 us
    pallas_call x3, Pallas kernels, gather(): pl.pallas_call(functools.partial(gather_kernel, chips, askers), in_specs=...  4.76 us
    ppermute x2, starting transfers between devices, rotated(): lax.ppermute(shard, axis, [(i, (i + by) % count) for i in range(count)])  3.2 us
    ppermute x3, waiting for transfers between devices, to_mirror(): lax.ppermute(values, 'table', [(t, (t + half) % shards) for t in range(sh...  2.7 us
    pallas_call x1, Pallas kernels, local(): pl.pallas_call(functools.partial(query_grad_kernel, blocks), out_shape=[s...  2.39 us
    pallas_call x1, Pallas kernels, local(): pl.pallas_call(tower_kernel, out_shape=[struct((pairs, width), f32), stru...  1.84 us
  transfers between devices with their start and end apart: 18, of which 11 were waited for; matrix products, arithmetic and copies ran while one was open for 0% of the time, Pallas kernels for 20%

profile of v5, /device:TPU:0, one launch (start us, length us, event | category | flops | bytes accessed | tf_op | source)
XLA Modules:
  0.0 56.6 jit_solution(5863362060072850596)
XLA Ops:
  0.6 0.9 %multiply_add_fusion = s32[256,8]{0,1:T(8,128)S(1)} fusion(s32[256,8]{0,1:T(8,128)} %param.9, s32[256,8]{0,1:T(8,128)} %param.8), kind=kLoop, calls=%fused_computation | loop fusion | flops 4096 | bytes 24576 | tf_op jit(solution)/shard_map/add | solution.py:317
  1.5 4.0 %collective-permute-start.1 = (s32[256,8]{0,1:T(8,128)S(1)}, s32[256,8]{0,1:T(8,128)S(1)}, u32[]{:S(2)}, u32[]{:S(2)}) collective-permute-start(s32[256,8]{0,1:T(8,128)S(1)} %multiply_add_fusion), channel_id=1, source_target_pairs={{0,8},{1,9},{2,10},{3,11},{4,12},{5,13},{6,14},{7,15},{8,0},{9,1},... | collective-permute-start | bytes 24584 | tf_op jit(solution)/shard_map/ppermute | solution.py:315
  5.6 1.6 %collective-permute-done.1 = s32[256,8]{0,1:T(8,128)S(1)} collective-permute-done((s32[256,8]{0,1:T(8,128)S(1)}, s32[256,8]{0,1:T(8,128)S(1)}, u32[]{:S(2)}, u32[]{:S(2)}) %collective-permute-start.1) | collective-permute-done | bytes 8224 | tf_op jit(solution)/shard_map/ppermute | solution.py:315
  7.2 0.7 %touch.1.refs_4_ = f32[16,256]{1,0:T(8,128)S(1)} custom-call(bf16[8192,256]{1,0:T(8,128)(2,1)} %table_hbm.1), custom_call_target="tpu_custom_call" | custom-call | tf_op jit(solution)/shard_map/touch/pallas_call | solution.py:320
  8.3 0.8 %route.1 = (s32[4,192]{1,0:T(4,128)S(1)}, s32[4,192]{1,0:T(4,128)S(1)}, s32[4,192]{1,0:T(4,128)S(1)}, s32[4,192]{1,0:T(4,128)S(1)}) custom-call(s32[8,256]{1,0:T(8,128)S(1)} %bitcast.5, s32[8,256]{1,0:T(8,128)S(1)} %bitcast.9, s32[8,256]{1,0:T(8,128)S(1)} %bitcast.7, s32[8,256]{1,0:T(8,128)S(1)} %bitcast.11, f32[16,256]{1,0:T(8,128)S(1)} %touch.1.refs_4_), custom_call_target="tpu_custom_call" | custom-call | tf_op jit(solution)/shard_map/route/pallas_call | solution.py:335
  9.2 2.9 %collective-permute-start.3 = (s32[4,192]{1,0:T(4,128)S(1)}, s32[4,192]{1,0:T(4,128)S(1)}, u32[]{:S(2)}, u32[]{:S(2)}) collective-permute-start(s32[4,192]{1,0:T(4,128)S(1)} %get-tuple-element.52), channel_id=1, source_target_pairs={{0,6},{1,7},{2,4},{3,5},{4,2},{5,3},{6,0},{7,1},{8,14},{9,15},{10,... | collective-permute-start | bytes 9224 | tf_op jit(solution)/shard_map/ppermute | solution.py:312
  12.1 0.4 collective-permute-start.4
  12.7 0.7 %widen.1.refs_4_ = f32[16384,128]{1,0:T(8,128)S(1)} custom-call(bf16[8192,256]{1,0:T(8,128)(2,1)S(1)} %copy-done), custom_call_target="tpu_custom_call" | custom-call | tf_op jit(solution)/shard_map/widen/pallas_call | solution.py:328
  13.4 0.8 %bag_lists.1 = (s32[8,192]{1,0:T(8,128)S(1)}, s32[8,192]{1,0:T(8,128)S(1)}) custom-call(s32[8,256]{1,0:T(8,128)S(1)} %bitcast.6, s32[8,256]{1,0:T(8,128)S(1)} %bitcast.10, s32[8,256]{1,0:T(8,128)S(1)} %bitcast.8, s32[8,256]{1,0:T(8,128)S(1)} %bitcast.12), custom_call_target="tpu_custom_call" | custom-call | tf_op jit(solution)/shard_map/bag_lists/pallas_call | solution.py:342
  14.3 1.4 %collective-permute-done.4.refs_1_ = s32[4,192]{1,0:T(4,128)S(1)} collective-permute-done((s32[4,192]{1,0:T(4,128)S(1)}, s32[4,192]{1,0:T(4,128)S(1)}, u32[]{:S(2)}, u32[]{:S(2)}) %collective-permute-start.4) | collective-permute-done | bytes 3104 | tf_op jit(solution)/shard_map/ppermute | solution.py:312
  15.7 0.4 collective-permute-done.5.refs_2_
  16.1 2.0 %gather.4 = (bf16[4,192,256]{2,1,0:T(8,128)(2,1)S(1)}, bf16[4,192,256]{2,1,0:T(8,128)(2,1)S(1)}) custom-call(s32[4,192]{1,0:T(4,128)S(1)} %collective-permute-done.3.refs_0_, s32[4,192]{1,0:T(4,128)S(1)} %collective-permute-done.4.refs_1_, s32[4,192]{1,0:T(4,128)S(1)} %collective-permute-done.5.refs_2_, s32[4,192]{1,0:T(4,128)S(1)} %get-tuple-element.43.refs_3_, ...), custom_call_target="tpu_custom_call" | custom-call | tf_op jit(solution)/shard_map/gather/pallas_call | solution.py:353
  18.2 0.5 collective-permute-start.6
  18.7 1.4 %gather.5.same_ref = bf16[4,192,256]{2,1,0:T(8,128)(2,1)S(1)} custom-call(s32[4,192]{1,0:T(4,128)S(1)} %collective-permute-done.3.refs_0_, s32[4,192]{1,0:T(4,128)S(1)} %collective-permute-done.4.refs_1_, s32[4,192]{1,0:T(4,128)S(1)} %collective-permute-done.5.refs_2_, s32[4,192]{1,0:T(4,128)S(1)} %get-tuple-element.43.refs_3_, f32[16384,128]{1,0:T(8,128)S(1)} %widen.1.refs_4_), custom_call_target="tpu_custom_call" | custom-call | tf_op jit(solution)/shard_map/gather/pallas_call | solution.py:353
  20.2 1.6 %collective-permute-start.8 = (bf16[2,192,256]{2,1,0:T(8,128)(2,1)S(1)}, bf16[2,192,256]{2,1,0:T(8,128)(2,1)S(1)}, u32[]{:S(2)}, u32[]{:S(2)}) collective-permute-start(bf16[2,192,256]{2,1,0:T(8,128)(2,1)S(1)} %get-tuple-element.60), channel_id=1, source_target_pairs={{0,6},{1,7},{2,4},{3,5},{4,2},{5,3},{6,0},{7,1},{8,14},{9,15},{10,... | collective-permute-start | bytes 589832 | tf_op jit(solution)/shard_map/ppermute | solution.py:312
  21.9 1.8 %collective-permute-start.10 = (bf16[2,192,256]{2,1,0:T(8,128)(2,1)S(1)}, bf16[2,192,256]{2,1,0:T(8,128)(2,1)S(1)}, u32[]{:S(2)}, u32[]{:S(2)}) collective-permute-start(bf16[2,192,256]{2,1,0:T(8,128)(2,1)S(1)} %get-tuple-element.62), channel_id=1, source_target_pairs={{0,2},{1,3},{2,0},{3,1},{4,6},{5,7},{6,4},{7,5},{8,10},{9,11},{10,... | collective-permute-start | bytes 589832 | tf_op jit(solution)/shard_map/ppermute | solution.py:312
  23.7 1.4 %gather.3.same_ref = bf16[4,192,256]{2,1,0:T(8,128)(2,1)S(1)} custom-call(s32[4,192]{1,0:T(4,128)S(1)} %collective-permute-done.3.refs_0_, s32[4,192]{1,0:T(4,128)S(1)} %collective-permute-done.4.refs_1_, s32[4,192]{1,0:T(4,128)S(1)} %collective-permute-done.5.refs_2_, s32[4,192]{1,0:T(4,128)S(1)} %get-tuple-element.43.refs_3_, f32[16384,128]{1,0:T(8,128)S(1)} %widen.1.refs_4_), custom_call_target="tpu_custom_call" | custom-call | tf_op jit(solution)/shard_map/gather/pallas_call | solution.py:353
  25.2 1.6 %collective-permute-start.12 = (bf16[2,192,256]{2,1,0:T(8,128)(2,1)S(1)}, bf16[2,192,256]{2,1,0:T(8,128)(2,1)S(1)}, u32[]{:S(2)}, u32[]{:S(2)}) collective-permute-start(bf16[2,192,256]{2,1,0:T(8,128)(2,1)S(1)} %get-tuple-element.63), channel_id=1, source_target_pairs={{0,6},{1,7},{2,4},{3,5},{4,2},{5,3},{6,0},{7,1},{8,14},{9,15},{10,... | collective-permute-start | bytes 589832 | tf_op jit(solution)/shard_map/ppermute | solution.py:312
  26.9 2.0 %collective-permute-done.8.refs_0_ = bf16[2,192,256]{2,1,0:T(8,128)(2,1)S(1)} collective-permute-done((bf16[2,192,256]{2,1,0:T(8,128)(2,1)S(1)}, bf16[2,192,256]{2,1,0:T(8,128)(2,1)S(1)}, u32[]{:S(2)}, u32[]{:S(2)}) %collective-permute-start.8) | collective-permute-done | bytes 196640 | tf_op jit(solution)/shard_map/ppermute | solution.py:312
  29.1 2.7 %collective-permute-done.9.refs_1_ = bf16[2,192,256]{2,1,0:T(8,128)(2,1)S(1)} collective-permute-done((bf16[2,192,256]{2,1,0:T(8,128)(2,1)S(1)}, bf16[2,192,256]{2,1,0:T(8,128)(2,1)S(1)}, u32[]{:S(2)}, u32[]{:S(2)}) %collective-permute-start.9) | collective-permute-done | bytes 196640 | tf_op jit(solution)/shard_map/ppermute | solution.py:312
  31.8 1.4 %collective-permute-done.10.refs_2_ = bf16[2,192,256]{2,1,0:T(8,128)(2,1)S(1)} collective-permute-done((bf16[2,192,256]{2,1,0:T(8,128)(2,1)S(1)}, bf16[2,192,256]{2,1,0:T(8,128)(2,1)S(1)}, u32[]{:S(2)}, u32[]{:S(2)}) %collective-permute-start.10) | collective-permute-done | bytes 196640 | tf_op jit(solution)/shard_map/ppermute | solution.py:312
  33.6 2.6 %collective-permute-start.11 = (bf16[256,256]{1,0:T(8,128)(2,1)S(1)}, bf16[256,256]{1,0:T(8,128)(2,1)S(1)}, u32[]{:S(2)}, u32[]{:S(2)}) collective-permute-start(bf16[256,256]{1,0:T(8,128)(2,1)S(1)} %item_sums.1), channel_id=1, source_target_pairs={{0,8},{1,9},{2,10},{3,11},{4,12},{5,13},{6,14},{7,15},{8,0},{9,1},... | collective-permute-start | bytes 393224 | tf_op jit(solution)/shard_map/ppermute | solution.py:315
  37.1 5.6 %collective-permute-done.12.refs_0_ = bf16[2,192,256]{2,1,0:T(8,128)(2,1)S(1)} collective-permute-done((bf16[2,192,256]{2,1,0:T(8,128)(2,1)S(1)}, bf16[2,192,256]{2,1,0:T(8,128)(2,1)S(1)}, u32[]{:S(2)}, u32[]{:S(2)}) %collective-permute-start.12) | collective-permute-done | bytes 196640 | tf_op jit(solution)/shard_map/ppermute | solution.py:312
  42.7 1.8 %collective-permute-done.13.refs_1_ = bf16[2,192,256]{2,1,0:T(8,128)(2,1)S(1)} collective-permute-done((bf16[2,192,256]{2,1,0:T(8,128)(2,1)S(1)}, bf16[2,192,256]{2,1,0:T(8,128)(2,1)S(1)}, u32[]{:S(2)}, u32[]{:S(2)}) %collective-permute-start.13) | collective-permute-done | bytes 196640 | tf_op jit(solution)/shard_map/ppermute | solution.py:312
  44.6 0.5 items.1
  45.1 1.7 %collective-permute-start.17 = (bf16[256,256]{1,0:T(8,128)(2,1)S(1)}, bf16[256,256]{1,0:T(8,128)(2,1)S(1)}, u32[]{:S(2)}, u32[]{:S(2)}) collective-permute-start(bf16[256,256]{1,0:T(8,128)(2,1)S(1)} %get-tuple-element.65.refs_1_.refs_2_), channel_id=1, source_target_pairs={{0,16},{16,0},{1,17},{17,1},{2,18},{18,2},{3,19},{19,3},{4,20},{20... | collective-permute-start | bytes 393224 | tf_op jit(solution)/shard_map/ppermute | solution.py:282
  47.2 1.1 %collective-permute-done.15.far_ref = bf16[256,256]{1,0:T(8,128)(2,1)S(1)} collective-permute-done((bf16[256,256]{1,0:T(8,128)(2,1)S(1)}, bf16[256,256]{1,0:T(8,128)(2,1)S(1)}, u32[]{:S(2)}, u32[]{:S(2)}) %collective-permute-start.15) | collective-permute-done | bytes 131104 | tf_op jit(solution)/shard_map/ppermute | solution.py:315
  48.2 1.8 %tower.1 = (f32[256,256]{1,0:T(8,128)S(1)}, f32[256,1]{1,0:T(8,128)S(1)}, bf16[256,256]{1,0:T(8,128)(2,1)S(1)}, f32[256,4096]{1,0:T(8,128)S(1)}) custom-call(f32[256,256]{1,0:T(8,128)S(1)} %query_sums.2.near_ref, bf16[256,256]{1,0:T(8,128)(2,1)S(1)} %collective-permute-done.15.far_ref, bf16[256,4096]{1,0:T(8,128)(2,1)S(1)} %copy-done.1, ...), custom_call_target="tpu_custom_call" | custom-call | tf_op jit(solution)/shard_map/tower/pallas_call | solution.py:413
  50.1 1.6 %collective-permute-start.16 = (bf16[256,256]{1,0:T(8,128)(2,1)S(1)}, bf16[256,256]{1,0:T(8,128)(2,1)S(1)}, u32[]{:S(2)}, u32[]{:S(2)}) collective-permute-start(bf16[256,256]{1,0:T(8,128)(2,1)S(1)} %get-tuple-element.73.refs_0_), channel_id=1, source_target_pairs={{0,16},{16,0},{1,17},{17,1},{2,18},{18,2},{3,19},{19,3},{4,20},{20... | collective-permute-start | bytes 393224 | tf_op jit(solution)/shard_map/ppermute | solution.py:282
  51.6 2.4 %query_grads.1 = (f32[1,256]{1,0:T(1,128)S(1)}, f32[256,256]{1,0:T(8,128)S(1)}, f32[256,256]{1,0:T(8,128)S(1)}) custom-call(bf16[256,256]{1,0:T(8,128)(2,1)S(1)} %get-tuple-element.73.refs_0_, bf16[256,256]{1,0:T(8,128)(2,1)S(1)} %get-tuple-element.65.refs_1_.refs_2_, bf16[256,256]{1,0:T(8,128)(2,1)S(1)} %collective-permute-done.17.refs_2_.refs_3_, ...), custom_call_target="tpu_custom_call" | custom-call | tf_op jit(solution)/shard_map/query_grads/pallas_call | solution.py:425
  54.0 1.1 %collective-permute-done.16.refs_1_ = bf16[256,256]{1,0:T(8,128)(2,1)S(1)} collective-permute-done((bf16[256,256]{1,0:T(8,128)(2,1)S(1)}, bf16[256,256]{1,0:T(8,128)(2,1)S(1)}, u32[]{:S(2)}, u32[]{:S(2)}) %collective-permute-start.16) | collective-permute-done | bytes 131104 | tf_op jit(solution)/shard_map/ppermute | solution.py:282
  55.1 1.5 %item_grads.1 = (f32[256,256]{1,0:T(8,128)}, f32[1,256]{1,0:T(1,128)}, f32[256,256]{1,0:T(8,128)}) custom-call(bf16[256,256]{1,0:T(8,128)(2,1)S(1)} %get-tuple-element.73.refs_0_, bf16[256,256]{1,0:T(8,128)(2,1)S(1)} %collective-permute-done.16.refs_1_, bf16[256,256]{1,0:T(8,128)(2,1)S(1)} %get-tuple-element.65.refs_1_.refs_2_, ...), custom_call_target="tpu_custom_call" | custom-call | tf_op jit(solution)/shard_map/item_grads/pallas_call | solution.py:437
  (27 shorter events, 3.0 us)
Async XLA Ops:
  0.6 12.1 %copy-start = (bf16[8192,256]{1,0:T(8,128)(2,1)S(1)}, bf16[8192,256]{1,0:T(8,128)(2,1)}, u32[]{:S(2)}) copy-start(bf16[8192,256]{1,0:T(8,128)(2,1)} %table_hbm.1) | copy-start | bytes 12582916
  1.5 5.7 %collective-permute-start.1 = (s32[256,8]{0,1:T(8,128)S(1)}, s32[256,8]{0,1:T(8,128)S(1)}, u32[]{:S(2)}, u32[]{:S(2)}) collective-permute-start(s32[256,8]{0,1:T(8,128)S(1)} %multiply_add_fusion), channel_id=1, source_target_pairs={{0,8},{1,9},{2,10},{3,11},{4,12},{5,13},{6,14},{7,15},{8,0},{9,1},... | collective-permute-start | bytes 24584 | tf_op jit(solution)/shard_map/ppermute | solution.py:315
  5.5 2.3 %collective-permute-start = (s32[256,8]{0,1:T(8,128)S(1)}, s32[256,8]{0,1:T(8,128)S(1)}, u32[]{:S(2)}, u32[]{:S(2)}) collective-permute-start(s32[256,8]{0,1:T(8,128)S(1)} %multiply_add_fusion), channel_id=1, source_target_pairs={{0,1},{1,0},{2,3},{3,2},{4,5},{5,4},{6,7},{7,6},{8,9},{9,8},{10,11... | collective-permute-start | bytes 24584 | tf_op jit(solution)/shard_map/ppermute | solution.py:312
  7.2 1.2 %collective-permute-start.2 = (s32[256,8]{0,1:T(8,128)S(1)}, s32[256,8]{0,1:T(8,128)S(1)}, u32[]{:S(2)}, u32[]{:S(2)}) collective-permute-start(s32[256,8]{0,1:T(8,128)S(1)} %collective-permute-done.1), channel_id=1, source_target_pairs={{0,1},{1,0},{2,3},{3,2},{4,5},{5,4},{6,7},{7,6},{8,9},{9,8},{10,11... | collective-permute-start | bytes 24584 | tf_op jit(solution)/shard_map/ppermute | solution.py:312
  9.2 5.1 %collective-permute-start.3 = (s32[4,192]{1,0:T(4,128)S(1)}, s32[4,192]{1,0:T(4,128)S(1)}, u32[]{:S(2)}, u32[]{:S(2)}) collective-permute-start(s32[4,192]{1,0:T(4,128)S(1)} %get-tuple-element.52), channel_id=1, source_target_pairs={{0,6},{1,7},{2,4},{3,5},{4,2},{5,3},{6,0},{7,1},{8,14},{9,15},{10,... | collective-permute-start | bytes 9224 | tf_op jit(solution)/shard_map/ppermute | solution.py:312
  12.1 3.6 %collective-permute-start.4 = (s32[4,192]{1,0:T(4,128)S(1)}, s32[4,192]{1,0:T(4,128)S(1)}, u32[]{:S(2)}, u32[]{:S(2)}) collective-permute-start(s32[4,192]{1,0:T(4,128)S(1)} %get-tuple-element.53), channel_id=1, source_target_pairs={{0,4},{1,5},{2,6},{3,7},{4,0},{5,1},{6,2},{7,3},{8,12},{9,13},{10,... | collective-permute-start | bytes 9224 | tf_op jit(solution)/shard_map/ppermute | solution.py:312
  12.5 3.6 %collective-permute-start.5 = (s32[4,192]{1,0:T(4,128)S(1)}, s32[4,192]{1,0:T(4,128)S(1)}, u32[]{:S(2)}, u32[]{:S(2)}) collective-permute-start(s32[4,192]{1,0:T(4,128)S(1)} %get-tuple-element.54), channel_id=1, source_target_pairs={{0,2},{1,3},{2,0},{3,1},{4,6},{5,7},{6,4},{7,5},{8,10},{9,11},{10,... | collective-permute-start | bytes 9224 | tf_op jit(solution)/shard_map/ppermute | solution.py:312
  18.1 2.0 %collective-permute-start.7 = (bf16[4,192,256]{2,1,0:T(8,128)(2,1)S(1)}, bf16[4,192,256]{2,1,0:T(8,128)(2,1)S(1)}, u32[]{:S(2)}, u32[]{:S(2)}) collective-permute-start(bf16[4,192,256]{2,1,0:T(8,128)(2,1)S(1)} %get-tuple-element.59), channel_id=1, source_target_pairs={{0,1},{1,0},{2,3},{3,2},{4,5},{5,4},{6,7},{7,6},{8,9},{9,8},{10,11... | collective-permute-start | bytes 1179656 | tf_op jit(solution)/shard_map/ppermute | solution.py:312
  18.2 7.0 %collective-permute-start.6 = (bf16[4,192,256]{2,1,0:T(8,128)(2,1)S(1)}, bf16[4,192,256]{2,1,0:T(8,128)(2,1)S(1)}, u32[]{:S(2)}, u32[]{:S(2)}) collective-permute-start(bf16[4,192,256]{2,1,0:T(8,128)(2,1)S(1)} %get-tuple-element.56), channel_id=1, source_target_pairs={{0,1},{1,0},{2,3},{3,2},{4,5},{5,4},{6,7},{7,6},{8,9},{9,8},{10,11... | collective-permute-start | bytes 1179656 | tf_op jit(solution)/shard_map/ppermute | solution.py:312
  20.2 8.8 %collective-permute-start.8 = (bf16[2,192,256]{2,1,0:T(8,128)(2,1)S(1)}, bf16[2,192,256]{2,1,0:T(8,128)(2,1)S(1)}, u32[]{:S(2)}, u32[]{:S(2)}) collective-permute-start(bf16[2,192,256]{2,1,0:T(8,128)(2,1)S(1)} %get-tuple-element.60), channel_id=1, source_target_pairs={{0,6},{1,7},{2,4},{3,5},{4,2},{5,3},{6,0},{7,1},{8,14},{9,15},{10,... | collective-permute-start | bytes 589832 | tf_op jit(solution)/shard_map/ppermute | solution.py:312
  21.7 10.1 %collective-permute-start.9 = (bf16[2,192,256]{2,1,0:T(8,128)(2,1)S(1)}, bf16[2,192,256]{2,1,0:T(8,128)(2,1)S(1)}, u32[]{:S(2)}, u32[]{:S(2)}) collective-permute-start(bf16[2,192,256]{2,1,0:T(8,128)(2,1)S(1)} %get-tuple-element.61), channel_id=1, source_target_pairs={{0,4},{1,5},{2,6},{3,7},{4,0},{5,1},{6,2},{7,3},{8,12},{9,13},{10,... | collective-permute-start | bytes 589832 | tf_op jit(solution)/shard_map/ppermute | solution.py:312
  21.9 11.3 %collective-permute-start.10 = (bf16[2,192,256]{2,1,0:T(8,128)(2,1)S(1)}, bf16[2,192,256]{2,1,0:T(8,128)(2,1)S(1)}, u32[]{:S(2)}, u32[]{:S(2)}) collective-permute-start(bf16[2,192,256]{2,1,0:T(8,128)(2,1)S(1)} %get-tuple-element.62), channel_id=1, source_target_pairs={{0,2},{1,3},{2,0},{3,1},{4,6},{5,7},{6,4},{7,5},{8,10},{9,11},{10,... | collective-permute-start | bytes 589832 | tf_op jit(solution)/shard_map/ppermute | solution.py:312
  25.1 23.1 %copy-start.1 = (bf16[256,4096]{1,0:T(8,128)(2,1)S(1)}, bf16[256,4096]{1,0:T(8,128)(2,1)}, u32[]{:S(2)}) copy-start(bf16[256,4096]{1,0:T(8,128)(2,1)} %refs_3_.1) | copy-start | bytes 6291460
  25.1 23.1 %copy-start.2 = (bf16[4096,256]{1,0:T(8,128)(2,1)S(1)}, bf16[4096,256]{1,0:T(8,128)(2,1)}, u32[]{:S(2)}) copy-start(bf16[4096,256]{1,0:T(8,128)(2,1)} %refs_4_.1) | copy-start | bytes 6291460
  25.2 17.5 %collective-permute-start.12 = (bf16[2,192,256]{2,1,0:T(8,128)(2,1)S(1)}, bf16[2,192,256]{2,1,0:T(8,128)(2,1)S(1)}, u32[]{:S(2)}, u32[]{:S(2)}) collective-permute-start(bf16[2,192,256]{2,1,0:T(8,128)(2,1)S(1)} %get-tuple-element.63), channel_id=1, source_target_pairs={{0,6},{1,7},{2,4},{3,5},{4,2},{5,3},{6,0},{7,1},{8,14},{9,15},{10,... | collective-permute-start | bytes 589832 | tf_op jit(solution)/shard_map/ppermute | solution.py:312
  26.8 17.8 %collective-permute-start.13 = (bf16[2,192,256]{2,1,0:T(8,128)(2,1)S(1)}, bf16[2,192,256]{2,1,0:T(8,128)(2,1)S(1)}, u32[]{:S(2)}, u32[]{:S(2)}) collective-permute-start(bf16[2,192,256]{2,1,0:T(8,128)(2,1)S(1)} %get-tuple-element.64), channel_id=1, source_target_pairs={{0,4},{1,5},{2,6},{3,7},{4,0},{5,1},{6,2},{7,3},{8,12},{9,13},{10,... | collective-permute-start | bytes 589832 | tf_op jit(solution)/shard_map/ppermute | solution.py:312
  28.9 15.6 %collective-permute-start.14 = (bf16[2,192,256]{2,1,0:T(8,128)(2,1)S(1)}, bf16[2,192,256]{2,1,0:T(8,128)(2,1)S(1)}, u32[]{:S(2)}, u32[]{:S(2)}) collective-permute-start(bf16[2,192,256]{2,1,0:T(8,128)(2,1)S(1)} %get-tuple-element.57), channel_id=1, source_target_pairs={{0,2},{1,3},{2,0},{3,1},{4,6},{5,7},{6,4},{7,5},{8,10},{9,11},{10,... | collective-permute-start | bytes 589832 | tf_op jit(solution)/shard_map/ppermute | solution.py:312
  33.6 10.9 %collective-permute-start.11 = (bf16[256,256]{1,0:T(8,128)(2,1)S(1)}, bf16[256,256]{1,0:T(8,128)(2,1)S(1)}, u32[]{:S(2)}, u32[]{:S(2)}) collective-permute-start(bf16[256,256]{1,0:T(8,128)(2,1)S(1)} %item_sums.1), channel_id=1, source_target_pairs={{0,8},{1,9},{2,10},{3,11},{4,12},{5,13},{6,14},{7,15},{8,0},{9,1},... | collective-permute-start | bytes 393224 | tf_op jit(solution)/shard_map/ppermute | solution.py:315
  36.7 11.5 %collective-permute-start.15 = (bf16[256,256]{1,0:T(8,128)(2,1)S(1)}, bf16[256,256]{1,0:T(8,128)(2,1)S(1)}, u32[]{:S(2)}, u32[]{:S(2)}) collective-permute-start(bf16[256,256]{1,0:T(8,128)(2,1)S(1)} %query_sums.3), channel_id=1, source_target_pairs={{0,8},{1,9},{2,10},{3,11},{4,12},{5,13},{6,14},{7,15},{8,0},{9,1},... | collective-permute-start | bytes 393224 | tf_op jit(solution)/shard_map/ppermute | solution.py:315
  45.1 6.6 %collective-permute-start.17 = (bf16[256,256]{1,0:T(8,128)(2,1)S(1)}, bf16[256,256]{1,0:T(8,128)(2,1)S(1)}, u32[]{:S(2)}, u32[]{:S(2)}) collective-permute-start(bf16[256,256]{1,0:T(8,128)(2,1)S(1)} %get-tuple-element.65.refs_1_.refs_2_), channel_id=1, source_target_pairs={{0,16},{16,0},{1,17},{17,1},{2,18},{18,2},{3,19},{19,3},{4,20},{20... | collective-permute-start | bytes 393224 | tf_op jit(solution)/shard_map/ppermute | solution.py:282
  50.1 5.0 %collective-permute-start.16 = (bf16[256,256]{1,0:T(8,128)(2,1)S(1)}, bf16[256,256]{1,0:T(8,128)(2,1)S(1)}, u32[]{:S(2)}, u32[]{:S(2)}) collective-permute-start(bf16[256,256]{1,0:T(8,128)(2,1)S(1)} %get-tuple-element.73.refs_0_), channel_id=1, source_target_pairs={{0,16},{16,0},{1,17},{17,1},{2,18},{18,2},{3,19},{19,3},{4,20},{20... | collective-permute-start | bytes 393224 | tf_op jit(solution)/shard_map/ppermute | solution.py:282

commit v6 on v5

--- a/solution.py
+++ b/solution.py
@@ -364,7 +364,7 @@
             name="gather",
         )(*wanted[::-1], wide)
 
-    order = list(range(chips - 1, 0, -1))
+    order = list(range(1, chips))
 
     def answered(same, swapped):
         messages = pl.pallas_call(
@@ -383,7 +383,7 @@
     (far_same,), (near_same,) = gather((2,)), gather((0,))
     far_rows, _ = answered(far_same, far_other)
     near_rows, near_messages = answered(near_same, near_other)
-    far_bags, _ = lax.optimization_barrier((far_bags, near_messages[-1]))
+    far_bags, _ = lax.optimization_barrier((far_bags, near_messages[0]))
 
     def sums(kind, bags, rows, dtype):
         return pl.pallas_call(

time: 56.8 us -> 57.7 us (1.016)
  starting transfers between devices: 19.9 us -> 20.7 us
    ppermute x13, starting transfers between devices: 9.56 us -> 11.2 us  [to_chip(): return lax.ppermute(values, 'table', route)]
    ppermute x3, waiting for transfers between devices: 2.7 us -> 1.63 us  [to_mirror(): lax.ppermute(values, 'table', [(t, (t + half) % shards) for t in range(sh...]
    ppermute x2, starting transfers between devices: 3.2 us -> 2.35 us  [rotated(): lax.ppermute(shard, axis, [(i, (i + by) % count) for i in range(count)])]
    ppermute x2, waiting for transfers between devices: 1.08 us -> 1.85 us  [rotated(): lax.ppermute(shard, axis, [(i, (i + by) % count) for i in range(count)])]
  transfers between devices with their start and end apart: 18 -> 18, of which waited for: 11 -> 9; matrix products, arithmetic and copies ran while one was open for 0% -> 0% of each run, Pallas kernels for 20% -> 19%
where the time goes in v6:
time: 57.7 us; the launch traced here: 57.5 us
  starting transfers between devices  20.7 us (36%)
  waiting for transfers between devices  19.7 us (34%)
  Pallas kernels  15.3 us (27%)
  other arithmetic  0.87 us (2%)
  between operations  0.83 us (1%)
    ppermute x13, waiting for transfers between devices, to_chip(): return lax.ppermute(values, 'table', route)  16.2 us
    ppermute x13, starting transfers between devices, to_chip(): return lax.ppermute(values, 'table', route)  11.2 us
    ppermute x3, starting transfers between devices, to_mirror(): lax.ppermute(values, 'table', [(t, (t + half) % shards) for t in range(sh...  7.09 us
    pallas_call x3, Pallas kernels, gather(): pl.pallas_call(functools.partial(gather_kernel, chips, askers), in_specs=...  4.74 us
    pallas_call x1, Pallas kernels, local(): pl.pallas_call(functools.partial(query_grad_kernel, blocks), out_shape=[s...  2.39 us
    ppermute x2, starting transfers between devices, rotated(): lax.ppermute(shard, axis, [(i, (i + by) % count) for i in range(count)])  2.35 us
    ppermute x2, waiting for transfers between devices, rotated(): lax.ppermute(shard, axis, [(i, (i + by) % count) for i in range(count)])  1.85 us
    pallas_call x1, Pallas kernels, local(): pl.pallas_call(tower_kernel, out_shape=[struct((pairs, width), f32), stru...  1.85 us
  transfers between devices with their start and end apart: 18, of which 9 were waited for; matrix products, arithmetic and copies ran while one was open for 0% of the time, Pallas kernels for 19%

profile of v6, /device:TPU:0, one launch (start us, length us, event | category | flops | bytes accessed | tf_op | source)
XLA Modules:
  0.0 57.5 jit_solution(5525669545926910287)
XLA Ops:
  0.6 0.9 %multiply_add_fusion = s32[256,8]{0,1:T(8,128)S(1)} fusion(s32[256,8]{0,1:T(8,128)} %param.9, s32[256,8]{0,1:T(8,128)} %param.8), kind=kLoop, calls=%fused_computation | loop fusion | flops 4096 | bytes 24576 | tf_op jit(solution)/shard_map/add | solution.py:317
  1.5 4.0 %collective-permute-start.1 = (s32[256,8]{0,1:T(8,128)S(1)}, s32[256,8]{0,1:T(8,128)S(1)}, u32[]{:S(2)}, u32[]{:S(2)}) collective-permute-start(s32[256,8]{0,1:T(8,128)S(1)} %multiply_add_fusion), channel_id=1, source_target_pairs={{0,8},{1,9},{2,10},{3,11},{4,12},{5,13},{6,14},{7,15},{8,0},{9,1},... | collective-permute-start | bytes 24584 | tf_op jit(solution)/shard_map/ppermute | solution.py:315
  5.6 1.6 %collective-permute-done.1 = s32[256,8]{0,1:T(8,128)S(1)} collective-permute-done((s32[256,8]{0,1:T(8,128)S(1)}, s32[256,8]{0,1:T(8,128)S(1)}, u32[]{:S(2)}, u32[]{:S(2)}) %collective-permute-start.1) | collective-permute-done | bytes 8224 | tf_op jit(solution)/shard_map/ppermute | solution.py:315
  7.2 0.7 %touch.1.refs_4_ = f32[16,256]{1,0:T(8,128)S(1)} custom-call(bf16[8192,256]{1,0:T(8,128)(2,1)} %table_hbm.1), custom_call_target="tpu_custom_call" | custom-call | tf_op jit(solution)/shard_map/touch/pallas_call | solution.py:320
  7.9 0.4 collective-permute-done.2
  8.3 0.8 %route.1 = (s32[4,192]{1,0:T(4,128)S(1)}, s32[4,192]{1,0:T(4,128)S(1)}, s32[4,192]{1,0:T(4,128)S(1)}, s32[4,192]{1,0:T(4,128)S(1)}) custom-call(s32[8,256]{1,0:T(8,128)S(1)} %bitcast.5, s32[8,256]{1,0:T(8,128)S(1)} %bitcast.9, s32[8,256]{1,0:T(8,128)S(1)} %bitcast.7, s32[8,256]{1,0:T(8,128)S(1)} %bitcast.11, f32[16,256]{1,0:T(8,128)S(1)} %touch.1.refs_4_), custom_call_target="tpu_custom_call" | custom-call | tf_op jit(solution)/shard_map/route/pallas_call | solution.py:335
  9.2 2.9 %collective-permute-start.3 = (s32[4,192]{1,0:T(4,128)S(1)}, s32[4,192]{1,0:T(4,128)S(1)}, u32[]{:S(2)}, u32[]{:S(2)}) collective-permute-start(s32[4,192]{1,0:T(4,128)S(1)} %get-tuple-element.52), channel_id=1, source_target_pairs={{0,6},{1,7},{2,4},{3,5},{4,2},{5,3},{6,0},{7,1},{8,14},{9,15},{10,... | collective-permute-start | bytes 9224 | tf_op jit(solution)/shard_map/ppermute | solution.py:312
  12.1 0.4 collective-permute-start.4
  12.7 0.7 %widen.1.refs_4_ = f32[16384,128]{1,0:T(8,128)S(1)} custom-call(bf16[8192,256]{1,0:T(8,128)(2,1)S(1)} %copy-done), custom_call_target="tpu_custom_call" | custom-call | tf_op jit(solution)/shard_map/widen/pallas_call | solution.py:328
  13.4 0.8 %bag_lists.1 = (s32[8,192]{1,0:T(8,128)S(1)}, s32[8,192]{1,0:T(8,128)S(1)}) custom-call(s32[8,256]{1,0:T(8,128)S(1)} %bitcast.6, s32[8,256]{1,0:T(8,128)S(1)} %bitcast.10, s32[8,256]{1,0:T(8,128)S(1)} %bitcast.8, s32[8,256]{1,0:T(8,128)S(1)} %bitcast.12), custom_call_target="tpu_custom_call" | custom-call | tf_op jit(solution)/shard_map/bag_lists/pallas_call | solution.py:342
  14.3 1.4 %collective-permute-done.4.refs_1_ = s32[4,192]{1,0:T(4,128)S(1)} collective-permute-done((s32[4,192]{1,0:T(4,128)S(1)}, s32[4,192]{1,0:T(4,128)S(1)}, u32[]{:S(2)}, u32[]{:S(2)}) %collective-permute-start.4) | collective-permute-done | bytes 3104 | tf_op jit(solution)/shard_map/ppermute | solution.py:312
  15.7 0.4 collective-permute-done.5.refs_2_
  16.1 1.9 %gather.4 = (bf16[4,192,256]{2,1,0:T(8,128)(2,1)S(1)}, bf16[4,192,256]{2,1,0:T(8,128)(2,1)S(1)}) custom-call(s32[4,192]{1,0:T(4,128)S(1)} %collective-permute-done.3.refs_0_, s32[4,192]{1,0:T(4,128)S(1)} %collective-permute-done.4.refs_1_, s32[4,192]{1,0:T(4,128)S(1)} %collective-permute-done.5.refs_2_, s32[4,192]{1,0:T(4,128)S(1)} %get-tuple-element.43.refs_3_, ...), custom_call_target="tpu_custom_call" | custom-call | tf_op jit(solution)/shard_map/gather/pallas_call | solution.py:353
  18.2 0.5 collective-permute-start.6
  18.7 1.4 %gather.5.same_ref = bf16[4,192,256]{2,1,0:T(8,128)(2,1)S(1)} custom-call(s32[4,192]{1,0:T(4,128)S(1)} %collective-permute-done.3.refs_0_, s32[4,192]{1,0:T(4,128)S(1)} %collective-permute-done.4.refs_1_, s32[4,192]{1,0:T(4,128)S(1)} %collective-permute-done.5.refs_2_, s32[4,192]{1,0:T(4,128)S(1)} %get-tuple-element.43.refs_3_, f32[16384,128]{1,0:T(8,128)S(1)} %widen.1.refs_4_), custom_call_target="tpu_custom_call" | custom-call | tf_op jit(solution)/shard_map/gather/pallas_call | solution.py:353
  20.4 1.9 %collective-permute-start.9 = (bf16[2,192,256]{2,1,0:T(8,128)(2,1)S(1)}, bf16[2,192,256]{2,1,0:T(8,128)(2,1)S(1)}, u32[]{:S(2)}, u32[]{:S(2)}) collective-permute-start(bf16[2,192,256]{2,1,0:T(8,128)(2,1)S(1)} %get-tuple-element.61), channel_id=1, source_target_pairs={{0,4},{1,5},{2,6},{3,7},{4,0},{5,1},{6,2},{7,3},{8,12},{9,13},{10,... | collective-permute-start | bytes 589832 | tf_op jit(solution)/shard_map/ppermute | solution.py:312
  22.3 1.4 %collective-permute-start.10 = (bf16[2,192,256]{2,1,0:T(8,128)(2,1)S(1)}, bf16[2,192,256]{2,1,0:T(8,128)(2,1)S(1)}, u32[]{:S(2)}, u32[]{:S(2)}) collective-permute-start(bf16[2,192,256]{2,1,0:T(8,128)(2,1)S(1)} %get-tuple-element.62), channel_id=1, source_target_pairs={{0,6},{1,7},{2,4},{3,5},{4,2},{5,3},{6,0},{7,1},{8,14},{9,15},{10,... | collective-permute-start | bytes 589832 | tf_op jit(solution)/shard_map/ppermute | solution.py:312
  23.7 1.4 %gather.3.same_ref = bf16[4,192,256]{2,1,0:T(8,128)(2,1)S(1)} custom-call(s32[4,192]{1,0:T(4,128)S(1)} %collective-permute-done.3.refs_0_, s32[4,192]{1,0:T(4,128)S(1)} %collective-permute-done.4.refs_1_, s32[4,192]{1,0:T(4,128)S(1)} %collective-permute-done.5.refs_2_, s32[4,192]{1,0:T(4,128)S(1)} %get-tuple-element.43.refs_3_, f32[16384,128]{1,0:T(8,128)S(1)} %widen.1.refs_4_), custom_call_target="tpu_custom_call" | custom-call | tf_op jit(solution)/shard_map/gather/pallas_call | solution.py:353
  25.5 1.9 %collective-permute-start.13 = (bf16[2,192,256]{2,1,0:T(8,128)(2,1)S(1)}, bf16[2,192,256]{2,1,0:T(8,128)(2,1)S(1)}, u32[]{:S(2)}, u32[]{:S(2)}) collective-permute-start(bf16[2,192,256]{2,1,0:T(8,128)(2,1)S(1)} %get-tuple-element.64), channel_id=1, source_target_pairs={{0,4},{1,5},{2,6},{3,7},{4,0},{5,1},{6,2},{7,3},{8,12},{9,13},{10,... | collective-permute-start | bytes 589832 | tf_op jit(solution)/shard_map/ppermute | solution.py:312
  27.3 1.4 %collective-permute-start.14 = (bf16[2,192,256]{2,1,0:T(8,128)(2,1)S(1)}, bf16[2,192,256]{2,1,0:T(8,128)(2,1)S(1)}, u32[]{:S(2)}, u32[]{:S(2)}) collective-permute-start(bf16[2,192,256]{2,1,0:T(8,128)(2,1)S(1)} %get-tuple-element.57), channel_id=1, source_target_pairs={{0,6},{1,7},{2,4},{3,5},{4,2},{5,3},{6,0},{7,1},{8,14},{9,15},{10,... | collective-permute-start | bytes 589832 | tf_op jit(solution)/shard_map/ppermute | solution.py:312
  28.7 5.0 %collective-permute-done.10.refs_2_ = bf16[2,192,256]{2,1,0:T(8,128)(2,1)S(1)} collective-permute-done((bf16[2,192,256]{2,1,0:T(8,128)(2,1)S(1)}, bf16[2,192,256]{2,1,0:T(8,128)(2,1)S(1)}, u32[]{:S(2)}, u32[]{:S(2)}) %collective-permute-start.10) | collective-permute-done | bytes 196640 | tf_op jit(solution)/shard_map/ppermute | solution.py:312
  33.7 0.4 item_sums.1
  34.2 2.7 %collective-permute-start.11 = (bf16[256,256]{1,0:T(8,128)(2,1)S(1)}, bf16[256,256]{1,0:T(8,128)(2,1)S(1)}, u32[]{:S(2)}, u32[]{:S(2)}) collective-permute-start(bf16[256,256]{1,0:T(8,128)(2,1)S(1)} %item_sums.1), channel_id=1, source_target_pairs={{0,8},{1,9},{2,10},{3,11},{4,12},{5,13},{6,14},{7,15},{8,0},{9,1},... | collective-permute-start | bytes 393224 | tf_op jit(solution)/shard_map/ppermute | solution.py:315
  38.1 8.5 %collective-permute-done.14.refs_2_ = bf16[2,192,256]{2,1,0:T(8,128)(2,1)S(1)} collective-permute-done((bf16[2,192,256]{2,1,0:T(8,128)(2,1)S(1)}, bf16[2,192,256]{2,1,0:T(8,128)(2,1)S(1)}, u32[]{:S(2)}, u32[]{:S(2)}) %collective-permute-start.14) | collective-permute-done | bytes 196640 | tf_op jit(solution)/shard_map/ppermute | solution.py:312
  46.5 0.5 items.1
  47.1 1.6 %collective-permute-start.17 = (bf16[256,256]{1,0:T(8,128)(2,1)S(1)}, bf16[256,256]{1,0:T(8,128)(2,1)S(1)}, u32[]{:S(2)}, u32[]{:S(2)}) collective-permute-start(bf16[256,256]{1,0:T(8,128)(2,1)S(1)} %get-tuple-element.65.refs_1_.refs_2_), channel_id=1, source_target_pairs={{0,16},{16,0},{1,17},{17,1},{2,18},{18,2},{3,19},{19,3},{4,20},{20... | collective-permute-start | bytes 393224 | tf_op jit(solution)/shard_map/ppermute | solution.py:282
  48.6 0.4 query_sums.2.near_ref
  49.1 1.8 %tower.1 = (f32[256,256]{1,0:T(8,128)S(1)}, f32[256,1]{1,0:T(8,128)S(1)}, bf16[256,256]{1,0:T(8,128)(2,1)S(1)}, f32[256,4096]{1,0:T(8,128)S(1)}) custom-call(f32[256,256]{1,0:T(8,128)S(1)} %query_sums.2.near_ref, bf16[256,256]{1,0:T(8,128)(2,1)S(1)} %collective-permute-done.15.far_ref, bf16[256,4096]{1,0:T(8,128)(2,1)S(1)} %copy-done.1, ...), custom_call_target="tpu_custom_call" | custom-call | tf_op jit(solution)/shard_map/tower/pallas_call | solution.py:413
  50.9 0.8 %collective-permute-start.16 = (bf16[256,256]{1,0:T(8,128)(2,1)S(1)}, bf16[256,256]{1,0:T(8,128)(2,1)S(1)}, u32[]{:S(2)}, u32[]{:S(2)}) collective-permute-start(bf16[256,256]{1,0:T(8,128)(2,1)S(1)} %get-tuple-element.73.refs_0_), channel_id=1, source_target_pairs={{0,16},{16,0},{1,17},{17,1},{2,18},{18,2},{3,19},{19,3},{4,20},{20... | collective-permute-start | bytes 393224 | tf_op jit(solution)/shard_map/ppermute | solution.py:282
  52.1 2.4 %query_grads.1 = (f32[1,256]{1,0:T(1,128)S(1)}, f32[256,256]{1,0:T(8,128)S(1)}, f32[256,256]{1,0:T(8,128)S(1)}) custom-call(bf16[256,256]{1,0:T(8,128)(2,1)S(1)} %get-tuple-element.73.refs_0_, bf16[256,256]{1,0:T(8,128)(2,1)S(1)} %get-tuple-element.65.refs_1_.refs_2_, bf16[256,256]{1,0:T(8,128)(2,1)S(1)} %collective-permute-done.17.refs_2_.refs_3_, ...), custom_call_target="tpu_custom_call" | custom-call | tf_op jit(solution)/shard_map/query_grads/pallas_call | solution.py:425
  54.5 1.5 %collective-permute-done.16.refs_1_ = bf16[256,256]{1,0:T(8,128)(2,1)S(1)} collective-permute-done((bf16[256,256]{1,0:T(8,128)(2,1)S(1)}, bf16[256,256]{1,0:T(8,128)(2,1)S(1)}, u32[]{:S(2)}, u32[]{:S(2)}) %collective-permute-start.16) | collective-permute-done | bytes 131104 | tf_op jit(solution)/shard_map/ppermute | solution.py:282
  56.0 1.5 %item_grads.1 = (f32[256,256]{1,0:T(8,128)}, f32[1,256]{1,0:T(1,128)}, f32[256,256]{1,0:T(8,128)}) custom-call(bf16[256,256]{1,0:T(8,128)(2,1)S(1)} %get-tuple-element.73.refs_0_, bf16[256,256]{1,0:T(8,128)(2,1)S(1)} %collective-permute-done.16.refs_1_, bf16[256,256]{1,0:T(8,128)(2,1)S(1)} %get-tuple-element.65.refs_1_.refs_2_, ...), custom_call_target="tpu_custom_call" | custom-call | tf_op jit(solution)/shard_map/item_grads/pallas_call | solution.py:437
  (27 shorter events, 2.5 us)
Async XLA Ops:
  0.6 12.1 %copy-start = (bf16[8192,256]{1,0:T(8,128)(2,1)S(1)}, bf16[8192,256]{1,0:T(8,128)(2,1)}, u32[]{:S(2)}) copy-start(bf16[8192,256]{1,0:T(8,128)(2,1)} %table_hbm.1) | copy-start | bytes 12582916
  1.5 5.7 %collective-permute-start.1 = (s32[256,8]{0,1:T(8,128)S(1)}, s32[256,8]{0,1:T(8,128)S(1)}, u32[]{:S(2)}, u32[]{:S(2)}) collective-permute-start(s32[256,8]{0,1:T(8,128)S(1)} %multiply_add_fusion), channel_id=1, source_target_pairs={{0,8},{1,9},{2,10},{3,11},{4,12},{5,13},{6,14},{7,15},{8,0},{9,1},... | collective-permute-start | bytes 24584 | tf_op jit(solution)/shard_map/ppermute | solution.py:315
  5.5 2.3 %collective-permute-start = (s32[256,8]{0,1:T(8,128)S(1)}, s32[256,8]{0,1:T(8,128)S(1)}, u32[]{:S(2)}, u32[]{:S(2)}) collective-permute-start(s32[256,8]{0,1:T(8,128)S(1)} %multiply_add_fusion), channel_id=1, source_target_pairs={{0,1},{1,0},{2,3},{3,2},{4,5},{5,4},{6,7},{7,6},{8,9},{9,8},{10,11... | collective-permute-start | bytes 24584 | tf_op jit(solution)/shard_map/ppermute | solution.py:312
  7.2 1.2 %collective-permute-start.2 = (s32[256,8]{0,1:T(8,128)S(1)}, s32[256,8]{0,1:T(8,128)S(1)}, u32[]{:S(2)}, u32[]{:S(2)}) collective-permute-start(s32[256,8]{0,1:T(8,128)S(1)} %collective-permute-done.1), channel_id=1, source_target_pairs={{0,1},{1,0},{2,3},{3,2},{4,5},{5,4},{6,7},{7,6},{8,9},{9,8},{10,11... | collective-permute-start | bytes 24584 | tf_op jit(solution)/shard_map/ppermute | solution.py:312
  9.2 5.1 %collective-permute-start.3 = (s32[4,192]{1,0:T(4,128)S(1)}, s32[4,192]{1,0:T(4,128)S(1)}, u32[]{:S(2)}, u32[]{:S(2)}) collective-permute-start(s32[4,192]{1,0:T(4,128)S(1)} %get-tuple-element.52), channel_id=1, source_target_pairs={{0,6},{1,7},{2,4},{3,5},{4,2},{5,3},{6,0},{7,1},{8,14},{9,15},{10,... | collective-permute-start | bytes 9224 | tf_op jit(solution)/shard_map/ppermute | solution.py:312
  12.1 3.6 %collective-permute-start.4 = (s32[4,192]{1,0:T(4,128)S(1)}, s32[4,192]{1,0:T(4,128)S(1)}, u32[]{:S(2)}, u32[]{:S(2)}) collective-permute-start(s32[4,192]{1,0:T(4,128)S(1)} %get-tuple-element.53), channel_id=1, source_target_pairs={{0,4},{1,5},{2,6},{3,7},{4,0},{5,1},{6,2},{7,3},{8,12},{9,13},{10,... | collective-permute-start | bytes 9224 | tf_op jit(solution)/shard_map/ppermute | solution.py:312
  12.5 3.6 %collective-permute-start.5 = (s32[4,192]{1,0:T(4,128)S(1)}, s32[4,192]{1,0:T(4,128)S(1)}, u32[]{:S(2)}, u32[]{:S(2)}) collective-permute-start(s32[4,192]{1,0:T(4,128)S(1)} %get-tuple-element.54), channel_id=1, source_target_pairs={{0,2},{1,3},{2,0},{3,1},{4,6},{5,7},{6,4},{7,5},{8,10},{9,11},{10,... | collective-permute-start | bytes 9224 | tf_op jit(solution)/shard_map/ppermute | solution.py:312
  18.1 2.0 %collective-permute-start.7 = (bf16[4,192,256]{2,1,0:T(8,128)(2,1)S(1)}, bf16[4,192,256]{2,1,0:T(8,128)(2,1)S(1)}, u32[]{:S(2)}, u32[]{:S(2)}) collective-permute-start(bf16[4,192,256]{2,1,0:T(8,128)(2,1)S(1)} %get-tuple-element.59), channel_id=1, source_target_pairs={{0,1},{1,0},{2,3},{3,2},{4,5},{5,4},{6,7},{7,6},{8,9},{9,8},{10,11... | collective-permute-start | bytes 1179656 | tf_op jit(solution)/shard_map/ppermute | solution.py:312
  18.2 6.9 %collective-permute-start.6 = (bf16[4,192,256]{2,1,0:T(8,128)(2,1)S(1)}, bf16[4,192,256]{2,1,0:T(8,128)(2,1)S(1)}, u32[]{:S(2)}, u32[]{:S(2)}) collective-permute-start(bf16[4,192,256]{2,1,0:T(8,128)(2,1)S(1)} %get-tuple-element.56), channel_id=1, source_target_pairs={{0,1},{1,0},{2,3},{3,2},{4,5},{5,4},{6,7},{7,6},{8,9},{9,8},{10,11... | collective-permute-start | bytes 1179656 | tf_op jit(solution)/shard_map/ppermute | solution.py:312
  20.1 7.2 %collective-permute-start.8 = (bf16[2,192,256]{2,1,0:T(8,128)(2,1)S(1)}, bf16[2,192,256]{2,1,0:T(8,128)(2,1)S(1)}, u32[]{:S(2)}, u32[]{:S(2)}) collective-permute-start(bf16[2,192,256]{2,1,0:T(8,128)(2,1)S(1)} %get-tuple-element.60), channel_id=1, source_target_pairs={{0,2},{1,3},{2,0},{3,1},{4,6},{5,7},{6,4},{7,5},{8,10},{9,11},{10,... | collective-permute-start | bytes 589832 | tf_op jit(solution)/shard_map/ppermute | solution.py:312
  20.4 8.3 %collective-permute-start.9 = (bf16[2,192,256]{2,1,0:T(8,128)(2,1)S(1)}, bf16[2,192,256]{2,1,0:T(8,128)(2,1)S(1)}, u32[]{:S(2)}, u32[]{:S(2)}) collective-permute-start(bf16[2,192,256]{2,1,0:T(8,128)(2,1)S(1)} %get-tuple-element.61), channel_id=1, source_target_pairs={{0,4},{1,5},{2,6},{3,7},{4,0},{5,1},{6,2},{7,3},{8,12},{9,13},{10,... | collective-permute-start | bytes 589832 | tf_op jit(solution)/shard_map/ppermute | solution.py:312
  22.3 11.4 %collective-permute-start.10 = (bf16[2,192,256]{2,1,0:T(8,128)(2,1)S(1)}, bf16[2,192,256]{2,1,0:T(8,128)(2,1)S(1)}, u32[]{:S(2)}, u32[]{:S(2)}) collective-permute-start(bf16[2,192,256]{2,1,0:T(8,128)(2,1)S(1)} %get-tuple-element.62), channel_id=1, source_target_pairs={{0,6},{1,7},{2,4},{3,5},{4,2},{5,3},{6,0},{7,1},{8,14},{9,15},{10,... | collective-permute-start | bytes 589832 | tf_op jit(solution)/shard_map/ppermute | solution.py:312
  25.1 24.0 %copy-start.1 = (bf16[256,4096]{1,0:T(8,128)(2,1)S(1)}, bf16[256,4096]{1,0:T(8,128)(2,1)}, u32[]{:S(2)}) copy-start(bf16[256,4096]{1,0:T(8,128)(2,1)} %refs_3_.1) | copy-start | bytes 6291460
  25.1 24.0 %copy-start.2 = (bf16[4096,256]{1,0:T(8,128)(2,1)S(1)}, bf16[4096,256]{1,0:T(8,128)(2,1)}, u32[]{:S(2)}) copy-start(bf16[4096,256]{1,0:T(8,128)(2,1)} %refs_4_.1) | copy-start | bytes 6291460
  25.2 12.5 %collective-permute-start.12 = (bf16[2,192,256]{2,1,0:T(8,128)(2,1)S(1)}, bf16[2,192,256]{2,1,0:T(8,128)(2,1)S(1)}, u32[]{:S(2)}, u32[]{:S(2)}) collective-permute-start(bf16[2,192,256]{2,1,0:T(8,128)(2,1)S(1)} %get-tuple-element.63), channel_id=1, source_target_pairs={{0,2},{1,3},{2,0},{3,1},{4,6},{5,7},{6,4},{7,5},{8,10},{9,11},{10,... | collective-permute-start | bytes 589832 | tf_op jit(solution)/shard_map/ppermute | solution.py:312
  25.5 12.6 %collective-permute-start.13 = (bf16[2,192,256]{2,1,0:T(8,128)(2,1)S(1)}, bf16[2,192,256]{2,1,0:T(8,128)(2,1)S(1)}, u32[]{:S(2)}, u32[]{:S(2)}) collective-permute-start(bf16[2,192,256]{2,1,0:T(8,128)(2,1)S(1)} %get-tuple-element.64), channel_id=1, source_target_pairs={{0,4},{1,5},{2,6},{3,7},{4,0},{5,1},{6,2},{7,3},{8,12},{9,13},{10,... | collective-permute-start | bytes 589832 | tf_op jit(solution)/shard_map/ppermute | solution.py:312
  27.3 19.2 %collective-permute-start.14 = (bf16[2,192,256]{2,1,0:T(8,128)(2,1)S(1)}, bf16[2,192,256]{2,1,0:T(8,128)(2,1)S(1)}, u32[]{:S(2)}, u32[]{:S(2)}) collective-permute-start(bf16[2,192,256]{2,1,0:T(8,128)(2,1)S(1)} %get-tuple-element.57), channel_id=1, source_target_pairs={{0,6},{1,7},{2,4},{3,5},{4,2},{5,3},{6,0},{7,1},{8,14},{9,15},{10,... | collective-permute-start | bytes 589832 | tf_op jit(solution)/shard_map/ppermute | solution.py:312
  34.2 12.4 %collective-permute-start.11 = (bf16[256,256]{1,0:T(8,128)(2,1)S(1)}, bf16[256,256]{1,0:T(8,128)(2,1)S(1)}, u32[]{:S(2)}, u32[]{:S(2)}) collective-permute-start(bf16[256,256]{1,0:T(8,128)(2,1)S(1)} %item_sums.1), channel_id=1, source_target_pairs={{0,8},{1,9},{2,10},{3,11},{4,12},{5,13},{6,14},{7,15},{8,0},{9,1},... | collective-permute-start | bytes 393224 | tf_op jit(solution)/shard_map/ppermute | solution.py:315
  37.2 11.8 %collective-permute-start.15 = (bf16[256,256]{1,0:T(8,128)(2,1)S(1)}, bf16[256,256]{1,0:T(8,128)(2,1)S(1)}, u32[]{:S(2)}, u32[]{:S(2)}) collective-permute-start(bf16[256,256]{1,0:T(8,128)(2,1)S(1)} %query_sums.3), channel_id=1, source_target_pairs={{0,8},{1,9},{2,10},{3,11},{4,12},{5,13},{6,14},{7,15},{8,0},{9,1},... | collective-permute-start | bytes 393224 | tf_op jit(solution)/shard_map/ppermute | solution.py:315
  47.1 5.0 %collective-permute-start.17 = (bf16[256,256]{1,0:T(8,128)(2,1)S(1)}, bf16[256,256]{1,0:T(8,128)(2,1)S(1)}, u32[]{:S(2)}, u32[]{:S(2)}) collective-permute-start(bf16[256,256]{1,0:T(8,128)(2,1)S(1)} %get-tuple-element.65.refs_1_.refs_2_), channel_id=1, source_target_pairs={{0,16},{16,0},{1,17},{17,1},{2,18},{18,2},{3,19},{19,3},{4,20},{20... | collective-permute-start | bytes 393224 | tf_op jit(solution)/shard_map/ppermute | solution.py:282
  50.9 5.0 %collective-permute-start.16 = (bf16[256,256]{1,0:T(8,128)(2,1)S(1)}, bf16[256,256]{1,0:T(8,128)(2,1)S(1)}, u32[]{:S(2)}, u32[]{:S(2)}) collective-permute-start(bf16[256,256]{1,0:T(8,128)(2,1)S(1)} %get-tuple-element.73.refs_0_), channel_id=1, source_target_pairs={{0,16},{16,0},{1,17},{17,1},{2,18},{18,2},{3,19},{19,3},{4,20},{20... | collective-permute-start | bytes 393224 | tf_op jit(solution)/shard_map/ppermute | solution.py:282

commit v7 on v6

--- a/solution.py
+++ b/solution.py
@@ -382,6 +382,7 @@
     far_other, near_other = [to_chip(rows, 0, 1) for rows in gather((3, 1))]
     (far_same,), (near_same,) = gather((2,)), gather((0,))
     far_rows, _ = answered(far_same, far_other)
+    near_same, near_other, _ = lax.optimization_barrier((near_same, near_other, far_rows[2]))
     near_rows, near_messages = answered(near_same, near_other)
     far_bags, _ = lax.optimization_barrier((far_bags, near_messages[0]))
 

time: 57.7 us -> 57.7 us (level)
    ppermute x3, waiting for transfers between devices: 1.63 us -> 7.13 us  [to_mirror(): lax.ppermute(values, 'table', [(t, (t + half) % shards) for t in range(sh...]
    ppermute x13, waiting for transfers between devices: 16.2 us -> 10.7 us  [to_chip(): return lax.ppermute(values, 'table', route)]
  transfers between devices with their start and end apart: 18 -> 18, of which waited for: 9 -> 10; matrix products, arithmetic and copies ran while one was open for 0% -> 0% of each run, Pallas kernels for 19% -> 19%
where the time goes in v7:
time: 57.7 us; the launch traced here: 57.4 us
  starting transfers between devices  20.7 us (36%)
  waiting for transfers between devices  19.7 us (34%)
  Pallas kernels  15.3 us (27%)
  other arithmetic  0.87 us (2%)
  between operations  0.83 us (1%)
    ppermute x13, starting transfers between devices, to_chip(): return lax.ppermute(values, 'table', route)  11.2 us
    ppermute x13, waiting for transfers between devices, to_chip(): return lax.ppermute(values, 'table', route)  10.7 us
    ppermute x3, waiting for transfers between devices, to_mirror(): lax.ppermute(values, 'table', [(t, (t + half) % shards) for t in range(sh...  7.13 us
    ppermute x3, starting transfers between devices, to_mirror(): lax.ppermute(values, 'table', [(t, (t + half) % shards) for t in range(sh...  7.09 us
    pallas_call x3, Pallas kernels, gather(): pl.pallas_call(functools.partial(gather_kernel, chips, askers), in_specs=...  4.73 us
    pallas_call x1, Pallas kernels, local(): pl.pallas_call(functools.partial(query_grad_kernel, blocks), out_shape=[s...  2.39 us
    ppermute x2, starting transfers between devices, rotated(): lax.ppermute(shard, axis, [(i, (i + by) % count) for i in range(count)])  2.36 us
    pallas_call x1, Pallas kernels, local(): pl.pallas_call(tower_kernel, out_shape=[struct((pairs, width), f32), stru...  1.85 us
  transfers between devices with their start and end apart: 18, of which 10 were waited for; matrix products, arithmetic and copies ran while one was open for 0% of the time, Pallas kernels for 19%

profile of v7, /device:TPU:0, one launch (start us, length us, event | category | flops | bytes accessed | tf_op | source)
XLA Modules:
  0.0 57.4 jit_solution(8359941242305864213)
XLA Ops:
  0.6 0.9 %multiply_add_fusion = s32[256,8]{0,1:T(8,128)S(1)} fusion(s32[256,8]{0,1:T(8,128)} %param.9, s32[256,8]{0,1:T(8,128)} %param.8), kind=kLoop, calls=%fused_computation | loop fusion | flops 4096 | bytes 24576 | tf_op jit(solution)/shard_map/add | solution.py:317
  1.5 4.0 %collective-permute-start.1 = (s32[256,8]{0,1:T(8,128)S(1)}, s32[256,8]{0,1:T(8,128)S(1)}, u32[]{:S(2)}, u32[]{:S(2)}) collective-permute-start(s32[256,8]{0,1:T(8,128)S(1)} %multiply_add_fusion), channel_id=1, source_target_pairs={{0,8},{1,9},{2,10},{3,11},{4,12},{5,13},{6,14},{7,15},{8,0},{9,1},... | collective-permute-start | bytes 24584 | tf_op jit(solution)/shard_map/ppermute | solution.py:315
  5.6 1.6 %collective-permute-done.1 = s32[256,8]{0,1:T(8,128)S(1)} collective-permute-done((s32[256,8]{0,1:T(8,128)S(1)}, s32[256,8]{0,1:T(8,128)S(1)}, u32[]{:S(2)}, u32[]{:S(2)}) %collective-permute-start.1) | collective-permute-done | bytes 8224 | tf_op jit(solution)/shard_map/ppermute | solution.py:315
  7.2 0.7 %touch.1.refs_4_ = f32[16,256]{1,0:T(8,128)S(1)} custom-call(bf16[8192,256]{1,0:T(8,128)(2,1)} %table_hbm.1), custom_call_target="tpu_custom_call" | custom-call | tf_op jit(solution)/shard_map/touch/pallas_call | solution.py:320
  7.9 0.4 collective-permute-done.2
  8.3 0.8 %route.1 = (s32[4,192]{1,0:T(4,128)S(1)}, s32[4,192]{1,0:T(4,128)S(1)}, s32[4,192]{1,0:T(4,128)S(1)}, s32[4,192]{1,0:T(4,128)S(1)}) custom-call(s32[8,256]{1,0:T(8,128)S(1)} %bitcast.5, s32[8,256]{1,0:T(8,128)S(1)} %bitcast.9, s32[8,256]{1,0:T(8,128)S(1)} %bitcast.7, s32[8,256]{1,0:T(8,128)S(1)} %bitcast.11, f32[16,256]{1,0:T(8,128)S(1)} %touch.1.refs_4_), custom_call_target="tpu_custom_call" | custom-call | tf_op jit(solution)/shard_map/route/pallas_call | solution.py:335
  9.2 2.9 %collective-permute-start.3 = (s32[4,192]{1,0:T(4,128)S(1)}, s32[4,192]{1,0:T(4,128)S(1)}, u32[]{:S(2)}, u32[]{:S(2)}) collective-permute-start(s32[4,192]{1,0:T(4,128)S(1)} %get-tuple-element.54), channel_id=1, source_target_pairs={{0,6},{1,7},{2,4},{3,5},{4,2},{5,3},{6,0},{7,1},{8,14},{9,15},{10,... | collective-permute-start | bytes 9224 | tf_op jit(solution)/shard_map/ppermute | solution.py:312
  12.1 0.4 collective-permute-start.4
  12.7 0.7 %widen.1.refs_4_ = f32[16384,128]{1,0:T(8,128)S(1)} custom-call(bf16[8192,256]{1,0:T(8,128)(2,1)S(1)} %copy-done), custom_call_target="tpu_custom_call" | custom-call | tf_op jit(solution)/shard_map/widen/pallas_call | solution.py:328
  13.4 0.8 %bag_lists.1 = (s32[8,192]{1,0:T(8,128)S(1)}, s32[8,192]{1,0:T(8,128)S(1)}) custom-call(s32[8,256]{1,0:T(8,128)S(1)} %bitcast.6, s32[8,256]{1,0:T(8,128)S(1)} %bitcast.10, s32[8,256]{1,0:T(8,128)S(1)} %bitcast.8, s32[8,256]{1,0:T(8,128)S(1)} %bitcast.12), custom_call_target="tpu_custom_call" | custom-call | tf_op jit(solution)/shard_map/bag_lists/pallas_call | solution.py:342
  14.3 1.4 %collective-permute-done.4.refs_1_ = s32[4,192]{1,0:T(4,128)S(1)} collective-permute-done((s32[4,192]{1,0:T(4,128)S(1)}, s32[4,192]{1,0:T(4,128)S(1)}, u32[]{:S(2)}, u32[]{:S(2)}) %collective-permute-start.4) | collective-permute-done | bytes 3104 | tf_op jit(solution)/shard_map/ppermute | solution.py:312
  15.7 0.4 collective-permute-done.5.refs_2_
  16.1 1.9 %gather.4 = (bf16[4,192,256]{2,1,0:T(8,128)(2,1)S(1)}, bf16[4,192,256]{2,1,0:T(8,128)(2,1)S(1)}) custom-call(s32[4,192]{1,0:T(4,128)S(1)} %collective-permute-done.3.refs_0_, s32[4,192]{1,0:T(4,128)S(1)} %collective-permute-done.4.refs_1_, s32[4,192]{1,0:T(4,128)S(1)} %collective-permute-done.5.refs_2_, s32[4,192]{1,0:T(4,128)S(1)} %get-tuple-element.45.refs_3_, ...), custom_call_target="tpu_custom_call" | custom-call | tf_op jit(solution)/shard_map/gather/pallas_call | solution.py:353
  18.2 0.5 collective-permute-start.6
  18.7 1.4 %gather.5.same_ref = bf16[4,192,256]{2,1,0:T(8,128)(2,1)S(1)} custom-call(s32[4,192]{1,0:T(4,128)S(1)} %collective-permute-done.3.refs_0_, s32[4,192]{1,0:T(4,128)S(1)} %collective-permute-done.4.refs_1_, s32[4,192]{1,0:T(4,128)S(1)} %collective-permute-done.5.refs_2_, s32[4,192]{1,0:T(4,128)S(1)} %get-tuple-element.45.refs_3_, f32[16384,128]{1,0:T(8,128)S(1)} %widen.1.refs_4_), custom_call_target="tpu_custom_call" | custom-call | tf_op jit(solution)/shard_map/gather/pallas_call | solution.py:353
  20.4 1.9 %collective-permute-start.9 = (bf16[2,192,256]{2,1,0:T(8,128)(2,1)S(1)}, bf16[2,192,256]{2,1,0:T(8,128)(2,1)S(1)}, u32[]{:S(2)}, u32[]{:S(2)}) collective-permute-start(bf16[2,192,256]{2,1,0:T(8,128)(2,1)S(1)} %get-tuple-element.65), channel_id=1, source_target_pairs={{0,4},{1,5},{2,6},{3,7},{4,0},{5,1},{6,2},{7,3},{8,12},{9,13},{10,... | collective-permute-start | bytes 589832 | tf_op jit(solution)/shard_map/ppermute | solution.py:312
  22.3 1.4 %collective-permute-start.10 = (bf16[2,192,256]{2,1,0:T(8,128)(2,1)S(1)}, bf16[2,192,256]{2,1,0:T(8,128)(2,1)S(1)}, u32[]{:S(2)}, u32[]{:S(2)}) collective-permute-start(bf16[2,192,256]{2,1,0:T(8,128)(2,1)S(1)} %get-tuple-element.66), channel_id=1, source_target_pairs={{0,6},{1,7},{2,4},{3,5},{4,2},{5,3},{6,0},{7,1},{8,14},{9,15},{10,... | collective-permute-start | bytes 589832 | tf_op jit(solution)/shard_map/ppermute | solution.py:312
  23.7 1.4 %gather.3.same_ref = bf16[4,192,256]{2,1,0:T(8,128)(2,1)S(1)} custom-call(s32[4,192]{1,0:T(4,128)S(1)} %collective-permute-done.3.refs_0_, s32[4,192]{1,0:T(4,128)S(1)} %collective-permute-done.4.refs_1_, s32[4,192]{1,0:T(4,128)S(1)} %collective-permute-done.5.refs_2_, s32[4,192]{1,0:T(4,128)S(1)} %get-tuple-element.45.refs_3_, f32[16384,128]{1,0:T(8,128)S(1)} %widen.1.refs_4_), custom_call_target="tpu_custom_call" | custom-call | tf_op jit(solution)/shard_map/gather/pallas_call | solution.py:353
  25.1 2.0 %collective-permute-done.8.refs_0_ = bf16[2,192,256]{2,1,0:T(8,128)(2,1)S(1)} collective-permute-done((bf16[2,192,256]{2,1,0:T(8,128)(2,1)S(1)}, bf16[2,192,256]{2,1,0:T(8,128)(2,1)S(1)}, u32[]{:S(2)}, u32[]{:S(2)}) %collective-permute-start.8) | collective-permute-done | bytes 196640 | tf_op jit(solution)/shard_map/ppermute | solution.py:312
  27.5 1.8 %collective-permute-start.13 = (bf16[2,192,256]{2,1,0:T(8,128)(2,1)S(1)}, bf16[2,192,256]{2,1,0:T(8,128)(2,1)S(1)}, u32[]{:S(2)}, u32[]{:S(2)}) collective-permute-start(bf16[2,192,256]{2,1,0:T(8,128)(2,1)S(1)} %get-tuple-element.68), channel_id=1, source_target_pairs={{0,4},{1,5},{2,6},{3,7},{4,0},{5,1},{6,2},{7,3},{8,12},{9,13},{10,... | collective-permute-start | bytes 589832 | tf_op jit(solution)/shard_map/ppermute | solution.py:312
  29.3 1.4 %collective-permute-start.14 = (bf16[2,192,256]{2,1,0:T(8,128)(2,1)S(1)}, bf16[2,192,256]{2,1,0:T(8,128)(2,1)S(1)}, u32[]{:S(2)}, u32[]{:S(2)}) collective-permute-start(bf16[2,192,256]{2,1,0:T(8,128)(2,1)S(1)} %get-tuple-element.63), channel_id=1, source_target_pairs={{0,6},{1,7},{2,4},{3,5},{4,2},{5,3},{6,0},{7,1},{8,14},{9,15},{10,... | collective-permute-start | bytes 589832 | tf_op jit(solution)/shard_map/ppermute | solution.py:312
  30.7 3.0 %collective-permute-done.10.refs_2_ = bf16[2,192,256]{2,1,0:T(8,128)(2,1)S(1)} collective-permute-done((bf16[2,192,256]{2,1,0:T(8,128)(2,1)S(1)}, bf16[2,192,256]{2,1,0:T(8,128)(2,1)S(1)}, u32[]{:S(2)}, u32[]{:S(2)}) %collective-permute-start.10) | collective-permute-done | bytes 196640 | tf_op jit(solution)/shard_map/ppermute | solution.py:312
  34.2 2.7 %collective-permute-start.11 = (bf16[256,256]{1,0:T(8,128)(2,1)S(1)}, bf16[256,256]{1,0:T(8,128)(2,1)S(1)}, u32[]{:S(2)}, u32[]{:S(2)}) collective-permute-start(bf16[256,256]{1,0:T(8,128)(2,1)S(1)} %item_sums.1), channel_id=1, source_target_pairs={{0,8},{1,9},{2,10},{3,11},{4,12},{5,13},{6,14},{7,15},{8,0},{9,1},... | collective-permute-start | bytes 393224 | tf_op jit(solution)/shard_map/ppermute | solution.py:315
  37.6 5.5 %collective-permute-done.11.far_ref = bf16[256,256]{1,0:T(8,128)(2,1)S(1)} collective-permute-done((bf16[256,256]{1,0:T(8,128)(2,1)S(1)}, bf16[256,256]{1,0:T(8,128)(2,1)S(1)}, u32[]{:S(2)}, u32[]{:S(2)}) %collective-permute-start.11) | collective-permute-done | bytes 131104 | tf_op jit(solution)/shard_map/ppermute | solution.py:315
  43.2 3.4 %collective-permute-done.14.refs_2_ = bf16[2,192,256]{2,1,0:T(8,128)(2,1)S(1)} collective-permute-done((bf16[2,192,256]{2,1,0:T(8,128)(2,1)S(1)}, bf16[2,192,256]{2,1,0:T(8,128)(2,1)S(1)}, u32[]{:S(2)}, u32[]{:S(2)}) %collective-permute-start.14) | collective-permute-done | bytes 196640 | tf_op jit(solution)/shard_map/ppermute | solution.py:312
  46.5 0.5 items.1
  47.1 1.6 %collective-permute-start.17 = (bf16[256,256]{1,0:T(8,128)(2,1)S(1)}, bf16[256,256]{1,0:T(8,128)(2,1)S(1)}, u32[]{:S(2)}, u32[]{:S(2)}) collective-permute-start(bf16[256,256]{1,0:T(8,128)(2,1)S(1)} %get-tuple-element.69.refs_1_.refs_2_), channel_id=1, source_target_pairs={{0,16},{16,0},{1,17},{17,1},{2,18},{18,2},{3,19},{19,3},{4,20},{20... | collective-permute-start | bytes 393224 | tf_op jit(solution)/shard_map/ppermute | solution.py:282
  49.1 1.8 %tower.1 = (f32[256,256]{1,0:T(8,128)S(1)}, f32[256,1]{1,0:T(8,128)S(1)}, bf16[256,256]{1,0:T(8,128)(2,1)S(1)}, f32[256,4096]{1,0:T(8,128)S(1)}) custom-call(f32[256,256]{1,0:T(8,128)S(1)} %query_sums.2.near_ref, bf16[256,256]{1,0:T(8,128)(2,1)S(1)} %collective-permute-done.15.far_ref, bf16[256,4096]{1,0:T(8,128)(2,1)S(1)} %copy-done.1, ...), custom_call_target="tpu_custom_call" | custom-call | tf_op jit(solution)/shard_map/tower/pallas_call | solution.py:414
  50.9 0.8 %collective-permute-start.16 = (bf16[256,256]{1,0:T(8,128)(2,1)S(1)}, bf16[256,256]{1,0:T(8,128)(2,1)S(1)}, u32[]{:S(2)}, u32[]{:S(2)}) collective-permute-start(bf16[256,256]{1,0:T(8,128)(2,1)S(1)} %get-tuple-element.77.refs_0_), channel_id=1, source_target_pairs={{0,16},{16,0},{1,17},{17,1},{2,18},{18,2},{3,19},{19,3},{4,20},{20... | collective-permute-start | bytes 393224 | tf_op jit(solution)/shard_map/ppermute | solution.py:282
  52.1 2.4 %query_grads.1 = (f32[1,256]{1,0:T(1,128)S(1)}, f32[256,256]{1,0:T(8,128)S(1)}, f32[256,256]{1,0:T(8,128)S(1)}) custom-call(bf16[256,256]{1,0:T(8,128)(2,1)S(1)} %get-tuple-element.77.refs_0_, bf16[256,256]{1,0:T(8,128)(2,1)S(1)} %get-tuple-element.69.refs_1_.refs_2_, bf16[256,256]{1,0:T(8,128)(2,1)S(1)} %collective-permute-done.17.refs_2_.refs_3_, ...), custom_call_target="tpu_custom_call" | custom-call | tf_op jit(solution)/shard_map/query_grads/pallas_call | solution.py:426
  54.5 1.5 %collective-permute-done.16.refs_1_ = bf16[256,256]{1,0:T(8,128)(2,1)S(1)} collective-permute-done((bf16[256,256]{1,0:T(8,128)(2,1)S(1)}, bf16[256,256]{1,0:T(8,128)(2,1)S(1)}, u32[]{:S(2)}, u32[]{:S(2)}) %collective-permute-start.16) | collective-permute-done | bytes 131104 | tf_op jit(solution)/shard_map/ppermute | solution.py:282
  56.0 1.5 %item_grads.1 = (f32[256,256]{1,0:T(8,128)}, f32[1,256]{1,0:T(1,128)}, f32[256,256]{1,0:T(8,128)}) custom-call(bf16[256,256]{1,0:T(8,128)(2,1)S(1)} %get-tuple-element.77.refs_0_, bf16[256,256]{1,0:T(8,128)(2,1)S(1)} %collective-permute-done.16.refs_1_, bf16[256,256]{1,0:T(8,128)(2,1)S(1)} %get-tuple-element.69.refs_1_.refs_2_, ...), custom_call_target="tpu_custom_call" | custom-call | tf_op jit(solution)/shard_map/item_grads/pallas_call | solution.py:438
  (27 shorter events, 3.0 us)
Async XLA Ops:
  0.6 12.1 %copy-start = (bf16[8192,256]{1,0:T(8,128)(2,1)S(1)}, bf16[8192,256]{1,0:T(8,128)(2,1)}, u32[]{:S(2)}) copy-start(bf16[8192,256]{1,0:T(8,128)(2,1)} %table_hbm.1) | copy-start | bytes 12582916
  1.5 5.7 %collective-permute-start.1 = (s32[256,8]{0,1:T(8,128)S(1)}, s32[256,8]{0,1:T(8,128)S(1)}, u32[]{:S(2)}, u32[]{:S(2)}) collective-permute-start(s32[256,8]{0,1:T(8,128)S(1)} %multiply_add_fusion), channel_id=1, source_target_pairs={{0,8},{1,9},{2,10},{3,11},{4,12},{5,13},{6,14},{7,15},{8,0},{9,1},... | collective-permute-start | bytes 24584 | tf_op jit(solution)/shard_map/ppermute | solution.py:315
  5.5 2.3 %collective-permute-start = (s32[256,8]{0,1:T(8,128)S(1)}, s32[256,8]{0,1:T(8,128)S(1)}, u32[]{:S(2)}, u32[]{:S(2)}) collective-permute-start(s32[256,8]{0,1:T(8,128)S(1)} %multiply_add_fusion), channel_id=1, source_target_pairs={{0,1},{1,0},{2,3},{3,2},{4,5},{5,4},{6,7},{7,6},{8,9},{9,8},{10,11... | collective-permute-start | bytes 24584 | tf_op jit(solution)/shard_map/ppermute | solution.py:312
  7.2 1.2 %collective-permute-start.2 = (s32[256,8]{0,1:T(8,128)S(1)}, s32[256,8]{0,1:T(8,128)S(1)}, u32[]{:S(2)}, u32[]{:S(2)}) collective-permute-start(s32[256,8]{0,1:T(8,128)S(1)} %collective-permute-done.1), channel_id=1, source_target_pairs={{0,1},{1,0},{2,3},{3,2},{4,5},{5,4},{6,7},{7,6},{8,9},{9,8},{10,11... | collective-permute-start | bytes 24584 | tf_op jit(solution)/shard_map/ppermute | solution.py:312
  9.2 5.1 %collective-permute-start.3 = (s32[4,192]{1,0:T(4,128)S(1)}, s32[4,192]{1,0:T(4,128)S(1)}, u32[]{:S(2)}, u32[]{:S(2)}) collective-permute-start(s32[4,192]{1,0:T(4,128)S(1)} %get-tuple-element.54), channel_id=1, source_target_pairs={{0,6},{1,7},{2,4},{3,5},{4,2},{5,3},{6,0},{7,1},{8,14},{9,15},{10,... | collective-permute-start | bytes 9224 | tf_op jit(solution)/shard_map/ppermute | solution.py:312
  12.1 3.6 %collective-permute-start.4 = (s32[4,192]{1,0:T(4,128)S(1)}, s32[4,192]{1,0:T(4,128)S(1)}, u32[]{:S(2)}, u32[]{:S(2)}) collective-permute-start(s32[4,192]{1,0:T(4,128)S(1)} %get-tuple-element.55), channel_id=1, source_target_pairs={{0,4},{1,5},{2,6},{3,7},{4,0},{5,1},{6,2},{7,3},{8,12},{9,13},{10,... | collective-permute-start | bytes 9224 | tf_op jit(solution)/shard_map/ppermute | solution.py:312
  12.5 3.6 %collective-permute-start.5 = (s32[4,192]{1,0:T(4,128)S(1)}, s32[4,192]{1,0:T(4,128)S(1)}, u32[]{:S(2)}, u32[]{:S(2)}) collective-permute-start(s32[4,192]{1,0:T(4,128)S(1)} %get-tuple-element.56), channel_id=1, source_target_pairs={{0,2},{1,3},{2,0},{3,1},{4,6},{5,7},{6,4},{7,5},{8,10},{9,11},{10,... | collective-permute-start | bytes 9224 | tf_op jit(solution)/shard_map/ppermute | solution.py:312
  18.1 2.0 %collective-permute-start.7 = (bf16[4,192,256]{2,1,0:T(8,128)(2,1)S(1)}, bf16[4,192,256]{2,1,0:T(8,128)(2,1)S(1)}, u32[]{:S(2)}, u32[]{:S(2)}) collective-permute-start(bf16[4,192,256]{2,1,0:T(8,128)(2,1)S(1)} %get-tuple-element.59), channel_id=1, source_target_pairs={{0,1},{1,0},{2,3},{3,2},{4,5},{5,4},{6,7},{7,6},{8,9},{9,8},{10,11... | collective-permute-start | bytes 1179656 | tf_op jit(solution)/shard_map/ppermute | solution.py:312
  18.2 6.9 %collective-permute-start.6 = (bf16[4,192,256]{2,1,0:T(8,128)(2,1)S(1)}, bf16[4,192,256]{2,1,0:T(8,128)(2,1)S(1)}, u32[]{:S(2)}, u32[]{:S(2)}) collective-permute-start(bf16[4,192,256]{2,1,0:T(8,128)(2,1)S(1)} %get-tuple-element.58), channel_id=1, source_target_pairs={{0,1},{1,0},{2,3},{3,2},{4,5},{5,4},{6,7},{7,6},{8,9},{9,8},{10,11... | collective-permute-start | bytes 1179656 | tf_op jit(solution)/shard_map/ppermute | solution.py:312
  20.1 7.0 %collective-permute-start.8 = (bf16[2,192,256]{2,1,0:T(8,128)(2,1)S(1)}, bf16[2,192,256]{2,1,0:T(8,128)(2,1)S(1)}, u32[]{:S(2)}, u32[]{:S(2)}) collective-permute-start(bf16[2,192,256]{2,1,0:T(8,128)(2,1)S(1)} %get-tuple-element.60), channel_id=1, source_target_pairs={{0,2},{1,3},{2,0},{3,1},{4,6},{5,7},{6,4},{7,5},{8,10},{9,11},{10,... | collective-permute-start | bytes 589832 | tf_op jit(solution)/shard_map/ppermute | solution.py:312
  20.4 10.3 %collective-permute-start.9 = (bf16[2,192,256]{2,1,0:T(8,128)(2,1)S(1)}, bf16[2,192,256]{2,1,0:T(8,128)(2,1)S(1)}, u32[]{:S(2)}, u32[]{:S(2)}) collective-permute-start(bf16[2,192,256]{2,1,0:T(8,128)(2,1)S(1)} %get-tuple-element.65), channel_id=1, source_target_pairs={{0,4},{1,5},{2,6},{3,7},{4,0},{5,1},{6,2},{7,3},{8,12},{9,13},{10,... | collective-permute-start | bytes 589832 | tf_op jit(solution)/shard_map/ppermute | solution.py:312
  22.3 11.4 %collective-permute-start.10 = (bf16[2,192,256]{2,1,0:T(8,128)(2,1)S(1)}, bf16[2,192,256]{2,1,0:T(8,128)(2,1)S(1)}, u32[]{:S(2)}, u32[]{:S(2)}) collective-permute-start(bf16[2,192,256]{2,1,0:T(8,128)(2,1)S(1)} %get-tuple-element.66), channel_id=1, source_target_pairs={{0,6},{1,7},{2,4},{3,5},{4,2},{5,3},{6,0},{7,1},{8,14},{9,15},{10,... | collective-permute-start | bytes 589832 | tf_op jit(solution)/shard_map/ppermute | solution.py:312
  25.1 24.0 %copy-start.1 = (bf16[256,4096]{1,0:T(8,128)(2,1)S(1)}, bf16[256,4096]{1,0:T(8,128)(2,1)}, u32[]{:S(2)}) copy-start(bf16[256,4096]{1,0:T(8,128)(2,1)} %refs_3_.1) | copy-start | bytes 6291460
  25.1 24.0 %copy-start.2 = (bf16[4096,256]{1,0:T(8,128)(2,1)S(1)}, bf16[4096,256]{1,0:T(8,128)(2,1)}, u32[]{:S(2)}) copy-start(bf16[4096,256]{1,0:T(8,128)(2,1)} %refs_4_.1) | copy-start | bytes 6291460
  27.1 16.0 %collective-permute-start.12 = (bf16[2,192,256]{2,1,0:T(8,128)(2,1)S(1)}, bf16[2,192,256]{2,1,0:T(8,128)(2,1)S(1)}, u32[]{:S(2)}, u32[]{:S(2)}) collective-permute-start(bf16[2,192,256]{2,1,0:T(8,128)(2,1)S(1)} %get-tuple-element.67), channel_id=1, source_target_pairs={{0,2},{1,3},{2,0},{3,1},{4,6},{5,7},{6,4},{7,5},{8,10},{9,11},{10,... | collective-permute-start | bytes 589832 | tf_op jit(solution)/shard_map/ppermute | solution.py:312
  27.5 15.7 %collective-permute-start.13 = (bf16[2,192,256]{2,1,0:T(8,128)(2,1)S(1)}, bf16[2,192,256]{2,1,0:T(8,128)(2,1)S(1)}, u32[]{:S(2)}, u32[]{:S(2)}) collective-permute-start(bf16[2,192,256]{2,1,0:T(8,128)(2,1)S(1)} %get-tuple-element.68), channel_id=1, source_target_pairs={{0,4},{1,5},{2,6},{3,7},{4,0},{5,1},{6,2},{7,3},{8,12},{9,13},{10,... | collective-permute-start | bytes 589832 | tf_op jit(solution)/shard_map/ppermute | solution.py:312
  29.3 17.2 %collective-permute-start.14 = (bf16[2,192,256]{2,1,0:T(8,128)(2,1)S(1)}, bf16[2,192,256]{2,1,0:T(8,128)(2,1)S(1)}, u32[]{:S(2)}, u32[]{:S(2)}) collective-permute-start(bf16[2,192,256]{2,1,0:T(8,128)(2,1)S(1)} %get-tuple-element.63), channel_id=1, source_target_pairs={{0,6},{1,7},{2,4},{3,5},{4,2},{5,3},{6,0},{7,1},{8,14},{9,15},{10,... | collective-permute-start | bytes 589832 | tf_op jit(solution)/shard_map/ppermute | solution.py:312
  34.2 9.0 %collective-permute-start.11 = (bf16[256,256]{1,0:T(8,128)(2,1)S(1)}, bf16[256,256]{1,0:T(8,128)(2,1)S(1)}, u32[]{:S(2)}, u32[]{:S(2)}) collective-permute-start(bf16[256,256]{1,0:T(8,128)(2,1)S(1)} %item_sums.1), channel_id=1, source_target_pairs={{0,8},{1,9},{2,10},{3,11},{4,12},{5,13},{6,14},{7,15},{8,0},{9,1},... | collective-permute-start | bytes 393224 | tf_op jit(solution)/shard_map/ppermute | solution.py:315
  37.2 11.8 %collective-permute-start.15 = (bf16[256,256]{1,0:T(8,128)(2,1)S(1)}, bf16[256,256]{1,0:T(8,128)(2,1)S(1)}, u32[]{:S(2)}, u32[]{:S(2)}) collective-permute-start(bf16[256,256]{1,0:T(8,128)(2,1)S(1)} %query_sums.3), channel_id=1, source_target_pairs={{0,8},{1,9},{2,10},{3,11},{4,12},{5,13},{6,14},{7,15},{8,0},{9,1},... | collective-permute-start | bytes 393224 | tf_op jit(solution)/shard_map/ppermute | solution.py:315
  47.1 5.0 %collective-permute-start.17 = (bf16[256,256]{1,0:T(8,128)(2,1)S(1)}, bf16[256,256]{1,0:T(8,128)(2,1)S(1)}, u32[]{:S(2)}, u32[]{:S(2)}) collective-permute-start(bf16[256,256]{1,0:T(8,128)(2,1)S(1)} %get-tuple-element.69.refs_1_.refs_2_), channel_id=1, source_target_pairs={{0,16},{16,0},{1,17},{17,1},{2,18},{18,2},{3,19},{19,3},{4,20},{20... | collective-permute-start | bytes 393224 | tf_op jit(solution)/shard_map/ppermute | solution.py:282
  50.9 5.0 %collective-permute-start.16 = (bf16[256,256]{1,0:T(8,128)(2,1)S(1)}, bf16[256,256]{1,0:T(8,128)(2,1)S(1)}, u32[]{:S(2)}, u32[]{:S(2)}) collective-permute-start(bf16[256,256]{1,0:T(8,128)(2,1)S(1)} %get-tuple-element.77.refs_0_), channel_id=1, source_target_pairs={{0,16},{16,0},{1,17},{17,1},{2,18},{18,2},{3,19},{19,3},{4,20},{20... | collective-permute-start | bytes 393224 | tf_op jit(solution)/shard_map/ppermute | solution.py:282

commit v8 on v6

--- a/solution.py
+++ b/solution.py
@@ -364,9 +364,9 @@
             name="gather",
         )(*wanted[::-1], wide)
 
-    order = list(range(1, chips))
-
-    def answered(same, swapped):
+    order = list(range(chips - 1, 0, -1))
+
+    def answered(same, swapped, order):
         messages = pl.pallas_call(
             functools.partial(pack_kernel, chips),
             out_shape=[struct((2, capacity, width), bf)] * (chips - 1),
@@ -381,11 +381,11 @@
 
     far_other, near_other = [to_chip(rows, 0, 1) for rows in gather((3, 1))]
     (far_same,), (near_same,) = gather((2,)), gather((0,))
-    far_rows, _ = answered(far_same, far_other)
-    near_rows, near_messages = answered(near_same, near_other)
+    far_rows, _ = answered(far_same, far_other, order)
+    near_rows, near_messages = answered(near_same, near_other, order[::-1])
     far_bags, _ = lax.optimization_barrier((far_bags, near_messages[0]))
 
-    def sums(kind, bags, rows, dtype):
+    def sums(order, kind, bags, rows, dtype):
         return pl.pallas_call(
             functools.partial(sum_kernel, order, kind),
             out_shape=struct((pairs, width), dtype),
@@ -393,12 +393,12 @@
             name="item_sums" if kind else "query_sums",
         )(bags, *rows)
 
-    far_item = sums(1, far_bags, far_rows, bf)
+    far_item = sums(order, 1, far_bags, far_rows, bf)
     far_bags, _ = lax.optimization_barrier((far_bags, far_item))
-    far_query = to_mirror(sums(0, far_bags, far_rows, bf))
+    far_query = to_mirror(sums(order, 0, far_bags, far_rows, bf))
     far_item = to_mirror(far_item)
     item_unit, item_scale, item_bf = pl.pallas_call(
-        functools.partial(item_kernel, order),
+        functools.partial(item_kernel, order[::-1]),
         out_shape=[
             struct((pairs, width), f32),
             struct((pairs, 1), f32),
@@ -408,7 +408,7 @@
         name="items",
     )(near_bags, far_item, *near_rows)
     near_bags, _ = lax.optimization_barrier((near_bags, item_bf))
-    near_query = sums(0, near_bags, near_rows, f32)
+    near_query = sums(order[::-1], 0, near_bags, near_rows, f32)
     items = [item_bf] + [rotated(item_bf, "blk", by) for by in range(1, blocks)]
     query_unit, query_scale, query_bf, slope = pl.pallas_call(
         tower_kernel,

time: 57.7 us -> 57.5 us (level)
  transfers between devices with their start and end apart: 18 -> 18, of which waited for: 9 -> 11; matrix products, arithmetic and copies ran while one was open for 0% -> 0% of each run, Pallas kernels for 19% -> 19%
where the time goes in v8:
time: 57.5 us; the launch traced here: 57.2 us
  starting transfers between devices  20.6 us (36%)
  waiting for transfers between devices  19.5 us (34%)
  Pallas kernels  15.3 us (27%)
  other arithmetic  0.87 us (2%)
  between operations  0.83 us (1%)
    ppermute x13, waiting for transfers between devices, to_chip(): return lax.ppermute(values, 'table', route)  15.9 us
    ppermute x13, starting transfers between devices, to_chip(): return lax.ppermute(values, 'table', route)  11.4 us
    ppermute x3, starting transfers between devices, to_mirror(): lax.ppermute(values, 'table', [(t, (t + half) % shards) for t in range(sh...  7.09 us
    pallas_call x3, Pallas kernels, gather(): pl.pallas_call(functools.partial(gather_kernel, chips, askers), in_specs=...  4.73 us
    pallas_call x1, Pallas kernels, local(): pl.pallas_call(functools.partial(query_grad_kernel, blocks), out_shape=[s...  2.39 us
    ppermute x2, starting transfers between devices, rotated(): lax.ppermute(shard, axis, [(i, (i + by) % count) for i in range(count)])  2.16 us
    ppermute x2, waiting for transfers between devices, rotated(): lax.ppermute(shard, axis, [(i, (i + by) % count) for i in range(count)])  2.04 us
    pallas_call x1, Pallas kernels, local(): pl.pallas_call(tower_kernel, out_shape=[struct((pairs, width), f32), stru...  1.85 us
  transfers between devices with their start and end apart: 18, of which 11 were waited for; matrix products, arithmetic and copies ran while one was open for 0% of the time, Pallas kernels for 19%

profile of v8, /device:TPU:0, one launch (start us, length us, event | category | flops | bytes accessed | tf_op | source)
XLA Modules:
  0.0 57.2 jit_solution(15087106579733138126)
XLA Ops:
  0.6 0.9 %multiply_add_fusion = s32[256,8]{0,1:T(8,128)S(1)} fusion(s32[256,8]{0,1:T(8,128)} %param.9, s32[256,8]{0,1:T(8,128)} %param.8), kind=kLoop, calls=%fused_computation | loop fusion | flops 4096 | bytes 24576 | tf_op jit(solution)/shard_map/add | solution.py:317
  1.5 4.0 %collective-permute-start.1 = (s32[256,8]{0,1:T(8,128)S(1)}, s32[256,8]{0,1:T(8,128)S(1)}, u32[]{:S(2)}, u32[]{:S(2)}) collective-permute-start(s32[256,8]{0,1:T(8,128)S(1)} %multiply_add_fusion), channel_id=1, source_target_pairs={{0,8},{1,9},{2,10},{3,11},{4,12},{5,13},{6,14},{7,15},{8,0},{9,1},... | collective-permute-start | bytes 24584 | tf_op jit(solution)/shard_map/ppermute | solution.py:315
  5.6 1.6 %collective-permute-done.1 = s32[256,8]{0,1:T(8,128)S(1)} collective-permute-done((s32[256,8]{0,1:T(8,128)S(1)}, s32[256,8]{0,1:T(8,128)S(1)}, u32[]{:S(2)}, u32[]{:S(2)}) %collective-permute-start.1) | collective-permute-done | bytes 8224 | tf_op jit(solution)/shard_map/ppermute | solution.py:315
  7.2 0.7 %touch.1.refs_4_ = f32[16,256]{1,0:T(8,128)S(1)} custom-call(bf16[8192,256]{1,0:T(8,128)(2,1)} %table_hbm.1), custom_call_target="tpu_custom_call" | custom-call | tf_op jit(solution)/shard_map/touch/pallas_call | solution.py:320
  8.3 0.8 %route.1 = (s32[4,192]{1,0:T(4,128)S(1)}, s32[4,192]{1,0:T(4,128)S(1)}, s32[4,192]{1,0:T(4,128)S(1)}, s32[4,192]{1,0:T(4,128)S(1)}) custom-call(s32[8,256]{1,0:T(8,128)S(1)} %bitcast.5, s32[8,256]{1,0:T(8,128)S(1)} %bitcast.9, s32[8,256]{1,0:T(8,128)S(1)} %bitcast.7, s32[8,256]{1,0:T(8,128)S(1)} %bitcast.11, f32[16,256]{1,0:T(8,128)S(1)} %touch.1.refs_4_), custom_call_target="tpu_custom_call" | custom-call | tf_op jit(solution)/shard_map/route/pallas_call | solution.py:335
  9.2 2.9 %collective-permute-start.3 = (s32[4,192]{1,0:T(4,128)S(1)}, s32[4,192]{1,0:T(4,128)S(1)}, u32[]{:S(2)}, u32[]{:S(2)}) collective-permute-start(s32[4,192]{1,0:T(4,128)S(1)} %get-tuple-element.52), channel_id=1, source_target_pairs={{0,6},{1,7},{2,4},{3,5},{4,2},{5,3},{6,0},{7,1},{8,14},{9,15},{10,... | collective-permute-start | bytes 9224 | tf_op jit(solution)/shard_map/ppermute | solution.py:312
  12.1 0.4 collective-permute-start.4
  12.7 0.7 %widen.1.refs_4_ = f32[16384,128]{1,0:T(8,128)S(1)} custom-call(bf16[8192,256]{1,0:T(8,128)(2,1)S(1)} %copy-done), custom_call_target="tpu_custom_call" | custom-call | tf_op jit(solution)/shard_map/widen/pallas_call | solution.py:328
  13.4 0.8 %bag_lists.1 = (s32[8,192]{1,0:T(8,128)S(1)}, s32[8,192]{1,0:T(8,128)S(1)}) custom-call(s32[8,256]{1,0:T(8,128)S(1)} %bitcast.6, s32[8,256]{1,0:T(8,128)S(1)} %bitcast.10, s32[8,256]{1,0:T(8,128)S(1)} %bitcast.8, s32[8,256]{1,0:T(8,128)S(1)} %bitcast.12), custom_call_target="tpu_custom_call" | custom-call | tf_op jit(solution)/shard_map/bag_lists/pallas_call | solution.py:342
  14.3 1.4 %collective-permute-done.4.refs_1_ = s32[4,192]{1,0:T(4,128)S(1)} collective-permute-done((s32[4,192]{1,0:T(4,128)S(1)}, s32[4,192]{1,0:T(4,128)S(1)}, u32[]{:S(2)}, u32[]{:S(2)}) %collective-permute-start.4) | collective-permute-done | bytes 3104 | tf_op jit(solution)/shard_map/ppermute | solution.py:312
  16.1 1.9 %gather.4 = (bf16[4,192,256]{2,1,0:T(8,128)(2,1)S(1)}, bf16[4,192,256]{2,1,0:T(8,128)(2,1)S(1)}) custom-call(s32[4,192]{1,0:T(4,128)S(1)} %collective-permute-done.3.refs_0_, s32[4,192]{1,0:T(4,128)S(1)} %collective-permute-done.4.refs_1_, s32[4,192]{1,0:T(4,128)S(1)} %collective-permute-done.5.refs_2_, s32[4,192]{1,0:T(4,128)S(1)} %get-tuple-element.43.refs_3_, ...), custom_call_target="tpu_custom_call" | custom-call | tf_op jit(solution)/shard_map/gather/pallas_call | solution.py:353
  18.2 0.5 collective-permute-start.6
  18.7 1.4 %gather.5.same_ref = bf16[4,192,256]{2,1,0:T(8,128)(2,1)S(1)} custom-call(s32[4,192]{1,0:T(4,128)S(1)} %collective-permute-done.3.refs_0_, s32[4,192]{1,0:T(4,128)S(1)} %collective-permute-done.4.refs_1_, s32[4,192]{1,0:T(4,128)S(1)} %collective-permute-done.5.refs_2_, s32[4,192]{1,0:T(4,128)S(1)} %get-tuple-element.43.refs_3_, f32[16384,128]{1,0:T(8,128)S(1)} %widen.1.refs_4_), custom_call_target="tpu_custom_call" | custom-call | tf_op jit(solution)/shard_map/gather/pallas_call | solution.py:353
  20.1 1.6 %collective-permute-start.8 = (bf16[2,192,256]{2,1,0:T(8,128)(2,1)S(1)}, bf16[2,192,256]{2,1,0:T(8,128)(2,1)S(1)}, u32[]{:S(2)}, u32[]{:S(2)}) collective-permute-start(bf16[2,192,256]{2,1,0:T(8,128)(2,1)S(1)} %get-tuple-element.60), channel_id=1, source_target_pairs={{0,6},{1,7},{2,4},{3,5},{4,2},{5,3},{6,0},{7,1},{8,14},{9,15},{10,... | collective-permute-start | bytes 589832 | tf_op jit(solution)/shard_map/ppermute | solution.py:312
  21.9 1.8 %collective-permute-start.10 = (bf16[2,192,256]{2,1,0:T(8,128)(2,1)S(1)}, bf16[2,192,256]{2,1,0:T(8,128)(2,1)S(1)}, u32[]{:S(2)}, u32[]{:S(2)}) collective-permute-start(bf16[2,192,256]{2,1,0:T(8,128)(2,1)S(1)} %get-tuple-element.62), channel_id=1, source_target_pairs={{0,2},{1,3},{2,0},{3,1},{4,6},{5,7},{6,4},{7,5},{8,10},{9,11},{10,... | collective-permute-start | bytes 589832 | tf_op jit(solution)/shard_map/ppermute | solution.py:312
  23.7 1.4 %gather.3.same_ref = bf16[4,192,256]{2,1,0:T(8,128)(2,1)S(1)} custom-call(s32[4,192]{1,0:T(4,128)S(1)} %collective-permute-done.3.refs_0_, s32[4,192]{1,0:T(4,128)S(1)} %collective-permute-done.4.refs_1_, s32[4,192]{1,0:T(4,128)S(1)} %collective-permute-done.5.refs_2_, s32[4,192]{1,0:T(4,128)S(1)} %get-tuple-element.43.refs_3_, f32[16384,128]{1,0:T(8,128)S(1)} %widen.1.refs_4_), custom_call_target="tpu_custom_call" | custom-call | tf_op jit(solution)/shard_map/gather/pallas_call | solution.py:353
  25.4 1.9 %collective-permute-start.13 = (bf16[2,192,256]{2,1,0:T(8,128)(2,1)S(1)}, bf16[2,192,256]{2,1,0:T(8,128)(2,1)S(1)}, u32[]{:S(2)}, u32[]{:S(2)}) collective-permute-start(bf16[2,192,256]{2,1,0:T(8,128)(2,1)S(1)} %get-tuple-element.64), channel_id=1, source_target_pairs={{0,4},{1,5},{2,6},{3,7},{4,0},{5,1},{6,2},{7,3},{8,12},{9,13},{10,... | collective-permute-start | bytes 589832 | tf_op jit(solution)/shard_map/ppermute | solution.py:312
  27.3 1.6 %collective-permute-done.8.refs_0_ = bf16[2,192,256]{2,1,0:T(8,128)(2,1)S(1)} collective-permute-done((bf16[2,192,256]{2,1,0:T(8,128)(2,1)S(1)}, bf16[2,192,256]{2,1,0:T(8,128)(2,1)S(1)}, u32[]{:S(2)}, u32[]{:S(2)}) %collective-permute-start.8) | collective-permute-done | bytes 196640 | tf_op jit(solution)/shard_map/ppermute | solution.py:312
  28.9 1.5 %collective-permute-start.14 = (bf16[2,192,256]{2,1,0:T(8,128)(2,1)S(1)}, bf16[2,192,256]{2,1,0:T(8,128)(2,1)S(1)}, u32[]{:S(2)}, u32[]{:S(2)}) collective-permute-start(bf16[2,192,256]{2,1,0:T(8,128)(2,1)S(1)} %get-tuple-element.57), channel_id=1, source_target_pairs={{0,6},{1,7},{2,4},{3,5},{4,2},{5,3},{6,0},{7,1},{8,14},{9,15},{10,... | collective-permute-start | bytes 589832 | tf_op jit(solution)/shard_map/ppermute | solution.py:312
  30.4 1.4 %collective-permute-done.9.refs_1_ = bf16[2,192,256]{2,1,0:T(8,128)(2,1)S(1)} collective-permute-done((bf16[2,192,256]{2,1,0:T(8,128)(2,1)S(1)}, bf16[2,192,256]{2,1,0:T(8,128)(2,1)S(1)}, u32[]{:S(2)}, u32[]{:S(2)}) %collective-permute-start.9) | collective-permute-done | bytes 196640 | tf_op jit(solution)/shard_map/ppermute | solution.py:312
  31.8 0.5 collective-permute-done.10.refs_2_
  32.7 2.7 %collective-permute-start.11 = (bf16[256,256]{1,0:T(8,128)(2,1)S(1)}, bf16[256,256]{1,0:T(8,128)(2,1)S(1)}, u32[]{:S(2)}, u32[]{:S(2)}) collective-permute-start(bf16[256,256]{1,0:T(8,128)(2,1)S(1)} %item_sums.1), channel_id=1, source_target_pairs={{0,8},{1,9},{2,10},{3,11},{4,12},{5,13},{6,14},{7,15},{8,0},{9,1},... | collective-permute-start | bytes 393224 | tf_op jit(solution)/shard_map/ppermute | solution.py:315
  36.2 0.5 collective-permute-done.12.refs_0_
  36.7 9.6 %collective-permute-done.14.refs_2_ = bf16[2,192,256]{2,1,0:T(8,128)(2,1)S(1)} collective-permute-done((bf16[2,192,256]{2,1,0:T(8,128)(2,1)S(1)}, bf16[2,192,256]{2,1,0:T(8,128)(2,1)S(1)}, u32[]{:S(2)}, u32[]{:S(2)}) %collective-permute-start.14) | collective-permute-done | bytes 196640 | tf_op jit(solution)/shard_map/ppermute | solution.py:312
  46.3 0.5 items.1
  46.8 1.6 %collective-permute-start.17 = (bf16[256,256]{1,0:T(8,128)(2,1)S(1)}, bf16[256,256]{1,0:T(8,128)(2,1)S(1)}, u32[]{:S(2)}, u32[]{:S(2)}) collective-permute-start(bf16[256,256]{1,0:T(8,128)(2,1)S(1)} %get-tuple-element.65.refs_1_.refs_2_), channel_id=1, source_target_pairs={{0,16},{16,0},{1,17},{17,1},{2,18},{18,2},{3,19},{19,3},{4,20},{20... | collective-permute-start | bytes 393224 | tf_op jit(solution)/shard_map/ppermute | solution.py:282
  48.8 1.8 %tower.1 = (f32[256,256]{1,0:T(8,128)S(1)}, f32[256,1]{1,0:T(8,128)S(1)}, bf16[256,256]{1,0:T(8,128)(2,1)S(1)}, f32[256,4096]{1,0:T(8,128)S(1)}) custom-call(f32[256,256]{1,0:T(8,128)S(1)} %query_sums.2.near_ref, bf16[256,256]{1,0:T(8,128)(2,1)S(1)} %collective-permute-done.15.far_ref, bf16[256,4096]{1,0:T(8,128)(2,1)S(1)} %copy-done.1, ...), custom_call_target="tpu_custom_call" | custom-call | tf_op jit(solution)/shard_map/tower/pallas_call | solution.py:413
  50.7 0.6 %collective-permute-start.16 = (bf16[256,256]{1,0:T(8,128)(2,1)S(1)}, bf16[256,256]{1,0:T(8,128)(2,1)S(1)}, u32[]{:S(2)}, u32[]{:S(2)}) collective-permute-start(bf16[256,256]{1,0:T(8,128)(2,1)S(1)} %get-tuple-element.73.refs_0_), channel_id=1, source_target_pairs={{0,16},{16,0},{1,17},{17,1},{2,18},{18,2},{3,19},{19,3},{4,20},{20... | collective-permute-start | bytes 393224 | tf_op jit(solution)/shard_map/ppermute | solution.py:282
  51.3 0.6 collective-permute-done.17.refs_2_.refs_3_
  51.8 2.4 %query_grads.1 = (f32[1,256]{1,0:T(1,128)S(1)}, f32[256,256]{1,0:T(8,128)S(1)}, f32[256,256]{1,0:T(8,128)S(1)}) custom-call(bf16[256,256]{1,0:T(8,128)(2,1)S(1)} %get-tuple-element.73.refs_0_, bf16[256,256]{1,0:T(8,128)(2,1)S(1)} %get-tuple-element.65.refs_1_.refs_2_, bf16[256,256]{1,0:T(8,128)(2,1)S(1)} %collective-permute-done.17.refs_2_.refs_3_, ...), custom_call_target="tpu_custom_call" | custom-call | tf_op jit(solution)/shard_map/query_grads/pallas_call | solution.py:425
  54.2 1.5 %collective-permute-done.16.refs_1_ = bf16[256,256]{1,0:T(8,128)(2,1)S(1)} collective-permute-done((bf16[256,256]{1,0:T(8,128)(2,1)S(1)}, bf16[256,256]{1,0:T(8,128)(2,1)S(1)}, u32[]{:S(2)}, u32[]{:S(2)}) %collective-permute-start.16) | collective-permute-done | bytes 131104 | tf_op jit(solution)/shard_map/ppermute | solution.py:282
  55.7 1.5 %item_grads.1 = (f32[256,256]{1,0:T(8,128)}, f32[1,256]{1,0:T(1,128)}, f32[256,256]{1,0:T(8,128)}) custom-call(bf16[256,256]{1,0:T(8,128)(2,1)S(1)} %get-tuple-element.73.refs_0_, bf16[256,256]{1,0:T(8,128)(2,1)S(1)} %collective-permute-done.16.refs_1_, bf16[256,256]{1,0:T(8,128)(2,1)S(1)} %get-tuple-element.65.refs_1_.refs_2_, ...), custom_call_target="tpu_custom_call" | custom-call | tf_op jit(solution)/shard_map/item_grads/pallas_call | solution.py:437
  (27 shorter events, 3.4 us)
Async XLA Ops:
  0.6 12.1 %copy-start = (bf16[8192,256]{1,0:T(8,128)(2,1)S(1)}, bf16[8192,256]{1,0:T(8,128)(2,1)}, u32[]{:S(2)}) copy-start(bf16[8192,256]{1,0:T(8,128)(2,1)} %table_hbm.1) | copy-start | bytes 12582916
  1.5 5.7 %collective-permute-start.1 = (s32[256,8]{0,1:T(8,128)S(1)}, s32[256,8]{0,1:T(8,128)S(1)}, u32[]{:S(2)}, u32[]{:S(2)}) collective-permute-start(s32[256,8]{0,1:T(8,128)S(1)} %multiply_add_fusion), channel_id=1, source_target_pairs={{0,8},{1,9},{2,10},{3,11},{4,12},{5,13},{6,14},{7,15},{8,0},{9,1},... | collective-permute-start | bytes 24584 | tf_op jit(solution)/shard_map/ppermute | solution.py:315
  5.5 2.3 %collective-permute-start = (s32[256,8]{0,1:T(8,128)S(1)}, s32[256,8]{0,1:T(8,128)S(1)}, u32[]{:S(2)}, u32[]{:S(2)}) collective-permute-start(s32[256,8]{0,1:T(8,128)S(1)} %multiply_add_fusion), channel_id=1, source_target_pairs={{0,1},{1,0},{2,3},{3,2},{4,5},{5,4},{6,7},{7,6},{8,9},{9,8},{10,11... | collective-permute-start | bytes 24584 | tf_op jit(solution)/shard_map/ppermute | solution.py:312
  7.2 1.2 %collective-permute-start.2 = (s32[256,8]{0,1:T(8,128)S(1)}, s32[256,8]{0,1:T(8,128)S(1)}, u32[]{:S(2)}, u32[]{:S(2)}) collective-permute-start(s32[256,8]{0,1:T(8,128)S(1)} %collective-permute-done.1), channel_id=1, source_target_pairs={{0,1},{1,0},{2,3},{3,2},{4,5},{5,4},{6,7},{7,6},{8,9},{9,8},{10,11... | collective-permute-start | bytes 24584 | tf_op jit(solution)/shard_map/ppermute | solution.py:312
  9.2 5.1 %collective-permute-start.3 = (s32[4,192]{1,0:T(4,128)S(1)}, s32[4,192]{1,0:T(4,128)S(1)}, u32[]{:S(2)}, u32[]{:S(2)}) collective-permute-start(s32[4,192]{1,0:T(4,128)S(1)} %get-tuple-element.52), channel_id=1, source_target_pairs={{0,6},{1,7},{2,4},{3,5},{4,2},{5,3},{6,0},{7,1},{8,14},{9,15},{10,... | collective-permute-start | bytes 9224 | tf_op jit(solution)/shard_map/ppermute | solution.py:312
  12.1 3.6 %collective-permute-start.4 = (s32[4,192]{1,0:T(4,128)S(1)}, s32[4,192]{1,0:T(4,128)S(1)}, u32[]{:S(2)}, u32[]{:S(2)}) collective-permute-start(s32[4,192]{1,0:T(4,128)S(1)} %get-tuple-element.53), channel_id=1, source_target_pairs={{0,4},{1,5},{2,6},{3,7},{4,0},{5,1},{6,2},{7,3},{8,12},{9,13},{10,... | collective-permute-start | bytes 9224 | tf_op jit(solution)/shard_map/ppermute | solution.py:312
  12.5 3.6 %collective-permute-start.5 = (s32[4,192]{1,0:T(4,128)S(1)}, s32[4,192]{1,0:T(4,128)S(1)}, u32[]{:S(2)}, u32[]{:S(2)}) collective-permute-start(s32[4,192]{1,0:T(4,128)S(1)} %get-tuple-element.54), channel_id=1, source_target_pairs={{0,2},{1,3},{2,0},{3,1},{4,6},{5,7},{6,4},{7,5},{8,10},{9,11},{10,... | collective-permute-start | bytes 9224 | tf_op jit(solution)/shard_map/ppermute | solution.py:312
  18.1 2.0 %collective-permute-start.7 = (bf16[4,192,256]{2,1,0:T(8,128)(2,1)S(1)}, bf16[4,192,256]{2,1,0:T(8,128)(2,1)S(1)}, u32[]{:S(2)}, u32[]{:S(2)}) collective-permute-start(bf16[4,192,256]{2,1,0:T(8,128)(2,1)S(1)} %get-tuple-element.59), channel_id=1, source_target_pairs={{0,1},{1,0},{2,3},{3,2},{4,5},{5,4},{6,7},{7,6},{8,9},{9,8},{10,11... | collective-permute-start | bytes 1179656 | tf_op jit(solution)/shard_map/ppermute | solution.py:312
  18.2 6.9 %collective-permute-start.6 = (bf16[4,192,256]{2,1,0:T(8,128)(2,1)S(1)}, bf16[4,192,256]{2,1,0:T(8,128)(2,1)S(1)}, u32[]{:S(2)}, u32[]{:S(2)}) collective-permute-start(bf16[4,192,256]{2,1,0:T(8,128)(2,1)S(1)} %get-tuple-element.56), channel_id=1, source_target_pairs={{0,1},{1,0},{2,3},{3,2},{4,5},{5,4},{6,7},{7,6},{8,9},{9,8},{10,11... | collective-permute-start | bytes 1179656 | tf_op jit(solution)/shard_map/ppermute | solution.py:312
  20.1 8.8 %collective-permute-start.8 = (bf16[2,192,256]{2,1,0:T(8,128)(2,1)S(1)}, bf16[2,192,256]{2,1,0:T(8,128)(2,1)S(1)}, u32[]{:S(2)}, u32[]{:S(2)}) collective-permute-start(bf16[2,192,256]{2,1,0:T(8,128)(2,1)S(1)} %get-tuple-element.60), channel_id=1, source_target_pairs={{0,6},{1,7},{2,4},{3,5},{4,2},{5,3},{6,0},{7,1},{8,14},{9,15},{10,... | collective-permute-start | bytes 589832 | tf_op jit(solution)/shard_map/ppermute | solution.py:312
  21.7 10.1 %collective-permute-start.9 = (bf16[2,192,256]{2,1,0:T(8,128)(2,1)S(1)}, bf16[2,192,256]{2,1,0:T(8,128)(2,1)S(1)}, u32[]{:S(2)}, u32[]{:S(2)}) collective-permute-start(bf16[2,192,256]{2,1,0:T(8,128)(2,1)S(1)} %get-tuple-element.61), channel_id=1, source_target_pairs={{0,4},{1,5},{2,6},{3,7},{4,0},{5,1},{6,2},{7,3},{8,12},{9,13},{10,... | collective-permute-start | bytes 589832 | tf_op jit(solution)/shard_map/ppermute | solution.py:312
  21.9 10.4 %collective-permute-start.10 = (bf16[2,192,256]{2,1,0:T(8,128)(2,1)S(1)}, bf16[2,192,256]{2,1,0:T(8,128)(2,1)S(1)}, u32[]{:S(2)}, u32[]{:S(2)}) collective-permute-start(bf16[2,192,256]{2,1,0:T(8,128)(2,1)S(1)} %get-tuple-element.62), channel_id=1, source_target_pairs={{0,2},{1,3},{2,0},{3,1},{4,6},{5,7},{6,4},{7,5},{8,10},{9,11},{10,... | collective-permute-start | bytes 589832 | tf_op jit(solution)/shard_map/ppermute | solution.py:312
  25.1 23.7 %copy-start.1 = (bf16[256,4096]{1,0:T(8,128)(2,1)S(1)}, bf16[256,4096]{1,0:T(8,128)(2,1)}, u32[]{:S(2)}) copy-start(bf16[256,4096]{1,0:T(8,128)(2,1)} %refs_3_.1) | copy-start | bytes 6291460
  25.1 23.7 %copy-start.2 = (bf16[4096,256]{1,0:T(8,128)(2,1)S(1)}, bf16[4096,256]{1,0:T(8,128)(2,1)}, u32[]{:S(2)}) copy-start(bf16[4096,256]{1,0:T(8,128)(2,1)} %refs_4_.1) | copy-start | bytes 6291460
  25.2 11.6 %collective-permute-start.12 = (bf16[2,192,256]{2,1,0:T(8,128)(2,1)S(1)}, bf16[2,192,256]{2,1,0:T(8,128)(2,1)S(1)}, u32[]{:S(2)}, u32[]{:S(2)}) collective-permute-start(bf16[2,192,256]{2,1,0:T(8,128)(2,1)S(1)} %get-tuple-element.63), channel_id=1, source_target_pairs={{0,2},{1,3},{2,0},{3,1},{4,6},{5,7},{6,4},{7,5},{8,10},{9,11},{10,... | collective-permute-start | bytes 589832 | tf_op jit(solution)/shard_map/ppermute | solution.py:312
  25.4 11.3 %collective-permute-start.13 = (bf16[2,192,256]{2,1,0:T(8,128)(2,1)S(1)}, bf16[2,192,256]{2,1,0:T(8,128)(2,1)S(1)}, u32[]{:S(2)}, u32[]{:S(2)}) collective-permute-start(bf16[2,192,256]{2,1,0:T(8,128)(2,1)S(1)} %get-tuple-element.64), channel_id=1, source_target_pairs={{0,4},{1,5},{2,6},{3,7},{4,0},{5,1},{6,2},{7,3},{8,12},{9,13},{10,... | collective-permute-start | bytes 589832 | tf_op jit(solution)/shard_map/ppermute | solution.py:312
  28.9 17.4 %collective-permute-start.14 = (bf16[2,192,256]{2,1,0:T(8,128)(2,1)S(1)}, bf16[2,192,256]{2,1,0:T(8,128)(2,1)S(1)}, u32[]{:S(2)}, u32[]{:S(2)}) collective-permute-start(bf16[2,192,256]{2,1,0:T(8,128)(2,1)S(1)} %get-tuple-element.57), channel_id=1, source_target_pairs={{0,6},{1,7},{2,4},{3,5},{4,2},{5,3},{6,0},{7,1},{8,14},{9,15},{10,... | collective-permute-start | bytes 589832 | tf_op jit(solution)/shard_map/ppermute | solution.py:312
  32.7 13.6 %collective-permute-start.11 = (bf16[256,256]{1,0:T(8,128)(2,1)S(1)}, bf16[256,256]{1,0:T(8,128)(2,1)S(1)}, u32[]{:S(2)}, u32[]{:S(2)}) collective-permute-start(bf16[256,256]{1,0:T(8,128)(2,1)S(1)} %item_sums.1), channel_id=1, source_target_pairs={{0,8},{1,9},{2,10},{3,11},{4,12},{5,13},{6,14},{7,15},{8,0},{9,1},... | collective-permute-start | bytes 393224 | tf_op jit(solution)/shard_map/ppermute | solution.py:315
  35.8 13.0 %collective-permute-start.15 = (bf16[256,256]{1,0:T(8,128)(2,1)S(1)}, bf16[256,256]{1,0:T(8,128)(2,1)S(1)}, u32[]{:S(2)}, u32[]{:S(2)}) collective-permute-start(bf16[256,256]{1,0:T(8,128)(2,1)S(1)} %query_sums.3), channel_id=1, source_target_pairs={{0,8},{1,9},{2,10},{3,11},{4,12},{5,13},{6,14},{7,15},{8,0},{9,1},... | collective-permute-start | bytes 393224 | tf_op jit(solution)/shard_map/ppermute | solution.py:315
  46.8 5.0 %collective-permute-start.17 = (bf16[256,256]{1,0:T(8,128)(2,1)S(1)}, bf16[256,256]{1,0:T(8,128)(2,1)S(1)}, u32[]{:S(2)}, u32[]{:S(2)}) collective-permute-start(bf16[256,256]{1,0:T(8,128)(2,1)S(1)} %get-tuple-element.65.refs_1_.refs_2_), channel_id=1, source_target_pairs={{0,16},{16,0},{1,17},{17,1},{2,18},{18,2},{3,19},{19,3},{4,20},{20... | collective-permute-start | bytes 393224 | tf_op jit(solution)/shard_map/ppermute | solution.py:282
  50.7 5.0 %collective-permute-start.16 = (bf16[256,256]{1,0:T(8,128)(2,1)S(1)}, bf16[256,256]{1,0:T(8,128)(2,1)S(1)}, u32[]{:S(2)}, u32[]{:S(2)}) collective-permute-start(bf16[256,256]{1,0:T(8,128)(2,1)S(1)} %get-tuple-element.73.refs_0_), channel_id=1, source_target_pairs={{0,16},{16,0},{1,17},{17,1},{2,18},{18,2},{3,19},{19,3},{4,20},{20... | collective-permute-start | bytes 393224 | tf_op jit(solution)/shard_map/ppermute | solution.py:282
